TPU v7x, 32 devices: a whole 2x2x4 slice. The times are simulated.
32 devices in a mesh: lon: 16 (over z, y, core), lat: 2 (over x).
Axes of the slice: x: 2, y: 2, z: 4, core: 2. Of those that a mesh axis runs over, the one named last changes fastest.
Arguments:
- node_feat: bfloat16 [16, 2, 64, 512], P('lon', 'lat'), may hold values from -6 to 6
- edge_feat: bfloat16 [16, 2, 384, 512], P('lon', 'lat'), may hold values from -6 to 6
- senders: int32 [16, 2, 384], P('lon', 'lat'), may hold values from 0 to 383, as said below
- receivers: int32 [16, 2, 384], P('lon', 'lat'), may hold values from 0 to 63
- edge_count: int32 [16, 2], P('lon', 'lat'), may hold values from 8 to 384, as said below
- halo_list: int32 [16, 2, 32], P('lon', 'lat'), may hold values from 0 to 63, as said below
- coarse_list: int32 [16, 2, 1], P('lon', 'lat'), may hold values from 0 to 63
- w_edge_in: bfloat16 [1536, 512], replicated, may hold values from -0.15625 to 0.15625
- b_edge_in: float32 [512], replicated, may hold values from -3 to 3
- w_edge_out: bfloat16 [512, 512], replicated, may hold values from -0.25 to 0.25
- gain_edge: float32 [512], replicated, may hold values from 0.1 to 1.9
- shift_edge: float32 [512], replicated, may hold values from -3 to 3
- w_node_in: bfloat16 [1024, 512], replicated, may hold values from -0.1875 to 0.1875
- b_node_in: float32 [512], replicated, may hold values from -3 to 3
- w_node_out: bfloat16 [512, 512], replicated, may hold values from -0.25 to 0.25
- gain_node: float32 [512], replicated, may hold values from 0.1 to 1.9
- shift_node: float32 [512], replicated, may hold values from -3 to 3
- cot_node: bfloat16 [16, 2, 64, 512], P('lon', 'lat'), may hold values from -6 to 6
- cot_edge: bfloat16 [16, 2, 384, 512], P('lon', 'lat'), may hold values from -6 to 6
Outputs:
- new_nodes: bfloat16 [16, 2, 64, 512], P('lon', 'lat')
- grad_nodes: bfloat16 [16, 2, 64, 512], P('lon', 'lat')
- grad_edges: bfloat16 [16, 2, 384, 512], P('lon', 'lat')
Inputs may be any that keep to these rules, and one draw needn't show every extreme that they name: `senders`: A sender t < 64 is the patch's own node t; 64 <= t < 352 is border row of a neighbouring patch as in send_table, never one outside the latitude bands; larger t is a coarse-level row. `halo_list`: the 32 entries of a patch are distinct. Slots 0 to edge_count - 1 of a patch hold its edges, the rest are padding.
All inputs are finite; a program needn't handle non-finite values.
Results may differ from a plain program's by a relative error of at most 0.007.
Values may be sent and summed in bfloat16 or wider, within the bound.
No kernel may reach another device: no remote copies, remote signals or barrier semaphores. Data moves between devices by JAX's collectives and lax.ppermute only.
A program may use at most 64 MiB of HBM per device.

v0:
```python
import jax
import jax.numpy as jnp
from jax import lax
from jax.sharding import PartitionSpec as P


def extended(cells, sides, width, closed):
    for axis, dim in sides:
        count = lax.axis_size(axis)
        ends = count if closed else count - 1
        head = lax.slice_in_dim(cells, 0, width, axis=dim)
        tail = lax.slice_in_dim(cells, cells.shape[dim] - width, cells.shape[dim], axis=dim)
        cells = jnp.concatenate(
            [
                lax.ppermute(tail, axis, [(i, (i + 1) % count) for i in range(ends)]),
                cells,
                lax.ppermute(head, axis, [((i + 1) % count, i) for i in range(ends)]),
            ],
            axis=dim,
        )
    return cells


def passed_along(array, axis, by):
    length = lax.axis_size(axis)
    return lax.ppermute(array, axis, [(i, (i + by) % length) for i in range(length)])


def from_behind(array, axis, by):
    length = lax.axis_size(axis)
    pairs = [(i, i + by) for i in range(length) if 0 <= i + by < length]
    return lax.ppermute(array, axis, pairs)


def norm_rows(out_rows, gain, shift_vec):
    centre = out_rows - jnp.mean(out_rows, axis=1, keepdims=True)
    inv_std = lax.rsqrt(jnp.mean(centre * centre, axis=1, keepdims=True) + 1e-05)
    normed = centre * inv_std
    return (normed * gain + shift_vec, normed, inv_std)


def mlp_forward(joined, w_in, b_in, w_out, gain, shift_vec):
    pre_act = jnp.dot(joined, w_in, preferred_element_type=jnp.float32) + b_in
    activation = (pre_act * jax.nn.sigmoid(pre_act)).astype(jnp.bfloat16)
    out_rows = jnp.dot(activation, w_out, preferred_element_type=jnp.float32)
    update, normed, inv_std = norm_rows(out_rows, gain, shift_vec)
    return (update, (pre_act, normed, inv_std))


def mlp_backward(cotangent, stored, w_in, w_out, gain):
    pre_act, normed, inv_std = stored
    grad_norm = cotangent * gain
    grad_out = inv_std * (
        grad_norm
        - jnp.mean(grad_norm, axis=1, keepdims=True)
        - normed * jnp.mean(grad_norm * normed, axis=1, keepdims=True)
    )
    grad_act = jnp.dot(grad_out.astype(jnp.bfloat16), w_out.T, preferred_element_type=jnp.float32)
    sigmoid_val = jax.nn.sigmoid(pre_act)
    grad_pre = (grad_act * sigmoid_val * (1.0 + pre_act * (1.0 - sigmoid_val))).astype(jnp.bfloat16)
    return jnp.dot(grad_pre, w_in.T, preferred_element_type=jnp.float32)


def local_layer(
    node_rows,
    edge_rows,
    send_table,
    send_index,
    recv_index,
    live_count,
    w_edge_in,
    b_edge_in,
    w_edge_out,
    gain_edge,
    shift_edge,
    w_node_in,
    b_node_in,
    w_node_out,
    gain_node,
    shift_node,
    cot_node,
    cot_edge,
):
    num_nodes = node_rows.shape[0]
    num_edges = edge_rows.shape[0]
    width = node_rows.shape[1]
    live_bool = jnp.arange(num_edges, dtype=jnp.int32) < live_count
    live_mask = live_bool.astype(jnp.float32)[:, None]
    joined = jnp.concatenate([edge_rows, send_table[send_index], node_rows[recv_index]], axis=1)
    edge_upd, edge_stored = mlp_forward(
        joined, w_edge_in, b_edge_in, w_edge_out, gain_edge, shift_edge
    )
    new_edge = (edge_rows.astype(jnp.float32) + live_mask * edge_upd).astype(jnp.bfloat16)
    incidence = (
        (recv_index[None, :] == jnp.arange(num_nodes, dtype=jnp.int32)[:, None])
        & live_bool[None, :]
    ).astype(jnp.bfloat16)
    aggregated = jnp.dot(incidence, new_edge, preferred_element_type=jnp.float32).astype(
        jnp.bfloat16
    )
    node_join = jnp.concatenate([node_rows, aggregated], axis=1)
    node_upd, node_stored = mlp_forward(
        node_join, w_node_in, b_node_in, w_node_out, gain_node, shift_node
    )
    new_nodes = (node_rows.astype(jnp.float32) + node_upd).astype(jnp.bfloat16)
    cot_rows = cot_node.astype(jnp.float32)
    node_djoin = mlp_backward(cot_rows, node_stored, w_node_in, w_node_out, gain_node)
    edge_cot = cot_edge.astype(jnp.float32) + live_mask * node_djoin[:, width:][recv_index]
    edge_djoin = mlp_backward(live_mask * edge_cot, edge_stored, w_edge_in, w_edge_out, gain_edge)
    grad_edges = (edge_cot + edge_djoin[:, :width]).astype(jnp.bfloat16)
    table_grad = jax.ops.segment_sum(
        edge_djoin[:, width : 2 * width], send_index, num_segments=send_table.shape[0]
    )
    grad_local = (
        cot_rows
        + node_djoin[:, :width]
        + jax.ops.segment_sum(edge_djoin[:, 2 * width :], recv_index, num_segments=num_nodes)
        + table_grad[:num_nodes]
    )
    return (new_nodes, grad_edges, grad_local, table_grad[num_nodes:])


def gather_rim(border):
    widened = extended(border, (("lon", 0),), 1, True)
    return extended(widened, (("lat", 1),), 1, False)


def return_rim(rim_grad):
    lon_summed = rim_grad[1]
    for offset in (-1, 1):
        lon_summed = lon_summed + passed_along(
            rim_grad[offset + 1].astype(jnp.bfloat16), "lon", offset
        ).astype(jnp.float32)
    summed = lon_summed[1]
    for offset in (-1, 1):
        summed = summed + from_behind(
            lon_summed[offset + 1].astype(jnp.bfloat16), "lat", offset
        ).astype(jnp.float32)
    return summed


def body(
    node_feat,
    edge_feat,
    senders,
    receivers,
    edge_count,
    halo_list,
    coarse_list,
    w_edge_in,
    b_edge_in,
    w_edge_out,
    gain_edge,
    shift_edge,
    w_node_in,
    b_node_in,
    w_node_out,
    gain_node,
    shift_node,
    cot_node,
    cot_edge,
):
    node_rows = node_feat[0, 0]
    width = node_rows.shape[1]
    border_index = halo_list[0, 0]
    coarse_index = coarse_list[0, 0]
    halo_rows = border_index.shape[0]
    owned = coarse_index.shape[0]
    border = node_rows[border_index][None, None]
    rim_rows = gather_rim(border)
    coarse_all = lax.all_gather(node_rows[coarse_index], ("lon", "lat"), axis=0, tiled=True)
    send_table = jnp.concatenate(
        [node_rows, rim_rows.reshape(9 * halo_rows, width), coarse_all], axis=0
    )
    new_nodes, grad_edges, grad_local, rest_grad = local_layer(
        node_rows,
        edge_feat[0, 0],
        send_table,
        senders[0, 0],
        receivers[0, 0],
        edge_count[0, 0],
        w_edge_in,
        b_edge_in,
        w_edge_out,
        gain_edge,
        shift_edge,
        w_node_in,
        b_node_in,
        w_node_out,
        gain_node,
        shift_node,
        cot_node[0, 0],
        cot_edge[0, 0],
    )
    coarse_grad = rest_grad[9 * halo_rows :]
    summed_all = lax.psum(coarse_grad, ("lon", "lat"))
    own_share = lax.dynamic_slice_in_dim(
        summed_all, lax.axis_index(("lon", "lat")) * owned, owned, 0
    )
    returned = return_rim(rest_grad[: 9 * halo_rows].reshape(3, 3, halo_rows, width))
    grad_local = grad_local.at[border_index].add(returned)
    grad_local = grad_local.at[coarse_index].add(own_share)
    return (
        new_nodes[None, None],
        grad_local.astype(jnp.bfloat16)[None, None],
        grad_edges[None, None],
    )


def solution(mesh):
    return jax.shard_map(
        body,
        mesh=mesh,
        in_specs=(
            P("lon", "lat", None, None),
            P("lon", "lat", None, None),
            P("lon", "lat", None),
            P("lon", "lat", None),
            P("lon", "lat"),
            P("lon", "lat", None),
            P("lon", "lat", None),
            P(),
            P(),
            P(),
            P(),
            P(),
            P(),
            P(),
            P(),
            P(),
            P(),
            P("lon", "lat", None, None),
            P("lon", "lat", None, None),
        ),
        out_specs=(
            P("lon", "lat", None, None),
            P("lon", "lat", None, None),
            P("lon", "lat", None, None),
        ),
        check_vma=False,
    )
```

profile of v0, /device:TPU:0, one launch (start us, length us, event | category | flops | bytes accessed | tf_op | source)
XLA Modules:
  0.0 251.3 jit_solution(17932887219891549768)
XLA Ops:
  7.2 0.8 fusion.80
  8.6 1.5 gather_fusion
  10.6 5.1 %collective-permute-start.1 = (bf16[1,1,32,512]{3,2,1,0:T(8,128)(2,1)S(1)}, bf16[1,1,32,512]{3,2,1,0:T(8,128)(2,1)S(1)}, u32[]{:S(2)}, u32[]{:S(2)}) collective-permute-start(bf16[1,1,32,512]{3,2,1,0:T(8,128)(2,1)S(1)} %bitcast.85), channel_id=1, source_target_pairs={{2,0},{4,2},{6,4},{8,6},{10,8},{12,10},{14,12},{16,14},{18,16},{20... | collective-permute-start | bytes 98312 | tf_op jit(solution)/shard_map/ppermute | solution.py:17
  16.3 0.7 fusion.78
  17.0 0.7 fusion.79
  17.7 1.4 and_reduce_fusion
  19.2 0.7 constant_dynamic-slice_fusion
  19.9 1.3 reduce.7
  21.1 1.3 reduce.10
  22.4 65.7 %all-gather = bf16[32,1,1,512]{3,2,1,0:T(2,128)(2,1)S(1)} all-gather(bf16[1,1,1,512]{3,2,1,0:T(2,128)(2,1)S(1)} %constant_dynamic-slice_fusion), channel_id=2, replica_groups=mesh['lon'=16,'lat'=2] {'lon','lat'}, dimensions={0}, use_global_device_ids=true | all-gather | bytes 33792 | tf_op jit(solution)/shard_map/all_gather | solution.py:171
  88.1 2.1 gather_fusion.2
  90.9 2.1 collective-permute-start.2
  93.1 1.3 collective-permute-start.3
  95.2 4.3 %collective-permute-done.3 = bf16[3,1,32,512]{3,2,1,0:T(8,128)(2,1)S(1)} collective-permute-done((bf16[3,1,32,512]{3,2,1,0:T(8,128)(2,1)S(1)}, bf16[3,1,32,512]{3,2,1,0:T(8,128)(2,1)S(1)}, u32[]{:S(2)}, u32[]{:S(2)}) %collective-permute-start.3) | collective-permute-done | bytes 98336 | tf_op jit(solution)/shard_map/ppermute | solution.py:17
  99.6 2.1 gather_fusion.1
  101.8 0.8 convolution_add_fusion
  105.5 0.9 fusion.38
  106.4 2.5 fusion.10
  108.9 0.9 slice.96
  109.8 1.6 gather_fusion.3
  111.5 1.5 fusion.19
  112.9 4.2 %fusion.2 = f32[384,1536]{1,0:T(8,128)} fusion(bf16[1536,512]{1,0:T(8,128)(2,1)S(1)} %copy-done, bf16[512,512]{1,0:T(8,128)(2,1)} %param.30, f32[384,512]{1,0:T(8,128)} %copy-done.25, f32[384,512]{1,0:T(8,128)S(1)} %get-tuple-element.38, f32[384]{0:T(512)S(1)} %broadcast_multiply_fusion, f32[384]{0:T(512)S(1)} %broadcast_multiply_fusion.1, ...), kind=kOutput, calls=%fused_computation.11 | convolution fusion | flops 809435136 | bytes 7218688 | tf_op jit(solution)/shard_map/dot_general | solution.py:61
  117.1 3.7 %scatter_custom_fusion = f32[384,512]{1,0:T(8,128)S(1)} fusion(s32[384]{0:T(512)} %reduce.10, f32[384,1536]{1,0:T(8,128)} %fusion.2, f32[]{:T(128)} %constant.59.clone.1), kind=kCustom, calls=%fused_computation.27 | custom fusion | flops 196608 | bytes 1573376 | tf_op jit(solution)/shard_map/scatter-add | solution.py:111
  122.1 2.2 fusion.20
  124.9 3.7 %collective-permute-done.5 = bf16[3,32,512]{2,1,0:T(8,128)(2,1)} collective-permute-done((bf16[3,32,512]{2,1,0:T(8,128)(2,1)}, bf16[3,32,512]{2,1,0:T(8,128)(2,1)}, u32[]{:S(2)}, u32[]{:S(2)}) %collective-permute-start.5) | collective-permute-done | bytes 98336 | tf_op jit(solution)/shard_map/ppermute | solution.py:26
  128.6 1.0 fusion.89
  129.6 1.3 collective-permute-start.6
  130.9 4.5 %collective-permute-start.7 = (bf16[32,512]{1,0:T(8,128)(2,1)S(1)}, bf16[32,512]{1,0:T(8,128)(2,1)S(1)}, u32[]{:S(2)}, u32[]{:S(2)}) collective-permute-start(bf16[32,512]{1,0:T(8,128)(2,1)S(1)} %get-tuple-element.36), channel_id=1, source_target_pairs={{0,1},{2,3},{4,5},{6,7},{8,9},{10,11},{12,13},{14,15},{16,17},{18,... | collective-permute-start | bytes 98312 | tf_op jit(solution)/shard_map/ppermute | solution.py:32
  135.5 3.6 %scatter_custom_fusion.1 = f32[64,512]{1,0:T(8,128)S(1)} fusion(f32[64,512]{1,0:T(8,128)S(1)} %fusion.43, s32[384]{0:T(512)} %reduce.7, f32[384,1536]{1,0:T(8,128)} %fusion.2), kind=kCustom, calls=%fused_computation.25 | custom fusion | flops 196608 | bytes 917504 | tf_op jit(solution)/shard_map/scatter-add | solution.py:117
  139.1 1.0 scatter_custom_fusion.2
  140.1 102.3 %all-reduce.2.cloned.1.call-done = f32[32,512]{1,0:T(8,128)} async-done(((f32[32,512]{1,0:T(8,128)}), f32[32,512]{1,0:T(8,128)}) %all-reduce.2.cloned.1.call-update) | async-done | bytes 65552 | tf_op jit(solution)/shard_map/psum | solution.py:196
  242.4 1.4 broadcast_select_fusion
  (93 shorter events, 7.5 us)
Async XLA Ops:
  7.2 94.6 %copy-start = (bf16[1536,512]{1,0:T(8,128)(2,1)S(1)}, bf16[1536,512]{1,0:T(8,128)(2,1)}, u32[]{:S(2)}) copy-start(bf16[1536,512]{1,0:T(8,128)(2,1)} %param.28) | copy-start | bytes 4718596
  7.2 81.0 %copy-start.1 = (bf16[1,1,64,512]{3,2,1,0:T(8,128)(2,1)S(1)}, bf16[1,1,64,512]{3,2,1,0:T(8,128)(2,1)}, u32[]{:S(2)}) copy-start(bf16[1,1,64,512]{3,2,1,0:T(8,128)(2,1)} %param.21) | copy-start | bytes 196612
  7.2 235.2 %all-reduce.2.cloned.1.call-start = ((), (), s32[]{:S(2)}) async-start(), calls=%async_computation | async-start | bytes 131072 | tf_op jit(solution)/shard_map/psum | solution.py:196
  10.1 80.8 %collective-permute-start = (bf16[1,1,32,512]{3,2,1,0:T(8,128)(2,1)S(1)}, bf16[1,1,32,512]{3,2,1,0:T(8,128)(2,1)S(1)}, u32[]{:S(2)}, u32[]{:S(2)}) collective-permute-start(bf16[1,1,32,512]{3,2,1,0:T(8,128)(2,1)S(1)} %bitcast.84), channel_id=1, source_target_pairs={{0,2},{2,4},{4,6},{6,8},{8,10},{10,12},{12,14},{14,16},{16,18},{18... | collective-permute-start | bytes 98312 | tf_op jit(solution)/shard_map/ppermute | solution.py:15
  10.6 80.3 %collective-permute-start.1 = (bf16[1,1,32,512]{3,2,1,0:T(8,128)(2,1)S(1)}, bf16[1,1,32,512]{3,2,1,0:T(8,128)(2,1)S(1)}, u32[]{:S(2)}, u32[]{:S(2)}) collective-permute-start(bf16[1,1,32,512]{3,2,1,0:T(8,128)(2,1)S(1)} %bitcast.85), channel_id=1, source_target_pairs={{2,0},{4,2},{6,4},{8,6},{10,8},{12,10},{14,12},{16,14},{18,16},{20... | collective-permute-start | bytes 98312 | tf_op jit(solution)/shard_map/ppermute | solution.py:17
  90.9 4.3 %collective-permute-start.2 = (bf16[3,1,32,512]{3,2,1,0:T(8,128)(2,1)S(1)}, bf16[3,1,32,512]{3,2,1,0:T(8,128)(2,1)S(1)}, u32[]{:S(2)}, u32[]{:S(2)}) collective-permute-start(bf16[3,1,32,512]{3,2,1,0:T(8,128)(2,1)S(1)} %pad_maximum_fusion.2), channel_id=1, source_target_pairs={{0,1},{2,3},{4,5},{6,7},{8,9},{10,11},{12,13},{14,15},{16,17},{18,... | collective-permute-start | bytes 294920 | tf_op jit(solution)/shard_map/ppermute | solution.py:15
  93.1 6.5 %collective-permute-start.3 = (bf16[3,1,32,512]{3,2,1,0:T(8,128)(2,1)S(1)}, bf16[3,1,32,512]{3,2,1,0:T(8,128)(2,1)S(1)}, u32[]{:S(2)}, u32[]{:S(2)}) collective-permute-start(bf16[3,1,32,512]{3,2,1,0:T(8,128)(2,1)S(1)} %pad_maximum_fusion.2), channel_id=1, source_target_pairs={{1,0},{3,2},{5,4},{7,6},{9,8},{11,10},{13,12},{15,14},{17,16},{19,... | collective-permute-start | bytes 294920 | tf_op jit(solution)/shard_map/ppermute | solution.py:17
  94.9 6.9 %copy-start.21 = (bf16[1,1,384,512]{3,2,1,0:T(8,128)(2,1)S(1)}, bf16[1,1,384,512]{3,2,1,0:T(8,128)(2,1)}, u32[]{:S(2)}) copy-start(bf16[1,1,384,512]{3,2,1,0:T(8,128)(2,1)} %param.22) | copy-start | bytes 1179652
  94.9 6.9 %copy-start.23 = (f32[512]{0:T(512)S(1)}, f32[512]{0:T(512)}, u32[]{:S(2)}) copy-start(f32[512]{0:T(512)} %param.29) | copy-start | bytes 6148
  101.7 1.0 copy-start.20
  102.8 0.9 copy-start.14
  102.8 0.9 copy-start.15
  102.8 0.9 copy-start.19
  102.8 1.3 copy-start.22
  102.8 1.3 copy-start.24
  102.8 1.7 copy-start.2
  102.8 1.7 copy-start.12
  103.3 1.6 copy-start.7
  103.3 2.1 copy-start.5
  103.3 2.1 copy-start.8
  103.3 2.1 copy-start.13
  104.9 1.4 copy-start.6
  105.2 1.1 copy-start.3
  105.2 1.1 copy-start.11
  105.4 0.9 copy-start.17
  109.8 1.7 copy-start.10
  109.8 1.7 copy-start.16
  120.9 14.6 %copy-start.4 = (f32[64,1024]{1,0:T(8,128)S(1)}, f32[64,1024]{1,0:T(8,128)}, u32[]{:S(2)}) copy-start(f32[64,1024]{1,0:T(8,128)} %fusion.10) | copy-start | bytes 786436
  121.6 3.4 %collective-permute-start.4 = (bf16[3,32,512]{2,1,0:T(8,128)(2,1)}, bf16[3,32,512]{2,1,0:T(8,128)(2,1)}, u32[]{:S(2)}, u32[]{:S(2)}) collective-permute-start(bf16[3,32,512]{2,1,0:T(8,128)(2,1)} %bitcast.16), channel_id=1, source_target_pairs={{0,30},{2,0},{4,2},{6,4},{8,6},{10,8},{12,10},{14,12},{16,14},{18,... | collective-permute-start | bytes 294920 | tf_op jit(solution)/shard_map/ppermute | solution.py:26
  121.6 7.1 %collective-permute-start.5 = (bf16[3,32,512]{2,1,0:T(8,128)(2,1)}, bf16[3,32,512]{2,1,0:T(8,128)(2,1)}, u32[]{:S(2)}, u32[]{:S(2)}) collective-permute-start(bf16[3,32,512]{2,1,0:T(8,128)(2,1)} %bitcast.17), channel_id=1, source_target_pairs={{0,2},{2,4},{4,6},{6,8},{8,10},{10,12},{12,14},{14,16},{16,18},{18... | collective-permute-start | bytes 294920 | tf_op jit(solution)/shard_map/ppermute | solution.py:26
  129.6 9.5 %collective-permute-start.6 = (bf16[32,512]{1,0:T(8,128)(2,1)S(1)}, bf16[32,512]{1,0:T(8,128)(2,1)S(1)}, u32[]{:S(2)}, u32[]{:S(2)}) collective-permute-start(bf16[32,512]{1,0:T(8,128)(2,1)S(1)} %get-tuple-element.35), channel_id=1, source_target_pairs={{1,0},{3,2},{5,4},{7,6},{9,8},{11,10},{13,12},{15,14},{17,16},{19,... | collective-permute-start | bytes 98312 | tf_op jit(solution)/shard_map/ppermute | solution.py:32
  130.9 8.2 %collective-permute-start.7 = (bf16[32,512]{1,0:T(8,128)(2,1)S(1)}, bf16[32,512]{1,0:T(8,128)(2,1)S(1)}, u32[]{:S(2)}, u32[]{:S(2)}) collective-permute-start(bf16[32,512]{1,0:T(8,128)(2,1)S(1)} %get-tuple-element.36), channel_id=1, source_target_pairs={{0,1},{2,3},{4,5},{6,7},{8,9},{10,11},{12,13},{14,15},{16,17},{18,... | collective-permute-start | bytes 98312 | tf_op jit(solution)/shard_map/ppermute | solution.py:32
  (3 other events, 2.3 us)
Sparse Core Ops, SparseCore 0:
  125.0 117.3 all-reduce.1
where the time goes:
time: 253 us; the launch traced here: 251 us
  waiting for transfers between devices  111 us (44%)
  blocking collectives  65.7 us (26%)
  other arithmetic  23 us (9%)
  between operations  15.9 us (6%)
  starting transfers between devices  15.4 us (6%)
  local copies, waits for them, and re-layouts  11.7 us (5%)
  matrix products  8.96 us (4%)
    psum x1, waiting for transfers between devices, body(): summed_all = lax.psum(coarse_grad, ('lon', 'lat'))  102 us
    all_gather x1, blocking collectives, body(): lax.all_gather(node_rows[coarse_index], ('lon', 'lat'), axis=0, tiled=True)  65.7 us
    dot_general x2, matrix products, mlp_backward(): return jnp.dot(grad_pre, w_in.T, preferred_element_type=jnp.float32)  6.71 us
    ppermute x2, starting transfers between devices, extended(): lax.ppermute(head, axis, [((i + 1) % count, i) for i in range(ends)])  6.35 us
    ppermute x2, starting transfers between devices, from_behind(): return lax.ppermute(array, axis, pairs)  5.84 us
  transfers between devices with their start and end apart: 9, of which 4 were waited for; matrix products, arithmetic and copies ran while one was open for 7% of the time, Pallas kernels for 0%

commit v1 on v0

v1 whole, which is shorter than its diff:
```python
import functools

import jax
import jax.numpy as jnp
from jax import lax
from jax.experimental import pallas as pl
from jax.experimental.pallas import tpu as pltpu
from jax.sharding import PartitionSpec as P

F32 = jnp.float32
BF16 = jnp.bfloat16
VMEM = pltpu.VMEM
SMEM = pltpu.SMEM


def dot_nn(a, b):
    return jnp.dot(a, b, preferred_element_type=F32)


def dot_tn(a, b):
    return lax.dot_general(a, b, (((0,), (0,)), ((), ())), preferred_element_type=F32)


def dot_nt(a, b):
    return lax.dot_general(a, b, (((1,), (1,)), ((), ())), preferred_element_type=F32)


def as_one_hot(mask):
    return jnp.where(mask, 1.0, 0.0).astype(BF16)


def one_hot_rows(index_row, rows):
    return lax.broadcasted_iota(jnp.int32, (rows, index_row.shape[1]), 0) == index_row


def live_one_hot(index_row, rows, count):
    lanes = lax.broadcasted_iota(jnp.int32, (rows, index_row.shape[1]), 1)
    return as_one_hot(one_hot_rows(index_row, rows) & (lanes < count))


def in_two(values):
    head = values.astype(BF16)
    tail = (values - head.astype(F32)).astype(BF16)
    return jnp.concatenate([head, tail], axis=0)


def normed_rows(out_rows):
    centre = out_rows - jnp.mean(out_rows, axis=1, keepdims=True)
    inv_std = lax.rsqrt(jnp.mean(centre * centre, axis=1, keepdims=True) + 1e-05)
    return centre * inv_std, inv_std


def norm_backward(grad_norm, normed, inv_std):
    return inv_std * (
        grad_norm
        - jnp.mean(grad_norm, axis=1, keepdims=True)
        - normed * jnp.mean(grad_norm * normed, axis=1, keepdims=True)
    )


def silu_slope(pre, sig):
    return sig * (1.0 + pre * (1.0 - sig))


class Plan:
    def __init__(self, lon, lat, nodes, edges, halo, owned, width):
        self.lon, self.lat = lon, lat
        self.nodes, self.edges, self.halo, self.owned, self.width = nodes, edges, halo, owned, width
        self.coarse = lon * lat * owned
        flat = lambda i, j: (i % lon) * lat + j
        swap = lambda pairs: [p for a, b in pairs for p in ((a, b), (b, a))]
        lat_sets = [
            [(k, k + 1) for k in range(0, lat - 1, 2)],
            [(k, k + 1) for k in range(1, lat - 1, 2)],
        ]
        self.lat_pairs = [
            swap([(flat(i, a), flat(i, b)) for i in range(lon) for a, b in pairs])
            for pairs in lat_sets
            if pairs
        ]
        self.lon_pairs = [
            swap([(flat(i, j), flat(i + 1, j)) for i in range(first, lon, 2) for j in range(lat)])
            for first in (0, 1)
        ]
        self.per_lon = 1 + len(self.lat_pairs)
        self.blocks = 3 * self.per_lon
        self.table = nodes + self.blocks * halo + self.coarse

    def positions(self, sender):
        nodes, halo = self.nodes, self.halo
        lon_odd = lax.rem(lax.axis_index("lon"), 2)
        lat_odd = lax.rem(lax.axis_index("lat"), 2)
        lon_step = [1, 2 - 2 * lon_odd, 2 * lon_odd]
        lat_step = [1, 2 - 2 * lat_odd, 2 * lat_odd][: self.per_lon]
        past = sender - (nodes + 9 * halo)
        found = jnp.where(past >= 0, past + (nodes + self.blocks * halo), sender)
        place = 0
        for a in lon_step:
            for b in lat_step:
                row = sender - (nodes + (3 * a + b) * halo)
                inside = (row >= 0) & (row < halo) & (sender >= nodes)
                found = jnp.where(inside, row + (nodes + place * halo), found)
                place += 1
        return found


def pack_kernel(plan, node, halo_list, coarse_list, border, coarse):
    rows = node[0, 0]
    border[...] = dot_tn(as_one_hot(one_hot_rows(halo_list[0], plan.nodes)), rows).astype(BF16)
    shape = (plan.coarse, plan.nodes)
    which = lax.rem(lax.broadcasted_iota(jnp.int32, shape, 0), plan.owned)
    wanted = jnp.full(shape, coarse_list[0, 0, 0], jnp.int32)
    for k in range(1, plan.owned):
        wanted = jnp.where(which == k, coarse_list[0, 0, k], wanted)
    pick = as_one_hot(lax.broadcasted_iota(jnp.int32, shape, 1) == wanted)
    coarse[...] = dot_nn(pick, rows).astype(BF16)


def ahead_kernel(
    plan, count, node, edge, receivers, w_edge_in, b_edge_in, w_node_in, b_node_in, edge_part, node_part
):
    width = plan.width
    rows = node[0, 0]
    received = live_one_hot(receivers[0], plan.nodes, count[0, 0])
    at_receiver = dot_tn(received, rows).astype(BF16)
    edge_part[...] = (
        dot_nn(edge[0, 0], w_edge_in[:width])
        + dot_nn(at_receiver, w_edge_in[2 * width :])
        + b_edge_in[...]
    )
    node_part[...] = dot_nn(rows, w_node_in[:width]) + b_node_in[...]


def main_kernel(plan, *refs):
    lats = plan.per_lon - 1
    count, node, edge, senders, receivers, border = refs[:6]
    lat_rows = refs[6 : 6 + lats]
    (
        even_rows,
        odd_rows,
        coarse_rows,
        edge_part,
        node_part,
        w_edge_in,
        w_edge_out,
        gain_edge,
        shift_edge,
        w_node_in,
        w_node_out,
        gain_node,
        shift_node,
        cot_node,
        cot_edge,
        new_nodes,
        even_grad,
        odd_grad,
        kept_grad,
        coarse_grad,
        edge_cot_out,
        edge_dpre_out,
        node_dpre_out,
        table,
    ) = refs[6 + lats :]
    nodes, halo, width = plan.nodes, plan.halo, plan.width
    start = nodes
    table[:nodes] = node[0, 0]
    for part in (border, *lat_rows, even_rows, odd_rows, coarse_rows):
        table[start : start + part.shape[0]] = part[...]
        start += part.shape[0]
    live_count = count[0, 0]
    live = jnp.where(
        lax.broadcasted_iota(jnp.int32, (plan.edges, 1), 0) < live_count, 1.0, 0.0
    ).astype(F32)
    sent = as_one_hot(one_hot_rows(plan.positions(senders[0]), plan.table))
    received = live_one_hot(receivers[0], nodes, live_count)

    at_sender = dot_tn(sent, table[...]).astype(BF16)
    edge_pre = edge_part[...] + dot_nn(at_sender, w_edge_in[width : 2 * width])
    edge_sig = jax.nn.sigmoid(edge_pre)
    edge_out = dot_nn((edge_pre * edge_sig).astype(BF16), w_edge_out[...])
    edge_normed, edge_rstd = normed_rows(edge_out)
    edge_upd = edge_normed * gain_edge[...] + shift_edge[...]
    new_edge = (edge[0, 0].astype(F32) + live * edge_upd).astype(BF16)
    aggregated = dot_nn(received, new_edge).astype(BF16)

    node_pre = node_part[...] + dot_nn(aggregated, w_node_in[width:])
    node_sig = jax.nn.sigmoid(node_pre)
    node_out = dot_nn((node_pre * node_sig).astype(BF16), w_node_out[...])
    node_normed, node_rstd = normed_rows(node_out)
    node_upd = node_normed * gain_node[...] + shift_node[...]
    new_nodes[0, 0] = (node[0, 0].astype(F32) + node_upd).astype(BF16)

    node_dout = norm_backward(
        cot_node[0, 0].astype(F32) * gain_node[...], node_normed, node_rstd
    ).astype(BF16)
    node_dpre = (dot_nt(node_dout, w_node_out[...]) * silu_slope(node_pre, node_sig)).astype(BF16)
    node_dpre_out[...] = node_dpre
    agg_grad = dot_nt(node_dpre, w_node_in[width:])
    twice = jnp.concatenate([received, received], axis=0)
    edge_cot = cot_edge[0, 0].astype(F32) + dot_tn(twice, in_two(agg_grad))
    edge_cot_out[...] = edge_cot

    edge_dout = norm_backward(live * edge_cot * gain_edge[...], edge_normed, edge_rstd).astype(BF16)
    edge_dpre = (dot_nt(edge_dout, w_edge_out[...]) * silu_slope(edge_pre, edge_sig)).astype(BF16)
    edge_dpre_out[...] = edge_dpre
    away = dot_nn(sent[nodes:], edge_dpre).astype(BF16)
    away_grad = dot_nt(away, w_edge_in[width : 2 * width])
    kept = plan.per_lon * halo
    kept_grad[...] = away_grad[:kept]
    even_grad[...] = away_grad[kept : 2 * kept].astype(BF16)
    odd_grad[...] = away_grad[2 * kept : 3 * kept].astype(BF16)
    coarse_grad[...] = away_grad[3 * kept :].astype(BF16)


def behind_kernel(
    plan,
    count,
    senders,
    receivers,
    edge_dpre,
    node_dpre,
    edge_cot,
    cot_node,
    w_edge_in,
    w_node_in,
    grad_edges,
    grad_local,
):
    width, nodes = plan.width, plan.nodes
    dpre = edge_dpre[...]
    received = live_one_hot(receivers[0], nodes, count[0, 0])
    sent = as_one_hot(one_hot_rows(senders[0], nodes))
    both = dot_nn(jnp.concatenate([sent, received], axis=0), dpre).astype(BF16)
    grad_local[...] = (
        cot_node[0, 0].astype(F32)
        + dot_nt(node_dpre[...], w_node_in[:width])
        + dot_nt(both[:nodes], w_edge_in[width : 2 * width])
        + dot_nt(both[nodes:], w_edge_in[2 * width :])
    )
    grad_edges[0, 0] = (edge_cot[...] + dot_nt(dpre, w_edge_in[:width])).astype(BF16)


def middle_kernel(plan, kept, even, odd, mine, *lat_sends):
    total = kept[...] + even[...].astype(F32) + odd[...].astype(F32)
    mine[...] = total[: plan.halo]
    for k, out in enumerate(lat_sends):
        out[...] = total[(k + 1) * plan.halo : (k + 2) * plan.halo].astype(BF16)


def last_kernel(plan, *refs):
    lats = plan.per_lon - 1
    grad_local, mine, halo_list, coarse_list, coarse = refs[:5]
    out = refs[-1]
    total = mine[...]
    for part in refs[5 : 5 + lats]:
        total = total + part[...].astype(F32)
    place = as_one_hot(one_hot_rows(halo_list[0], plan.nodes))
    result = grad_local[...] + dot_nn(jnp.concatenate([place, place], axis=1), in_two(total))
    received = coarse[...].astype(F32)
    at_row = lax.broadcasted_iota(jnp.int32, result.shape, 0)
    for k in range(plan.owned):
        terms = received
        if plan.owned > 1:
            which = lax.rem(lax.broadcasted_iota(jnp.int32, received.shape, 0), plan.owned)
            terms = jnp.where(which == k, received, 0.0)
        share = jnp.sum(terms, axis=0, keepdims=True)
        result = result + jnp.where(at_row == coarse_list[0, 0, k], share, 0.0)
    out[0, 0] = result.astype(BF16)


def call(body, name, outs, operands, smem=(), scratch=(), flops=0, mib=8):
    whole = pl.BlockSpec(memory_space=VMEM)
    scalars = pl.BlockSpec(memory_space=SMEM)
    moved = sum(a.size * a.dtype.itemsize for a in operands)
    return pl.pallas_call(
        body,
        name=name,
        out_shape=[jax.ShapeDtypeStruct(shape, dtype) for shape, dtype in outs],
        in_specs=[scalars if k in smem else whole for k in range(len(operands))],
        out_specs=[whole] * len(outs),
        scratch_shapes=list(scratch),
        compiler_params=pltpu.CompilerParams(vmem_limit_bytes=mib * 1024 * 1024),
        cost_estimate=pl.CostEstimate(flops=flops, bytes_accessed=moved, transcendentals=0),
    )(*operands)


def body(
    plan,
    node_feat,
    edge_feat,
    senders,
    receivers,
    edge_count,
    halo_list,
    coarse_list,
    w_edge_in,
    b_edge_in,
    w_edge_out,
    gain_edge,
    shift_edge,
    w_node_in,
    b_node_in,
    w_node_out,
    gain_node,
    shift_node,
    cot_node,
    cot_edge,
):
    axes = ("lon", "lat")
    halo, width, nodes, edges = plan.halo, plan.width, plan.nodes, plan.edges
    row = lambda vec: vec.reshape(1, width)
    with_plan = lambda kernel: functools.partial(kernel, plan)

    border, coarse_out = call(
        with_plan(pack_kernel),
        "pack",
        [((halo, width), BF16), ((plan.coarse, width), BF16)],
        [node_feat, halo_list, coarse_list],
        smem=(2,),
    )
    coarse_rows = lax.all_to_all(coarse_out, axes, 0, 0, tiled=True)
    lat_rows = [lax.ppermute(border, axes, pairs) for pairs in plan.lat_pairs]
    wide = jnp.concatenate([border, *lat_rows], axis=0)
    even_rows, odd_rows = [lax.ppermute(wide, axes, pairs) for pairs in plan.lon_pairs]

    edge_part, node_part = call(
        with_plan(ahead_kernel),
        "ahead",
        [((edges, width), F32), ((nodes, width), F32)],
        [edge_count, node_feat, edge_feat, receivers, w_edge_in, row(b_edge_in), w_node_in, row(b_node_in)],
        smem=(0,),
        flops=2 * (2 * edges + nodes) * width * width,
    )

    kept = plan.per_lon * halo
    new_nodes, even_grad, odd_grad, kept_grad, coarse_grad, edge_cot, edge_dpre, node_dpre = call(
        with_plan(main_kernel),
        "main",
        [
            (node_feat.shape, BF16),
            ((kept, width), BF16),
            ((kept, width), BF16),
            ((kept, width), F32),
            ((plan.coarse, width), BF16),
            ((edges, width), F32),
            ((edges, width), BF16),
            ((nodes, width), BF16),
        ],
        [
            edge_count,
            node_feat,
            edge_feat,
            senders,
            receivers,
            border,
            *lat_rows,
            even_rows,
            odd_rows,
            coarse_rows,
            edge_part,
            node_part,
            w_edge_in,
            w_edge_out,
            row(gain_edge),
            row(shift_edge),
            w_node_in,
            w_node_out,
            row(gain_node),
            row(shift_node),
            cot_node,
            cot_edge,
        ],
        smem=(0,),
        scratch=[pltpu.VMEM((plan.table, width), BF16)],
        mib=20,
        flops=2 * 5 * edges * width * width,
    )

    coarse_back = lax.all_to_all(coarse_grad, axes, 0, 0, tiled=True)
    even_back, odd_back = [
        lax.ppermute(grad, axes, pairs)
        for grad, pairs in zip((even_grad, odd_grad), plan.lon_pairs)
    ]
    grad_edges, grad_local = call(
        with_plan(behind_kernel),
        "behind",
        [(edge_feat.shape, BF16), ((nodes, width), F32)],
        [edge_count, senders, receivers, edge_dpre, node_dpre, edge_cot, cot_node, w_edge_in, w_node_in],
        smem=(0,),
        flops=2 * (edges + 3 * nodes) * width * width,
    )
    mine, *lat_sends = call(
        with_plan(middle_kernel),
        "middle",
        [((halo, width), F32)] + [((halo, width), BF16)] * len(plan.lat_pairs),
        [kept_grad, even_back, odd_back],
    )
    lat_back = [
        lax.ppermute(grad, axes, pairs) for grad, pairs in zip(lat_sends, plan.lat_pairs)
    ]
    (grad_nodes,) = call(
        with_plan(last_kernel),
        "last",
        [(node_feat.shape, BF16)],
        [grad_local, mine, halo_list, coarse_list, coarse_back, *lat_back],
        smem=(3,),
    )
    return new_nodes, grad_nodes, grad_edges


def solution(mesh):
    lon, lat = mesh.shape["lon"], mesh.shape["lat"]
    cells = lambda rank: P("lon", "lat", *([None] * (rank - 2)))

    def sharded(*args):
        node_feat, edge_feat, halo_list, coarse_list = args[0], args[1], args[5], args[6]
        plan = Plan(
            lon,
            lat,
            node_feat.shape[2],
            edge_feat.shape[2],
            halo_list.shape[2],
            coarse_list.shape[2],
            node_feat.shape[3],
        )
        return body(plan, *args)

    ranks = (4, 4, 3, 3, 2, 3, 3)
    return jax.shard_map(
        sharded,
        mesh=mesh,
        in_specs=tuple(cells(r) for r in ranks) + (P(),) * 10 + (cells(4), cells(4)),
        out_specs=(cells(4), cells(4), cells(4)),
        check_vma=False,
    )
```

time: 253 us -> 64.1 us (0.25)
  waiting for transfers between devices: 111 us -> 0.68 us
  blocking collectives: 65.7 us -> 0 us
  other arithmetic: 23 us -> 1.86 us
  local copies, waits for them, and re-layouts: 11.7 us -> 30.5 us
  between operations: 15.9 us -> 2.22 us
  matrix products: 8.96 us -> 0 us
  Pallas kernels: 0 us -> 8.61 us
  starting transfers between devices: 15.4 us -> 19 us
    psum x1 -> x0, waiting for transfers between devices: 102 us -> none  [body(): summed_all = lax.psum(coarse_grad, ('lon', 'lat'))]
    all_gather x1 -> x0, blocking collectives: 65.7 us -> none  [body(): lax.all_gather(node_rows[coarse_index], ('lon', 'lat'), axis=0, tiled=True)]
    unnamed x53 -> x89, local copies, waits for them, and re-layouts: 1.43 us -> 29.4 us
    dot_general x7 -> x0, matrix products: 8.96 us -> none  [the longest x2 6.71 us: mlp_backward(): return jnp.dot(grad_pre, w_in.T, preferred_element_type=jnp.float32)]
    pallas_call x0 -> x6, Pallas kernels: none -> 8.61 us  [call(): pl.pallas_call(body, name=name, out_shape=[jax.ShapeDtypeStruct(shape, dt...]
    scatter-add x3 -> x0, other arithmetic: 8.21 us -> none  [the longest x1 3.66 us: local_layer(): jax.ops.segment_sum(edge_djoin[:, width:2 * width], send_index, num_segme...]
    gather x5 -> x0, local copies, waits for them, and re-layouts: 7.93 us -> none  [the longest x1 2.06 us: local_layer(): node_rows[recv_index]]
    ppermute x8 -> x6, waiting for transfers between devices: 8.39 us -> 0.67 us  [the longest x1 0.66 us: body(): lat_rows = [lax.ppermute(border, axes, pairs) for pairs in plan.lat_pairs]]
  transfers between devices with their start and end apart: 9 -> 8, of which waited for: 4 -> 1; matrix products, arithmetic and copies ran while one was open for 7% -> 10% of each run, Pallas kernels for 0% -> 4%
where the time goes in v1:
time: 64.1 us; the launch traced here: 62.9 us
  local copies, waits for them, and re-layouts  30.5 us (48%)
  starting transfers between devices  19 us (30%)
  Pallas kernels  8.61 us (13%)
  between operations  2.22 us (3%)
  other arithmetic  1.86 us (3%)
  waiting for transfers between devices  0.68 us (1%)
    unnamed x89, local copies, waits for them, and re-layouts  29.4 us
    pallas_call x6, Pallas kernels, call(): pl.pallas_call(body, name=name, out_shape=[jax.ShapeDtypeStruct(shape, dt...  8.61 us
    ppermute x3, starting transfers between devices, body(): lax.ppermute(grad, axes, pairs)  6.29 us
    all_to_all x1, starting transfers between devices, body(): coarse_rows = lax.all_to_all(coarse_out, axes, 0, 0, tiled=True)  3.81 us
    ppermute x2, starting transfers between devices, body(): lax.ppermute(wide, axes, pairs)  3.38 us
    ppermute x1, starting transfers between devices, body(): lat_rows = [lax.ppermute(border, axes, pairs) for pairs in plan.lat_pairs]  3 us
    all_to_all x1, starting transfers between devices, body(): coarse_back = lax.all_to_all(coarse_grad, axes, 0, 0, tiled=True)  2.54 us
    all_to_all x1, other arithmetic, body(): coarse_back = lax.all_to_all(coarse_grad, axes, 0, 0, tiled=True)  1.31 us
  transfers between devices with their start and end apart: 8, of which 1 were waited for; matrix products, arithmetic and copies ran while one was open for 10% of the time, Pallas kernels for 4%

profile of v1, /device:TPU:0, one launch (start us, length us, event | category | flops | bytes accessed | tf_op | source)
XLA Modules:
  0.0 62.9 jit_solution(17726519759864186647)
XLA Ops:
  1.3 0.8 %copy-done.10 = bf16[1,1,64,512]{3,2,1,0:T(8,128)(2,1)S(1)} copy-done((bf16[1,1,64,512]{3,2,1,0:T(8,128)(2,1)S(1)}, bf16[1,1,64,512]{3,2,1,0:T(8,128)(2,1)}, u32[]{:S(2)}) %copy-start.10) | copy-done | bytes 65560
  3.0 3.0 %collective-permute-start = (bf16[32,512]{1,0:T(8,128)(2,1)S(1)}, bf16[32,512]{1,0:T(8,128)(2,1)S(1)}, u32[]{:S(2)}, u32[]{:S(2)}) collective-permute-start(bf16[32,512]{1,0:T(8,128)(2,1)S(1)} %get-tuple-element.19.refs_5_), channel_id=1, source_target_pairs={{0,1},{1,0},{2,3},{3,2},{4,5},{5,4},{6,7},{7,6},{8,9},{9,8},{10,11... | collective-permute-start | bytes 98312 | tf_op jit(solution)/shard_map/ppermute | solution.py:322
  9.1 3.4 %collective-permute-start.2 = (bf16[64,512]{1,0:T(8,128)(2,1)}, bf16[64,512]{1,0:T(8,128)(2,1)}, u32[]{:S(2)}, u32[]{:S(2)}) collective-permute-start(bf16[64,512]{1,0:T(8,128)(2,1)} %constant_dynamic-update-slice_fusion), channel_id=1, source_target_pairs={{2,4},{4,2},{3,5},{5,3},{6,8},{8,6},{7,9},{9,7},{10,12},{12,10},{1... | collective-permute-start | bytes 196616 | tf_op jit(solution)/shard_map/ppermute | solution.py:324
  14.1 3.8 %all-to-all-start = ((bf16[32,2,256]{2,1,0:T(2,128)(2,1)}), bf16[32,2,256]{2,1,0:T(2,128)(2,1)}, u32[]{:S(2)}, u32[]{:S(2)}) async-start(bf16[32,2,256]{2,1,0:T(2,128)(2,1)} %reshape.34), calls=%async_computation | async-start | bytes 65536 | tf_op jit(solution)/shard_map/all_to_all | solution.py:321
  18.6 1.4 %copy-done = bf16[1536,512]{1,0:T(8,128)(2,1)S(1)} copy-done((bf16[1536,512]{1,0:T(8,128)(2,1)S(1)}, bf16[1536,512]{1,0:T(8,128)(2,1)}, u32[]{:S(2)}) %copy-start) | copy-done | bytes 1572888
  20.0 1.2 %copy-done.2 = bf16[1024,512]{1,0:T(8,128)(2,1)S(1)} copy-done((bf16[1024,512]{1,0:T(8,128)(2,1)S(1)}, bf16[1024,512]{1,0:T(8,128)(2,1)}, u32[]{:S(2)}) %copy-start.2) | copy-done | bytes 1048600
  21.2 1.0 %copy-done.4 = bf16[1,1,384,512]{3,2,1,0:T(8,128)(2,1)S(1)} copy-done((bf16[1,1,384,512]{3,2,1,0:T(8,128)(2,1)S(1)}, bf16[1,1,384,512]{3,2,1,0:T(8,128)(2,1)}, u32[]{:S(2)}) %copy-start.4) | copy-done | bytes 393240
  22.2 0.8 %copy-done.11 = bf16[1,1,64,512]{3,2,1,0:T(8,128)(2,1)S(1)} copy-done((bf16[1,1,64,512]{3,2,1,0:T(8,128)(2,1)S(1)}, bf16[1,1,64,512]{3,2,1,0:T(8,128)(2,1)}, u32[]{:S(2)}) %copy-start.11) | copy-done | bytes 65560
  24.4 0.7 %copy-done.40 = f32[512]{0:T(512)S(1)} copy-done((f32[512]{0:T(512)S(1)}, f32[512]{0:T(512)}, u32[]{:S(2)}) %copy-start.40) | copy-done | bytes 2072
  25.2 0.8 %ahead.1 = (f32[384,512]{1,0:T(8,128)S(1)}, f32[64,512]{1,0:T(8,128)S(1)}) custom-call(s32[1,1]{1,0:T(1,128)S(6)} %copy.35.count.refs_0_, bf16[1,1,64,512]{3,2,1,0:T(8,128)(2,1)S(1)} %copy-done.11, bf16[1,1,384,512]{3,2,1,0:T(8,128)(2,1)S(1)} %copy-done.4, s32[1,1,384]{2,1,0:T(1,128)S(1)} %copy-done.30, bf16[1536,512]{1,0:T(8,128)(2,1)S(1)} %copy-done, ...), custom_call_target="tpu_custom_call" | custom-call | flops 436207616 | bytes 3085828 | tf_op jit(solution)/shard_map/ahead/pallas_call | solution.py:275
  26.0 0.9 %copy-done.6 = f32[384,512]{1,0:T(8,128)} copy-done((f32[384,512]{1,0:T(8,128)}, f32[384,512]{1,0:T(8,128)S(1)}, u32[]{:S(2)}) %copy-start.6) | copy-done | bytes 786456
  27.5 1.4 %reshape.35 = bf16[32,1,512]{2,1,0:T(2,128)(2,1)} reshape(bf16[32,2,256]{2,1,0:T(2,128)(2,1)} %all-to-all-done) | data formatting | bytes 65536
  29.0 0.8 %copy.31 = bf16[32,1,512]{2,0,1:T(8,128)(2,1)S(1)} copy(bf16[32,1,512]{2,1,0:T(2,128)(2,1)} %reshape.35) | data formatting | bytes 65536
  29.9 1.1 %copy-done.7 = f32[384,512]{1,0:T(8,128)S(1)} copy-done((f32[384,512]{1,0:T(8,128)S(1)}, f32[384,512]{1,0:T(8,128)}, u32[]{:S(2)}) %copy-start.7) | copy-done | bytes 786456
  31.1 1.0 %copy-done.13 = bf16[512,512]{1,0:T(8,128)(2,1)S(1)} copy-done((bf16[512,512]{1,0:T(8,128)(2,1)S(1)}, bf16[512,512]{1,0:T(8,128)(2,1)}, u32[]{:S(2)}) %copy-start.13) | copy-done | bytes 524312
  32.1 1.0 %copy-done.14 = bf16[512,512]{1,0:T(8,128)(2,1)S(1)} copy-done((bf16[512,512]{1,0:T(8,128)(2,1)S(1)}, bf16[512,512]{1,0:T(8,128)(2,1)}, u32[]{:S(2)}) %copy-start.14) | copy-done | bytes 524312
  33.1 0.8 %copy-done.20 = bf16[32,512]{1,0:T(8,128)(2,1)S(1)} copy-done((bf16[32,512]{1,0:T(8,128)(2,1)S(1)}, bf16[32,512]{1,0:T(8,128)(2,1)}, u32[]{:S(2)}) %copy-start.20) | copy-done | bytes 32792
  33.9 0.8 %copy-done.22 = bf16[32,512]{1,0:T(8,128)(2,1)S(1)} copy-done((bf16[32,512]{1,0:T(8,128)(2,1)S(1)}, bf16[32,512]{1,0:T(8,128)(2,1)}, u32[]{:S(2)}) %copy-start.22) | copy-done | bytes 32792
  34.7 0.9 %copy-done.24 = f32[64,512]{1,0:T(8,128)S(1)} copy-done((f32[64,512]{1,0:T(8,128)S(1)}, f32[64,512]{1,0:T(8,128)}, u32[]{:S(2)}) %copy-start.24) | copy-done | bytes 131096
  36.9 5.1 %main.1 = (bf16[1,1,64,512]{3,2,1,0:T(8,128)(2,1)}, bf16[64,512]{1,0:T(8,128)(2,1)}, bf16[64,512]{1,0:T(8,128)(2,1)}, f32[64,512]{1,0:T(8,128)S(1)}, bf16[32,512...) custom-call(s32[1,1]{1,0:T(1,128)S(6)} %copy.35.count.refs_0_, ...), custom_call_target="tpu_custom_call" | custom-call | flops 1006632960 | bytes 5745668 | tf_op jit(solution)/shard_map/main/pallas_call | solution.py:275
  42.0 0.9 %copy-done.8 = f32[384,512]{1,0:T(8,128)} copy-done((f32[384,512]{1,0:T(8,128)}, f32[384,512]{1,0:T(8,128)S(1)}, u32[]{:S(2)}) %copy-start.8) | copy-done | bytes 786456
  42.9 0.7 %copy-done.16 = bf16[384,512]{1,0:T(8,128)(2,1)} copy-done((bf16[384,512]{1,0:T(8,128)(2,1)}, bf16[384,512]{1,0:T(8,128)(2,1)S(1)}, u32[]{:S(2)}) %copy-start.16) | copy-done | bytes 393240
  45.7 4.4 %collective-permute-start.4 = (bf16[64,512]{1,0:T(8,128)(2,1)}, bf16[64,512]{1,0:T(8,128)(2,1)S(1)}, u32[]{:S(2)}, u32[]{:S(2)}) collective-permute-start(bf16[64,512]{1,0:T(8,128)(2,1)} %get-tuple-element.30), channel_id=1, source_target_pairs={{2,4},{4,2},{3,5},{5,3},{6,8},{8,6},{7,9},{9,7},{10,12},{12,10},{1... | collective-permute-start | bytes 196616 | tf_op jit(solution)/shard_map/ppermute | solution.py:381
  50.1 1.3 %reduce.1 = bf16[32,512]{1,0:T(8,128)(2,1)S(1)} reduce(bf16[32,1,512]{2,0,1:T(8,128)(2,1)} %bitcast.16, bf16[]{:T(256)} %broadcast), dimensions={1}, to_apply=%copy.25.reduce_sub_computation | reduce | bytes 65538 | tf_op jit(solution)/shard_map/all_to_all | solution.py:379
  52.1 2.5 %all-to-all-start.1 = ((bf16[32,2,256]{2,1,0:T(2,128)(2,1)}), bf16[32,2,256]{2,1,0:T(2,128)(2,1)S(1)}, u32[]{:S(2)}, u32[]{:S(2)}) async-start(bf16[32,2,256]{2,1,0:T(2,128)(2,1)} %reshape.36), calls=%async_computation.1 | async-start | bytes 65536 | tf_op jit(solution)/shard_map/all_to_all | solution.py:379
  54.6 0.9 %copy-done.26 = f32[64,512]{1,0:T(8,128)S(1)} copy-done((f32[64,512]{1,0:T(8,128)S(1)}, f32[64,512]{1,0:T(8,128)}, u32[]{:S(2)}) %copy-start.26) | copy-done | bytes 131096
  55.6 1.7 %collective-permute-start.5 = (bf16[32,512]{1,0:T(8,128)(2,1)S(1)}, bf16[32,512]{1,0:T(8,128)(2,1)S(1)}, u32[]{:S(2)}, u32[]{:S(2)}) collective-permute-start(bf16[32,512]{1,0:T(8,128)(2,1)S(1)} %get-tuple-element.33), channel_id=1, source_target_pairs={{0,1},{1,0},{2,3},{3,2},{4,5},{5,4},{6,7},{7,6},{8,9},{9,8},{10,11... | collective-permute-start | bytes 98312 | tf_op jit(solution)/shard_map/ppermute | solution.py:399
  57.3 1.1 %copy-done.9 = f32[384,512]{1,0:T(8,128)S(1)} copy-done((f32[384,512]{1,0:T(8,128)S(1)}, f32[384,512]{1,0:T(8,128)}, u32[]{:S(2)}) %copy-start.9) | copy-done | bytes 786456
  58.4 1.0 %copy-done.17 = bf16[384,512]{1,0:T(8,128)(2,1)S(1)} copy-done((bf16[384,512]{1,0:T(8,128)(2,1)S(1)}, bf16[384,512]{1,0:T(8,128)(2,1)}, u32[]{:S(2)}) %copy-start.17) | copy-done | bytes 393240
  59.4 0.8 %copy-done.28 = bf16[64,512]{1,0:T(8,128)(2,1)S(1)} copy-done((bf16[64,512]{1,0:T(8,128)(2,1)S(1)}, bf16[64,512]{1,0:T(8,128)(2,1)}, u32[]{:S(2)}) %copy-start.28) | copy-done | bytes 65560
  60.2 1.7 %behind.1 = (bf16[1,1,384,512]{3,2,1,0:T(8,128)(2,1)}, f32[64,512]{1,0:T(8,128)S(1)}) custom-call(s32[1,1]{1,0:T(1,128)S(6)} %copy.35.count.refs_0_, s32[1,1,384]{2,1,0:T(1,128)S(1)} %copy-done.32, s32[1,1,384]{2,1,0:T(1,128)S(1)} %copy-done.31, bf16[384,512]{1,0:T(8,128)(2,1)S(1)} %copy-done.17, bf16[64,512]{1,0:T(8,128)(2,1)S(1)} %copy-done.28, ...), custom_call_target="tpu_custom_call" | custom-call | flops 301989888 | bytes 3935236 | tf_op jit(solution)/shard_map/behind/pallas_call | solution.py:275
  62.0 0.8 %last.1 = bf16[1,1,64,512]{3,2,1,0:T(8,128)(2,1)} custom-call(f32[64,512]{1,0:T(8,128)S(1)} %get-tuple-element.27.refs_0_, f32[32,512]{1,0:T(8,128)S(1)} %get-tuple-element.31.refs_1_, s32[1,1,32]{2,1,0:T(1,128)S(1)} %copy-done.38, s32[1,1,1]{2,1,0:T(1,128)S(6)} %copy.36.coarse_list.refs_3_, bf16[32,512]{1,0:T(8,128)(2,1)S(1)} %bitcast.15, ...), custom_call_target="tpu_custom_call" | custom-call | bytes 262276 | tf_op jit(solution)/shard_map/last/pallas_call | solution.py:275
  (83 shorter events, 11.9 us)
Async XLA Ops:
  1.3 0.8 %copy-start.10 = (bf16[1,1,64,512]{3,2,1,0:T(8,128)(2,1)S(1)}, bf16[1,1,64,512]{3,2,1,0:T(8,128)(2,1)}, u32[]{:S(2)}) copy-start(bf16[1,1,64,512]{3,2,1,0:T(8,128)(2,1)} %refs_1_.1) | copy-start | bytes 196612
  2.8 27.0 %copy-start.15 = (bf16[1,1,384,512]{3,2,1,0:T(8,128)(2,1)S(1)}, bf16[1,1,384,512]{3,2,1,0:T(8,128)(2,1)}, u32[]{:S(2)}) copy-start(bf16[1,1,384,512]{3,2,1,0:T(8,128)(2,1)} %refs_21_.1) | copy-start | bytes 1179652
  3.0 4.9 %collective-permute-start = (bf16[32,512]{1,0:T(8,128)(2,1)S(1)}, bf16[32,512]{1,0:T(8,128)(2,1)S(1)}, u32[]{:S(2)}, u32[]{:S(2)}) collective-permute-start(bf16[32,512]{1,0:T(8,128)(2,1)S(1)} %get-tuple-element.19.refs_5_), channel_id=1, source_target_pairs={{0,1},{1,0},{2,3},{3,2},{4,5},{5,4},{6,7},{7,6},{8,9},{9,8},{10,11... | collective-permute-start | bytes 98312 | tf_op jit(solution)/shard_map/ppermute | solution.py:322
  9.1 20.7 %collective-permute-start.2 = (bf16[64,512]{1,0:T(8,128)(2,1)}, bf16[64,512]{1,0:T(8,128)(2,1)}, u32[]{:S(2)}, u32[]{:S(2)}) collective-permute-start(bf16[64,512]{1,0:T(8,128)(2,1)} %constant_dynamic-update-slice_fusion), channel_id=1, source_target_pairs={{2,4},{4,2},{3,5},{5,3},{6,8},{8,6},{7,9},{9,7},{10,12},{12,10},{1... | collective-permute-start | bytes 196616 | tf_op jit(solution)/shard_map/ppermute | solution.py:324
  12.5 17.3 %collective-permute-start.1 = (bf16[64,512]{1,0:T(8,128)(2,1)}, bf16[64,512]{1,0:T(8,128)(2,1)}, u32[]{:S(2)}, u32[]{:S(2)}) collective-permute-start(bf16[64,512]{1,0:T(8,128)(2,1)} %constant_dynamic-update-slice_fusion), channel_id=1, source_target_pairs={{0,2},{2,0},{1,3},{3,1},{4,6},{6,4},{5,7},{7,5},{8,10},{10,8},{9,1... | collective-permute-start | bytes 196616 | tf_op jit(solution)/shard_map/ppermute | solution.py:324
  14.1 13.4 %all-to-all-start = ((bf16[32,2,256]{2,1,0:T(2,128)(2,1)}), bf16[32,2,256]{2,1,0:T(2,128)(2,1)}, u32[]{:S(2)}, u32[]{:S(2)}) async-start(bf16[32,2,256]{2,1,0:T(2,128)(2,1)} %reshape.34), calls=%async_computation | async-start | bytes 65536 | tf_op jit(solution)/shard_map/all_to_all | solution.py:321
  18.6 1.4 %copy-start = (bf16[1536,512]{1,0:T(8,128)(2,1)S(1)}, bf16[1536,512]{1,0:T(8,128)(2,1)}, u32[]{:S(2)}) copy-start(bf16[1536,512]{1,0:T(8,128)(2,1)} %w_edge_in.3) | copy-start | bytes 4718596
  20.0 1.2 %copy-start.2 = (bf16[1024,512]{1,0:T(8,128)(2,1)S(1)}, bf16[1024,512]{1,0:T(8,128)(2,1)}, u32[]{:S(2)}) copy-start(bf16[1024,512]{1,0:T(8,128)(2,1)} %w_node_in.3) | copy-start | bytes 3145732
  21.2 1.0 %copy-start.4 = (bf16[1,1,384,512]{3,2,1,0:T(8,128)(2,1)S(1)}, bf16[1,1,384,512]{3,2,1,0:T(8,128)(2,1)}, u32[]{:S(2)}) copy-start(bf16[1,1,384,512]{3,2,1,0:T(8,128)(2,1)} %refs_2_.2) | copy-start | bytes 1179652
  25.1 4.7 %copy-start.1 = (bf16[1536,512]{1,0:T(8,128)(2,1)S(1)}, bf16[1536,512]{1,0:T(8,128)(2,1)}, u32[]{:S(2)}) copy-start(bf16[1536,512]{1,0:T(8,128)(2,1)} %w_edge_in.3) | copy-start | bytes 4718596
  25.1 4.7 %copy-start.3 = (bf16[1024,512]{1,0:T(8,128)(2,1)S(1)}, bf16[1024,512]{1,0:T(8,128)(2,1)}, u32[]{:S(2)}) copy-start(bf16[1024,512]{1,0:T(8,128)(2,1)} %w_node_in.3) | copy-start | bytes 3145732
  25.1 4.7 %copy-start.5 = (bf16[1,1,384,512]{3,2,1,0:T(8,128)(2,1)S(1)}, bf16[1,1,384,512]{3,2,1,0:T(8,128)(2,1)}, u32[]{:S(2)}) copy-start(bf16[1,1,384,512]{3,2,1,0:T(8,128)(2,1)} %refs_2_.2) | copy-start | bytes 1179652
  25.1 4.7 %copy-start.12 = (bf16[1,1,64,512]{3,2,1,0:T(8,128)(2,1)S(1)}, bf16[1,1,64,512]{3,2,1,0:T(8,128)(2,1)}, u32[]{:S(2)}) copy-start(bf16[1,1,64,512]{3,2,1,0:T(8,128)(2,1)} %refs_1_.1) | copy-start | bytes 196612
  25.1 4.7 %copy-start.18 = (bf16[1,1,64,512]{3,2,1,0:T(8,128)(2,1)S(1)}, bf16[1,1,64,512]{3,2,1,0:T(8,128)(2,1)}, u32[]{:S(2)}) copy-start(bf16[1,1,64,512]{3,2,1,0:T(8,128)(2,1)} %cot_node.1) | copy-start | bytes 196612
  25.1 4.7 %copy-start.31 = (s32[1,1,384]{2,1,0:T(1,128)S(1)}, s32[1,1,384]{2,1,0:T(1,128)}, u32[]{:S(2)}) copy-start(s32[1,1,384]{2,1,0:T(1,128)} %receivers.3) | copy-start | bytes 4612
  25.2 4.7 %copy-start.32 = (s32[1,1,384]{2,1,0:T(1,128)S(1)}, s32[1,1,384]{2,1,0:T(1,128)}, u32[]{:S(2)}) copy-start(s32[1,1,384]{2,1,0:T(1,128)} %senders.1) | copy-start | bytes 4612
  25.2 4.7 %copy-start.33 = (f32[512]{0:T(512)S(1)}, f32[512]{0:T(512)}, u32[]{:S(2)}) copy-start(f32[512]{0:T(512)} %param.29) | copy-start | bytes 6148
  25.2 4.7 %copy-start.34 = (f32[512]{0:T(512)S(1)}, f32[512]{0:T(512)}, u32[]{:S(2)}) copy-start(f32[512]{0:T(512)} %param.30) | copy-start | bytes 6148
  26.0 0.9 %copy-start.6 = (f32[384,512]{1,0:T(8,128)}, f32[384,512]{1,0:T(8,128)S(1)}, u32[]{:S(2)}) copy-start(f32[384,512]{1,0:T(8,128)S(1)} %get-tuple-element.21.refs_10_) | copy-start | bytes 2359300
  29.9 1.1 %copy-start.7 = (f32[384,512]{1,0:T(8,128)S(1)}, f32[384,512]{1,0:T(8,128)}, u32[]{:S(2)}) copy-start(f32[384,512]{1,0:T(8,128)} %copy-done.6) | copy-start | bytes 2359300
  31.1 1.0 %copy-start.13 = (bf16[512,512]{1,0:T(8,128)(2,1)S(1)}, bf16[512,512]{1,0:T(8,128)(2,1)}, u32[]{:S(2)}) copy-start(bf16[512,512]{1,0:T(8,128)(2,1)} %refs_13_.1) | copy-start | bytes 1572868
  32.1 1.0 %copy-start.14 = (bf16[512,512]{1,0:T(8,128)(2,1)S(1)}, bf16[512,512]{1,0:T(8,128)(2,1)}, u32[]{:S(2)}) copy-start(bf16[512,512]{1,0:T(8,128)(2,1)} %refs_17_.1) | copy-start | bytes 1572868
  34.7 0.9 %copy-start.24 = (f32[64,512]{1,0:T(8,128)S(1)}, f32[64,512]{1,0:T(8,128)}, u32[]{:S(2)}) copy-start(f32[64,512]{1,0:T(8,128)} %copy-done.23) | copy-start | bytes 393220
  42.0 0.9 %copy-start.8 = (f32[384,512]{1,0:T(8,128)}, f32[384,512]{1,0:T(8,128)S(1)}, u32[]{:S(2)}) copy-start(f32[384,512]{1,0:T(8,128)S(1)} %get-tuple-element.26.edge_cot) | copy-start | bytes 2359300
  45.5 9.1 %collective-permute-start.3 = (bf16[64,512]{1,0:T(8,128)(2,1)}, bf16[64,512]{1,0:T(8,128)(2,1)S(1)}, u32[]{:S(2)}, u32[]{:S(2)}) collective-permute-start(bf16[64,512]{1,0:T(8,128)(2,1)} %get-tuple-element.29), channel_id=1, source_target_pairs={{0,2},{2,0},{1,3},{3,1},{4,6},{6,4},{5,7},{7,5},{8,10},{10,8},{9,1... | collective-permute-start | bytes 196616 | tf_op jit(solution)/shard_map/ppermute | solution.py:381
  45.7 8.9 %collective-permute-start.4 = (bf16[64,512]{1,0:T(8,128)(2,1)}, bf16[64,512]{1,0:T(8,128)(2,1)S(1)}, u32[]{:S(2)}, u32[]{:S(2)}) collective-permute-start(bf16[64,512]{1,0:T(8,128)(2,1)} %get-tuple-element.30), channel_id=1, source_target_pairs={{2,4},{4,2},{3,5},{5,3},{6,8},{8,6},{7,9},{9,7},{10,12},{12,10},{1... | collective-permute-start | bytes 196616 | tf_op jit(solution)/shard_map/ppermute | solution.py:381
  52.1 9.9 %all-to-all-start.1 = ((bf16[32,2,256]{2,1,0:T(2,128)(2,1)}), bf16[32,2,256]{2,1,0:T(2,128)(2,1)S(1)}, u32[]{:S(2)}, u32[]{:S(2)}) async-start(bf16[32,2,256]{2,1,0:T(2,128)(2,1)} %reshape.36), calls=%async_computation.1 | async-start | bytes 65536 | tf_op jit(solution)/shard_map/all_to_all | solution.py:379
  54.6 0.9 %copy-start.26 = (f32[64,512]{1,0:T(8,128)S(1)}, f32[64,512]{1,0:T(8,128)}, u32[]{:S(2)}) copy-start(f32[64,512]{1,0:T(8,128)} %copy-done.25) | copy-start | bytes 393220
  55.6 6.4 %collective-permute-start.5 = (bf16[32,512]{1,0:T(8,128)(2,1)S(1)}, bf16[32,512]{1,0:T(8,128)(2,1)S(1)}, u32[]{:S(2)}, u32[]{:S(2)}) collective-permute-start(bf16[32,512]{1,0:T(8,128)(2,1)S(1)} %get-tuple-element.33), channel_id=1, source_target_pairs={{0,1},{1,0},{2,3},{3,2},{4,5},{5,4},{6,7},{7,6},{8,9},{9,8},{10,11... | collective-permute-start | bytes 98312 | tf_op jit(solution)/shard_map/ppermute | solution.py:399
  57.3 1.1 %copy-start.9 = (f32[384,512]{1,0:T(8,128)S(1)}, f32[384,512]{1,0:T(8,128)}, u32[]{:S(2)}) copy-start(f32[384,512]{1,0:T(8,128)} %copy-done.8) | copy-start | bytes 2359300
  58.4 1.0 %copy-start.17 = (bf16[384,512]{1,0:T(8,128)(2,1)S(1)}, bf16[384,512]{1,0:T(8,128)(2,1)}, u32[]{:S(2)}) copy-start(bf16[384,512]{1,0:T(8,128)(2,1)} %copy-done.16) | copy-start | bytes 1179652
  60.2 1.8 %copy-start.38 = (s32[1,1,32]{2,1,0:T(1,128)S(1)}, s32[1,1,32]{2,1,0:T(1,128)}, u32[]{:S(2)}) copy-start(s32[1,1,32]{2,1,0:T(1,128)} %refs_2_.3) | copy-start | bytes 388
  (17 other events, 11.8 us)

commit v2 on v1

v2 whole, which is shorter than its diff:
```python
import functools

import jax
import jax.numpy as jnp
from jax import lax
from jax.experimental import pallas as pl
from jax.experimental.pallas import tpu as pltpu
from jax.sharding import PartitionSpec as P

F32 = jnp.float32
BF16 = jnp.bfloat16
VMEM = pltpu.VMEM


def dot_nn(a, b):
    return jnp.dot(a, b, preferred_element_type=F32)


def dot_tn(a, b):
    return lax.dot_general(a, b, (((0,), (0,)), ((), ())), preferred_element_type=F32)


def dot_nt(a, b):
    return lax.dot_general(a, b, (((1,), (1,)), ((), ())), preferred_element_type=F32)


def as_one_hot(mask):
    return jnp.where(mask, 1.0, 0.0).astype(BF16)


def one_hot_rows(index_row, rows):
    return lax.broadcasted_iota(jnp.int32, (rows, index_row.shape[1]), 0) == index_row


def live_one_hot(index_row, rows, count):
    lanes = lax.broadcasted_iota(jnp.int32, (rows, index_row.shape[1]), 1)
    return as_one_hot(one_hot_rows(index_row, rows) & (lanes < count))


def in_two(values):
    head = values.astype(BF16)
    tail = (values - head.astype(F32)).astype(BF16)
    return jnp.concatenate([head, tail], axis=0)


def normed_rows(out_rows):
    centre = out_rows - jnp.mean(out_rows, axis=1, keepdims=True)
    inv_std = lax.rsqrt(jnp.mean(centre * centre, axis=1, keepdims=True) + 1e-05)
    return centre * inv_std, inv_std


def norm_backward(grad_norm, normed, inv_std):
    return inv_std * (
        grad_norm
        - jnp.mean(grad_norm, axis=1, keepdims=True)
        - normed * jnp.mean(grad_norm * normed, axis=1, keepdims=True)
    )


def silu_slope(pre, sig):
    return sig * (1.0 + pre * (1.0 - sig))


class Moves:
    def __init__(self, sems):
        self.sems, self.used = sems, 0

    def start(self, source, target):
        copy = pltpu.make_async_copy(source, target, self.sems.at[self.used])
        self.used += 1
        copy.start()
        return copy


class Fetched:
    def __init__(self, moves, source, scratch):
        self.copy, self.scratch, self.waited = moves.start(source, scratch), scratch, False

    def __call__(self):
        if not self.waited:
            self.copy.wait()
            self.waited = True
        return self.scratch


class Plan:
    def __init__(self, lon, lat, nodes, edges, halo, owned, width):
        self.lon, self.lat = lon, lat
        self.nodes, self.edges, self.halo, self.owned, self.width = nodes, edges, halo, owned, width
        self.devices = lon * lat
        self.coarse = self.devices * owned
        flat = lambda i, j: (i % lon) * lat + j
        swap = lambda pairs: [p for a, b in pairs for p in ((a, b), (b, a))]
        lat_sets = [
            [(k, k + 1) for k in range(0, lat - 1, 2)],
            [(k, k + 1) for k in range(1, lat - 1, 2)],
        ]
        self.lat_pairs = [
            swap([(flat(i, a), flat(i, b)) for i in range(lon) for a, b in pairs])
            for pairs in lat_sets
            if pairs
        ]
        self.lon_pairs = [
            swap([(flat(i, j), flat(i + 1, j)) for i in range(first, lon, 2) for j in range(lat)])
            for first in (0, 1)
        ]
        self.per_lon = 1 + len(self.lat_pairs)
        self.blocks = 3 * self.per_lon
        self.table = nodes + self.blocks * halo + self.coarse

    def positions(self, sender):
        nodes, halo = self.nodes, self.halo
        lon_odd = lax.rem(lax.axis_index("lon"), 2)
        lat_odd = lax.rem(lax.axis_index("lat"), 2)
        lon_step = [1, 2 - 2 * lon_odd, 2 * lon_odd]
        lat_step = [1, 2 - 2 * lat_odd, 2 * lat_odd][: self.per_lon]
        past = sender - (nodes + 9 * halo)
        if self.owned > 1:
            past = jnp.where(
                past >= 0, lax.rem(past, self.owned) * self.devices + past // self.owned, past
            )
        found = jnp.where(past >= 0, past + (nodes + self.blocks * halo), sender)
        place = 0
        for a in lon_step:
            for b in lat_step:
                row = sender - (nodes + (3 * a + b) * halo)
                inside = (row >= 0) & (row < halo) & (sender >= nodes)
                found = jnp.where(inside, row + (nodes + place * halo), found)
                place += 1
        return found


def pack_kernel(plan, node, halo_list, coarse_list, border, coarse, node_s, halo_s, list_s, sems):
    moves = Moves(sems)
    node, halo_list, coarse_list = [
        Fetched(moves, *pair)
        for pair in ((node, node_s), (halo_list, halo_s), (coarse_list, list_s))
    ]
    pick = as_one_hot(one_hot_rows(halo_list()[0], plan.nodes))
    border[...] = dot_tn(pick, node()[0, 0]).astype(BF16)
    own = dot_tn(as_one_hot(one_hot_rows(coarse_list()[0], plan.nodes)), node()[0, 0])
    parts = plan.width // 128
    for k in range(plan.owned):
        for q in range(parts):
            piece = own[k : k + 1, q * 128 : (q + 1) * 128]
            coarse[:, k * parts + q, :] = jnp.broadcast_to(piece, (plan.devices, 128))


def ahead_kernel(plan, *refs):
    operands, (edge_part, node_part), scratch = refs[:8], refs[8:10], refs[10:]
    moves = Moves(scratch[-1])
    width = plan.width
    count, receivers, node, edge, w_node_in, b_node_in, w_edge_in, b_edge_in = [
        Fetched(moves, source.at[: held.shape[0]], held)
        for source, held in zip(operands, scratch[:-1])
    ]
    received = live_one_hot(receivers()[0], plan.nodes, count()[...])
    rows = node()[0, 0]
    node_part[...] = dot_nn(rows, w_node_in()[...]) + b_node_in()[...]
    at_receiver = dot_tn(received, rows).astype(BF16)
    edge_part[...] = (
        dot_nn(edge()[0, 0], w_edge_in()[:width])
        + dot_nn(at_receiver, w_edge_in()[2 * width :])
        + b_edge_in()[...]
    )


def main_kernel(plan, *refs):
    lats = plan.per_lon - 1
    total = plan.main_operands
    operands, outs, scratch = refs[:total], refs[total : total + 8], refs[total + 8 :]
    sems, table, out_vmem = scratch[-1], scratch[total], scratch[total + 1 : -1]
    moves = Moves(sems)
    nodes, halo, width = plan.nodes, plan.halo, plan.width
    start = nodes
    got = {}
    for k, (name, source) in enumerate(zip(plan.main_names, operands)):
        if name in ("w_edge_in", "w_node_in"):
            source = source.at[width : 2 * width]
        got[name] = Fetched(moves, source, scratch[k])
    count, node, edge, senders, receivers = [
        got[name] for name in ("count", "node", "edge", "senders", "receivers")
    ]
    live_count = count()[...]
    sent = as_one_hot(one_hot_rows(plan.positions(senders()[0]), plan.table))
    received = live_one_hot(receivers()[0], nodes, live_count)
    live = jnp.where(
        lax.broadcasted_iota(jnp.int32, (plan.edges, 1), 0) < live_count, 1.0, 0.0
    ).astype(F32)

    table[:nodes] = node()[0, 0]
    for name in plan.rim_names:
        part = got[name]()
        table[start : start + part.shape[0]] = part[...]
        start += part.shape[0]
    parts = width // 128
    for k in range(plan.owned):
        for q in range(parts):
            table[start : start + plan.devices, q * 128 : (q + 1) * 128] = got["coarse_rows"]()[
                :, k * parts + q, :
            ].astype(BF16)
        start += plan.devices

    at_sender = dot_tn(sent, table[...]).astype(BF16)
    edge_pre = got["edge_part"]()[...] + dot_nn(at_sender, got["w_edge_in"]()[...])
    edge_sig = jax.nn.sigmoid(edge_pre)
    edge_out = dot_nn((edge_pre * edge_sig).astype(BF16), got["w_edge_out"]()[...])
    edge_normed, edge_rstd = normed_rows(edge_out)
    edge_upd = edge_normed * got["gain_edge"]()[...] + got["shift_edge"]()[...]
    new_edge = (edge()[0, 0].astype(F32) + live * edge_upd).astype(BF16)
    aggregated = dot_nn(received, new_edge).astype(BF16)

    gain_node = got["gain_node"]()
    node_pre = got["node_part"]()[...] + dot_nn(aggregated, got["w_node_in"]()[...])
    node_sig = jax.nn.sigmoid(node_pre)
    node_out = dot_nn((node_pre * node_sig).astype(BF16), got["w_node_out"]()[...])
    node_normed, node_rstd = normed_rows(node_out)

    node_dout = norm_backward(
        got["cot_node"]()[0, 0].astype(F32) * gain_node[...], node_normed, node_rstd
    ).astype(BF16)
    node_dpre = (
        dot_nt(node_dout, got["w_node_out"]()[...]) * silu_slope(node_pre, node_sig)
    ).astype(BF16)
    agg_grad = dot_nt(node_dpre, got["w_node_in"]()[...])
    twice = jnp.concatenate([received, received], axis=0)
    edge_cot = got["cot_edge"]()[0, 0].astype(F32) + dot_tn(twice, in_two(agg_grad))

    edge_dout = norm_backward(
        live * edge_cot * got["gain_edge"]()[...], edge_normed, edge_rstd
    ).astype(BF16)
    edge_dpre = (
        dot_nt(edge_dout, got["w_edge_out"]()[...]) * silu_slope(edge_pre, edge_sig)
    ).astype(BF16)
    away = dot_nn(sent[nodes:], edge_dpre).astype(BF16)
    away_grad = dot_nt(away, got["w_edge_in"]()[...])
    kept = plan.per_lon * halo
    (even_out, odd_out, coarse_out, kept_out, new_out, cot_out, edpre_out, ndpre_out) = out_vmem
    even_out[...] = away_grad[kept : 2 * kept].astype(BF16)
    odd_out[...] = away_grad[2 * kept : 3 * kept].astype(BF16)
    start = 3 * kept
    for k in range(plan.owned):
        for q in range(parts):
            coarse_out[:, k * parts + q, :] = away_grad[
                start : start + plan.devices, q * 128 : (q + 1) * 128
            ]
        start += plan.devices
    copies = [moves.start(out_vmem[k], outs[k]) for k in range(3)]
    kept_out[...] = away_grad[:kept]
    node_upd = node_normed * gain_node[...] + got["shift_node"]()[...]
    new_out[0, 0] = (node()[0, 0].astype(F32) + node_upd).astype(BF16)
    cot_out[...] = edge_cot
    edpre_out[...] = edge_dpre
    ndpre_out[...] = node_dpre
    copies += [moves.start(out_vmem[k], outs[k]) for k in range(3, 8)]
    for copy in copies:
        copy.wait()


def behind_kernel(plan, *refs):
    operands, (grad_edges, grad_local), scratch = refs[:9], refs[9:11], refs[11:]
    moves = Moves(scratch[-1])
    (
        count,
        senders,
        receivers,
        edge_dpre,
        node_dpre,
        cot_node,
        w_node_in,
        edge_cot,
        w_edge_in,
    ) = [
        Fetched(moves, source.at[: held.shape[0]], held)
        for source, held in zip(operands, scratch[:-1])
    ]
    width, nodes = plan.width, plan.nodes
    received = live_one_hot(receivers()[0], nodes, count()[...])
    sent = as_one_hot(one_hot_rows(senders()[0], nodes))
    dpre = edge_dpre()[...]
    both = dot_nn(jnp.concatenate([sent, received], axis=0), dpre).astype(BF16)
    from_node = dot_nt(node_dpre()[...], w_node_in()[...])
    weights = w_edge_in()
    grad_local[...] = (
        cot_node()[0, 0].astype(F32)
        + from_node
        + dot_nt(both[:nodes], weights[width : 2 * width])
        + dot_nt(both[nodes:], weights[2 * width :])
    )
    grad_edges[0, 0] = (edge_cot()[...] + dot_nt(dpre, weights[:width])).astype(BF16)


def join_kernel(*refs):
    start = 0
    for part in refs[:-1]:
        refs[-1][start : start + part.shape[0]] = part[...]
        start += part.shape[0]


def middle_kernel(plan, kept, even, odd, mine, *lat_sends):
    total = kept[...] + even[...].astype(F32) + odd[...].astype(F32)
    mine[...] = total[: plan.halo]
    for k, out in enumerate(lat_sends):
        out[...] = total[(k + 1) * plan.halo : (k + 2) * plan.halo].astype(BF16)


def last_kernel(plan, *refs):
    lats = plan.per_lon - 1
    grad_local, mine, halo_list, coarse_list, coarse = refs[:5]
    out = refs[-1]
    total = mine[...]
    for part in refs[5 : 5 + lats]:
        total = total + part[...].astype(F32)
    place = as_one_hot(one_hot_rows(halo_list[0], plan.nodes))
    result = grad_local[...] + dot_nn(jnp.concatenate([place, place], axis=1), in_two(total))
    share = jnp.sum(coarse[...], axis=0)
    at_row = lax.broadcasted_iota(jnp.int32, (plan.nodes, 1), 0)
    parts = plan.width // 128
    for k in range(plan.owned):
        row = jnp.concatenate([share[k * parts + q : k * parts + q + 1] for q in range(parts)], axis=1)
        result = result + jnp.where(at_row == coarse_list[0, :, k : k + 1], row, 0.0)
    out[0, 0] = result.astype(BF16)


def call(body, name, outs, operands, scratch=(), flops=0, mib=8, copied=False):
    whole = pl.BlockSpec(memory_space=VMEM)
    moved = sum(a.size * a.dtype.itemsize for a in operands)
    return pl.pallas_call(
        body,
        name=name,
        out_shape=[jax.ShapeDtypeStruct(shape, dtype) for shape, dtype in outs],
        in_specs=[pl.BlockSpec(memory_space=pl.ANY) if scratch else whole] * len(operands),
        out_specs=[pl.BlockSpec(memory_space=pl.ANY) if copied else whole] * len(outs),
        scratch_shapes=list(scratch),
        compiler_params=pltpu.CompilerParams(vmem_limit_bytes=mib * 1024 * 1024),
        cost_estimate=pl.CostEstimate(flops=flops, bytes_accessed=moved, transcendentals=0),
    )(*operands)


def like(arrays, cut=-1):
    return [
        pltpu.VMEM((a.shape[0] // 2 if k == cut else a.shape[0],) + a.shape[1:], a.dtype)
        for k, a in enumerate(arrays)
    ]


def sems(count):
    return pltpu.SemaphoreType.DMA((count,))


def body(
    plan,
    node_feat,
    edge_feat,
    senders,
    receivers,
    edge_count,
    halo_list,
    coarse_list,
    w_edge_in,
    b_edge_in,
    w_edge_out,
    gain_edge,
    shift_edge,
    w_node_in,
    b_node_in,
    w_node_out,
    gain_node,
    shift_node,
    cot_node,
    cot_edge,
):
    axes = ("lon", "lat")
    halo, width, nodes, edges = plan.halo, plan.width, plan.nodes, plan.edges
    row = lambda vec: vec.reshape(1, width)
    with_plan = lambda kernel: functools.partial(kernel, plan)
    coarse_shape = (plan.devices, plan.owned * width // 128, 128)

    operands = [node_feat, halo_list, coarse_list]
    border, coarse_out = call(
        with_plan(pack_kernel),
        "pack",
        [((halo, width), BF16), (coarse_shape, F32)],
        operands,
        scratch=like(operands) + [sems(3)],
        mib=56,
    )
    coarse_rows = lax.all_to_all(coarse_out, axes, 0, 0, tiled=True)
    lat_rows = [lax.ppermute(border, axes, pairs) for pairs in plan.lat_pairs]
    (wide,) = call(
        join_kernel, "join", [((plan.per_lon * halo, width), BF16)], [border, *lat_rows]
    )
    even_rows, odd_rows = [lax.ppermute(wide, axes, pairs) for pairs in plan.lon_pairs]

    operands = [
        edge_count,
        receivers,
        node_feat,
        edge_feat,
        w_node_in,
        row(b_node_in),
        w_edge_in,
        row(b_edge_in),
    ]
    edge_part, node_part = call(
        with_plan(ahead_kernel),
        "ahead",
        [((edges, width), F32), ((nodes, width), F32)],
        operands,
        scratch=like(operands, 4) + [sems(len(operands))],
        flops=2 * (2 * edges + nodes) * width * width,
        mib=56,
    )

    kept = plan.per_lon * halo
    named = {
        "count": edge_count,
        "senders": senders,
        "receivers": receivers,
        "node": node_feat,
        "wide": wide,
        "even_rows": even_rows,
        "odd_rows": odd_rows,
        "coarse_rows": coarse_rows,
        "w_edge_in": w_edge_in,
        "edge_part": edge_part,
        "w_edge_out": w_edge_out,
        "gain_edge": row(gain_edge),
        "shift_edge": row(shift_edge),
        "edge": edge_feat,
        "w_node_in": w_node_in,
        "node_part": node_part,
        "w_node_out": w_node_out,
        "gain_node": row(gain_node),
        "cot_node": cot_node,
        "cot_edge": cot_edge,
        "shift_node": row(shift_node),
    }
    plan.main_names = list(named)
    plan.rim_names = ["wide", "even_rows", "odd_rows"]
    plan.main_operands = len(named)
    outs = [
        ((kept, width), BF16),
        ((kept, width), BF16),
        (coarse_shape, F32),
        ((kept, width), F32),
        (node_feat.shape, BF16),
        ((edges, width), F32),
        ((edges, width), BF16),
        ((nodes, width), BF16),
    ]
    operands = list(named.values())
    parts_of = {"w_edge_in": (width, width), "w_node_in": (width, width)}
    even_grad, odd_grad, coarse_grad, kept_grad, new_nodes, edge_cot, edge_dpre, node_dpre = call(
        with_plan(main_kernel),
        "main",
        outs,
        operands,
        scratch=[
            pltpu.VMEM(parts_of.get(name, a.shape), a.dtype) for name, a in named.items()
        ]
        + [pltpu.VMEM((plan.table, width), BF16)]
        + [pltpu.VMEM(shape, dtype) for shape, dtype in outs]
        + [sems(len(named) + len(outs))],
        flops=2 * 5 * edges * width * width,
        mib=56,
        copied=True,
    )

    coarse_back = lax.all_to_all(coarse_grad, axes, 0, 0, tiled=True)
    even_back, odd_back = [
        lax.ppermute(grad, axes, pairs)
        for grad, pairs in zip((even_grad, odd_grad), plan.lon_pairs)
    ]
    operands = [
        edge_count,
        senders,
        receivers,
        edge_dpre,
        node_dpre,
        cot_node,
        w_node_in,
        edge_cot,
        w_edge_in,
    ]
    grad_edges, grad_local = call(
        with_plan(behind_kernel),
        "behind",
        [(edge_feat.shape, BF16), ((nodes, width), F32)],
        operands,
        scratch=like(operands, 6) + [sems(len(operands))],
        flops=2 * (edges + 3 * nodes) * width * width,
        mib=56,
    )
    mine, *lat_sends = call(
        with_plan(middle_kernel),
        "middle",
        [((halo, width), F32)] + [((halo, width), BF16)] * len(plan.lat_pairs),
        [kept_grad, even_back, odd_back],
    )
    lat_back = [
        lax.ppermute(grad, axes, pairs) for grad, pairs in zip(lat_sends, plan.lat_pairs)
    ]
    (grad_nodes,) = call(
        with_plan(last_kernel),
        "last",
        [(node_feat.shape, BF16)],
        [grad_local, mine, halo_list, coarse_list, coarse_back, *lat_back],
    )
    return new_nodes, grad_nodes, grad_edges


def solution(mesh):
    lon, lat = mesh.shape["lon"], mesh.shape["lat"]
    cells = lambda rank: P("lon", "lat", *([None] * (rank - 2)))

    def sharded(*args):
        node_feat, edge_feat, halo_list, coarse_list = args[0], args[1], args[5], args[6]
        plan = Plan(
            lon,
            lat,
            node_feat.shape[2],
            edge_feat.shape[2],
            halo_list.shape[2],
            coarse_list.shape[2],
            node_feat.shape[3],
        )
        return body(plan, *args)

    ranks = (4, 4, 3, 3, 2, 3, 3)
    return jax.shard_map(
        sharded,
        mesh=mesh,
        in_specs=tuple(cells(r) for r in ranks) + (P(),) * 10 + (cells(4), cells(4)),
        out_specs=(cells(4), cells(4), cells(4)),
        check_vma=False,
    )
```

time: 64.1 us -> 49.5 us (0.77); the launches traced: 62.9 us -> 49 us
  local copies, waits for them, and re-layouts: 30.5 us -> 3.18 us
  Pallas kernels: 8.61 us -> 16.5 us
  waiting for transfers between devices: 0.68 us -> 5.11 us
  starting transfers between devices: 19 us -> 22.2 us
  other arithmetic: 1.86 us -> 0 us
    unnamed x89 -> x16, local copies, waits for them, and re-layouts: 29.4 us -> 3.18 us
    pallas_call x6 -> x7, Pallas kernels: 8.61 us -> 16.5 us  [call(): pl.pallas_call(body, name=name, out_shape=[jax.ShapeDtypeStruct(shape, dt...]
    all_to_all x1, starting transfers between devices: 3.81 us -> 7.3 us  [body(): coarse_rows = lax.all_to_all(coarse_out, axes, 0, 0, tiled=True)]
    ppermute x3, waiting for transfers between devices: 0.01 us -> 2.68 us  [body(): lax.ppermute(grad, axes, pairs)]
    all_to_all x2 -> x0, other arithmetic: 1.86 us -> none  [the longest x1 1.31 us: body(): coarse_back = lax.all_to_all(coarse_grad, axes, 0, 0, tiled=True)]
    ppermute x1, waiting for transfers between devices: 0.66 us -> 2.41 us  [body(): lat_rows = [lax.ppermute(border, axes, pairs) for pairs in plan.lat_pairs]]
    ppermute x1, starting transfers between devices: 3 us -> 1.83 us  [body(): lat_rows = [lax.ppermute(border, axes, pairs) for pairs in plan.lat_pairs]]
  transfers between devices with their start and end apart: 8 -> 8, of which waited for: 1 -> 2; matrix products, arithmetic and copies ran while one was open for 10% -> 0% of each run, Pallas kernels for 4% -> 14%
where the time goes in v2:
time: 49.5 us; the launch traced here: 49 us
  starting transfers between devices  22.2 us (45%)
  Pallas kernels  16.5 us (33%)
  waiting for transfers between devices  5.11 us (10%)
  local copies, waits for them, and re-layouts  3.18 us (6%)
  between operations  2.08 us (4%)
    pallas_call x7, Pallas kernels, call(): pl.pallas_call(body, name=name, out_shape=[jax.ShapeDtypeStruct(shape, dt...  16.5 us
    all_to_all x1, starting transfers between devices, body(): coarse_rows = lax.all_to_all(coarse_out, axes, 0, 0, tiled=True)  7.3 us
    ppermute x3, starting transfers between devices, body(): lax.ppermute(grad, axes, pairs)  6.28 us
    ppermute x2, starting transfers between devices, body(): lax.ppermute(wide, axes, pairs)  3.81 us
    unnamed x16, local copies, waits for them, and re-layouts  3.18 us
    all_to_all x1, starting transfers between devices, body(): coarse_back = lax.all_to_all(coarse_grad, axes, 0, 0, tiled=True)  2.98 us
    ppermute x3, waiting for transfers between devices, body(): lax.ppermute(grad, axes, pairs)  2.68 us
    ppermute x1, waiting for transfers between devices, body(): lat_rows = [lax.ppermute(border, axes, pairs) for pairs in plan.lat_pairs]  2.41 us
  transfers between devices with their start and end apart: 8, of which 2 were waited for; matrix products, arithmetic and copies ran while one was open for 0% of the time, Pallas kernels for 14%

profile of v2, /device:TPU:0, one launch (start us, length us, event | category | flops | bytes accessed | tf_op | source)
XLA Modules:
  0.0 49.0 jit_solution(14752336189297517003)
XLA Ops:
  1.3 1.9 %pack.1 = (bf16[32,512]{1,0:T(8,128)(2,1)}, f32[32,4,128]{2,1,0:T(4,128)}) custom-call(bf16[1,1,64,512]{3,2,1,0:T(8,128)(2,1)} %refs_3_.4, s32[1,1,32]{2,1,0:T(1,128)} %refs_2_.7, s32[1,1,1]{2,1,0:T(1,128)S(6)} %copy.23.coarse_list.refs_3_), custom_call_target="tpu_custom_call" | custom-call | bytes 65668 | tf_op jit(solution)/shard_map/pack/pallas_call | solution.py:328
  3.2 7.3 %all-to-all-start = ((f32[32,4,128]{2,1,0:T(4,128)}), f32[32,4,128]{2,1,0:T(4,128)S(1)}, u32[]{:S(2)}, u32[]{:S(2)}) async-start(f32[32,4,128]{2,1,0:T(4,128)} %get-tuple-element.20), calls=%async_computation | async-start | bytes 131072 | tf_op jit(solution)/shard_map/all_to_all | solution.py:388
  10.5 1.8 %collective-permute-start = (bf16[32,512]{1,0:T(8,128)(2,1)}, bf16[32,512]{1,0:T(8,128)(2,1)S(1)}, u32[]{:S(2)}, u32[]{:S(2)}) collective-permute-start(bf16[32,512]{1,0:T(8,128)(2,1)} %get-tuple-element.19.refs_0_), channel_id=1, source_target_pairs={{0,1},{1,0},{2,3},{3,2},{4,5},{5,4},{6,7},{7,6},{8,9},{9,8},{10,11... | collective-permute-start | bytes 98312 | tf_op jit(solution)/shard_map/ppermute | solution.py:389
  12.3 2.4 %collective-permute-done.refs_1_ = bf16[32,512]{1,0:T(8,128)(2,1)S(1)} collective-permute-done((bf16[32,512]{1,0:T(8,128)(2,1)}, bf16[32,512]{1,0:T(8,128)(2,1)S(1)}, u32[]{:S(2)}, u32[]{:S(2)}) %collective-permute-start) | collective-permute-done | bytes 32800 | tf_op jit(solution)/shard_map/ppermute | solution.py:389
  14.7 0.8 %copy-done.3 = bf16[32,512]{1,0:T(8,128)(2,1)S(1)} copy-done((bf16[32,512]{1,0:T(8,128)(2,1)S(1)}, bf16[32,512]{1,0:T(8,128)(2,1)}, u32[]{:S(2)}) %copy-start.3) | copy-done | bytes 32792
  15.5 3.8 %collective-permute-start.2 = (bf16[64,512]{1,0:T(8,128)(2,1)S(1)}, bf16[64,512]{1,0:T(8,128)(2,1)S(1)}, u32[]{:S(2)}, u32[]{:S(2)}) collective-permute-start(bf16[64,512]{1,0:T(8,128)(2,1)S(1)} %join.1.refs_4_), channel_id=1, source_target_pairs={{2,4},{4,2},{3,5},{5,3},{6,8},{8,6},{7,9},{9,7},{10,12},{12,10},{1... | collective-permute-start | bytes 196616 | tf_op jit(solution)/shard_map/ppermute | solution.py:393
  19.3 0.0 collective-permute-start.1
  19.9 3.4 %ahead.1 = (f32[384,512]{1,0:T(8,128)}, f32[64,512]{1,0:T(8,128)}) custom-call(s32[1,1]{1,0:T(1,128)S(6)} %copy.22.refs_0_, s32[1,1,384]{2,1,0:T(1,128)} %refs_2_.6, bf16[1,1,64,512]{3,2,1,0:T(8,128)(2,1)} %refs_3_.4, bf16[1,1,384,512]{3,2,1,0:T(8,128)(2,1)} %refs_13_.1, bf16[1024,512]{1,0:T(8,128)(2,1)} %refs_6_.3, f32[1,512]{1,0:T(1,128)} %bitcast.10, ...), custom_call_target="tpu_custom_call" | custom-call | flops 436207616 | bytes 3085828 | tf_op jit(solution)/shard_map/ahead/pallas_call | solution.py:328
  23.3 0.0 collective-permute-done.2.refs_6_
  23.3 0.0 copy-start.6
  23.4 0.0 collective-permute-done.1.refs_5_
  23.4 0.0 copy-start.7
  23.4 0.0 all-to-all-done.refs_7_
  23.4 0.0 copy-start.5
  23.4 0.6 %copy-done.6 = bf16[64,512]{1,0:T(8,128)(2,1)} copy-done((bf16[64,512]{1,0:T(8,128)(2,1)}, bf16[64,512]{1,0:T(8,128)(2,1)S(1)}, u32[]{:S(2)}) %copy-start.6) | copy-done | bytes 65560
  24.0 0.0 copy-done.7
  24.0 0.0 copy-done.5
  24.0 6.6 %main.1 = (bf16[64,512]{1,0:T(8,128)(2,1)}, bf16[64,512]{1,0:T(8,128)(2,1)}, f32[32,4,128]{2,1,0:T(4,128)}, f32[64,512]{1,0:T(8,128)}, bf16[1,1,64,512]{3,2,1,0:...) custom-call(s32[1,1]{1,0:T(1,128)S(6)} %copy.22.refs_0_, ...), custom_call_target="tpu_custom_call" | custom-call | flops 1006632960 | bytes 5778436 | tf_op jit(solution)/shard_map/main/pallas_call | solution.py:328
  30.7 3.0 %all-to-all-start.1 = ((f32[32,4,128]{2,1,0:T(4,128)}), f32[32,4,128]{2,1,0:T(4,128)S(1)}, u32[]{:S(2)}, u32[]{:S(2)}) async-start(f32[32,4,128]{2,1,0:T(4,128)} %get-tuple-element.32), calls=%async_computation.1 | async-start | bytes 131072 | tf_op jit(solution)/shard_map/all_to_all | solution.py:470
  33.6 0.3 collective-permute-start.3
  34.0 4.4 %collective-permute-start.4 = (bf16[64,512]{1,0:T(8,128)(2,1)}, bf16[64,512]{1,0:T(8,128)(2,1)S(1)}, u32[]{:S(2)}, u32[]{:S(2)}) collective-permute-start(bf16[64,512]{1,0:T(8,128)(2,1)} %get-tuple-element.30), channel_id=1, source_target_pairs={{2,4},{4,2},{3,5},{5,3},{6,8},{8,6},{7,9},{9,7},{10,12},{12,10},{1... | collective-permute-start | bytes 196616 | tf_op jit(solution)/shard_map/ppermute | solution.py:472
  38.4 0.0 collective-permute-done.3.even
  38.4 2.7 %collective-permute-done.4.odd = bf16[64,512]{1,0:T(8,128)(2,1)S(1)} collective-permute-done((bf16[64,512]{1,0:T(8,128)(2,1)}, bf16[64,512]{1,0:T(8,128)(2,1)S(1)}, u32[]{:S(2)}, u32[]{:S(2)}) %collective-permute-start.4) | collective-permute-done | bytes 65568 | tf_op jit(solution)/shard_map/ppermute | solution.py:472
  41.1 0.9 %copy-done.1 = f32[64,512]{1,0:T(8,128)S(1)} copy-done((f32[64,512]{1,0:T(8,128)S(1)}, f32[64,512]{1,0:T(8,128)}, u32[]{:S(2)}) %copy-start.1) | copy-done | bytes 131096
  42.0 1.5 %collective-permute-start.5 = (bf16[32,512]{1,0:T(8,128)(2,1)S(1)}, bf16[32,512]{1,0:T(8,128)(2,1)S(1)}, u32[]{:S(2)}, u32[]{:S(2)}) collective-permute-start(bf16[32,512]{1,0:T(8,128)(2,1)S(1)} %get-tuple-element.33), channel_id=1, source_target_pairs={{0,1},{1,0},{2,3},{3,2},{4,5},{5,4},{6,7},{7,6},{8,9},{9,8},{10,11... | collective-permute-start | bytes 98312 | tf_op jit(solution)/shard_map/ppermute | solution.py:502
  43.5 3.7 %behind.1 = (bf16[1,1,384,512]{3,2,1,0:T(8,128)(2,1)}, f32[64,512]{1,0:T(8,128)}) custom-call(s32[1,1]{1,0:T(1,128)S(6)} %copy.22.refs_0_, s32[1,1,384]{2,1,0:T(1,128)} %refs_1_.5, s32[1,1,384]{2,1,0:T(1,128)} %refs_2_.6, bf16[384,512]{1,0:T(8,128)(2,1)} %get-tuple-element.24.refs_3_, bf16[64,512]{1,0:T(8,128)(2,1)} %get-tuple-element.25.refs_4_, ...), custom_call_target="tpu_custom_call" | custom-call | flops 301989888 | bytes 3935236 | tf_op jit(solution)/shard_map/behind/pallas_call | solution.py:328
  47.2 0.0 collective-permute-done.5.refs_5_
  47.3 0.0 all-to-all-done.1.refs_4_
  47.3 0.0 copy-done.4
  47.3 0.0 copy-start.2
  47.3 0.9 %copy-done.2 = f32[64,512]{1,0:T(8,128)S(1)} copy-done((f32[64,512]{1,0:T(8,128)S(1)}, f32[64,512]{1,0:T(8,128)}, u32[]{:S(2)}) %copy-start.2) | copy-done | bytes 131096
  48.2 0.8 %last.1 = bf16[1,1,64,512]{3,2,1,0:T(8,128)(2,1)} custom-call(f32[64,512]{1,0:T(8,128)S(1)} %copy-done.2, f32[32,512]{1,0:T(8,128)S(1)} %get-tuple-element.31.refs_1_, s32[1,1,32]{2,1,0:T(1,128)S(1)} %copy-done.4, s32[1,1,1]{2,1,0:T(1,128)S(6)} %copy.23.coarse_list.refs_3_, f32[32,4,128]{2,1,0:T(4,128)S(1)} %all-to-all-done.1.refs_4_, ...), custom_call_target="tpu_custom_call" | custom-call | bytes 295044 | tf_op jit(solution)/shard_map/last/pallas_call | solution.py:328
  (7 shorter events, 0.0 us)
Async XLA Ops:
  3.2 20.2 %all-to-all-start = ((f32[32,4,128]{2,1,0:T(4,128)}), f32[32,4,128]{2,1,0:T(4,128)S(1)}, u32[]{:S(2)}, u32[]{:S(2)}) async-start(f32[32,4,128]{2,1,0:T(4,128)} %get-tuple-element.20), calls=%async_computation | async-start | bytes 131072 | tf_op jit(solution)/shard_map/all_to_all | solution.py:388
  10.5 4.2 %collective-permute-start = (bf16[32,512]{1,0:T(8,128)(2,1)}, bf16[32,512]{1,0:T(8,128)(2,1)S(1)}, u32[]{:S(2)}, u32[]{:S(2)}) collective-permute-start(bf16[32,512]{1,0:T(8,128)(2,1)} %get-tuple-element.19.refs_0_), channel_id=1, source_target_pairs={{0,1},{1,0},{2,3},{3,2},{4,5},{5,4},{6,7},{7,6},{8,9},{9,8},{10,11... | collective-permute-start | bytes 98312 | tf_op jit(solution)/shard_map/ppermute | solution.py:389
  14.7 0.8 %copy-start.3 = (bf16[32,512]{1,0:T(8,128)(2,1)S(1)}, bf16[32,512]{1,0:T(8,128)(2,1)}, u32[]{:S(2)}) copy-start(bf16[32,512]{1,0:T(8,128)(2,1)} %get-tuple-element.19.refs_0_) | copy-start | bytes 98308
  15.5 7.9 %copy-start = (bf16[64,512]{1,0:T(8,128)(2,1)}, bf16[64,512]{1,0:T(8,128)(2,1)S(1)}, u32[]{:S(2)}) copy-start(bf16[64,512]{1,0:T(8,128)(2,1)S(1)} %join.1.refs_4_) | copy-start | bytes 196612
  15.5 7.8 %collective-permute-start.2 = (bf16[64,512]{1,0:T(8,128)(2,1)S(1)}, bf16[64,512]{1,0:T(8,128)(2,1)S(1)}, u32[]{:S(2)}, u32[]{:S(2)}) collective-permute-start(bf16[64,512]{1,0:T(8,128)(2,1)S(1)} %join.1.refs_4_), channel_id=1, source_target_pairs={{2,4},{4,2},{3,5},{5,3},{6,8},{8,6},{7,9},{9,7},{10,12},{12,10},{1... | collective-permute-start | bytes 196616 | tf_op jit(solution)/shard_map/ppermute | solution.py:393
  19.3 4.1 %collective-permute-start.1 = (bf16[64,512]{1,0:T(8,128)(2,1)S(1)}, bf16[64,512]{1,0:T(8,128)(2,1)S(1)}, u32[]{:S(2)}, u32[]{:S(2)}) collective-permute-start(bf16[64,512]{1,0:T(8,128)(2,1)S(1)} %join.1.refs_4_), channel_id=1, source_target_pairs={{0,2},{2,0},{1,3},{3,1},{4,6},{6,4},{5,7},{7,5},{8,10},{10,8},{9,1... | collective-permute-start | bytes 196616 | tf_op jit(solution)/shard_map/ppermute | solution.py:393
  23.3 0.6 %copy-start.6 = (bf16[64,512]{1,0:T(8,128)(2,1)}, bf16[64,512]{1,0:T(8,128)(2,1)S(1)}, u32[]{:S(2)}) copy-start(bf16[64,512]{1,0:T(8,128)(2,1)S(1)} %collective-permute-done.2.refs_6_) | copy-start | bytes 196612
  23.4 0.6 %copy-start.7 = (bf16[64,512]{1,0:T(8,128)(2,1)}, bf16[64,512]{1,0:T(8,128)(2,1)S(1)}, u32[]{:S(2)}) copy-start(bf16[64,512]{1,0:T(8,128)(2,1)S(1)} %collective-permute-done.1.refs_5_) | copy-start | bytes 196612
  23.4 0.6 %copy-start.5 = (f32[32,4,128]{2,1,0:T(4,128)}, f32[32,4,128]{2,1,0:T(4,128)S(1)}, u32[]{:S(2)}) copy-start(f32[32,4,128]{2,1,0:T(4,128)S(1)} %all-to-all-done.refs_7_) | copy-start | bytes 196612
  30.7 16.6 %all-to-all-start.1 = ((f32[32,4,128]{2,1,0:T(4,128)}), f32[32,4,128]{2,1,0:T(4,128)S(1)}, u32[]{:S(2)}, u32[]{:S(2)}) async-start(f32[32,4,128]{2,1,0:T(4,128)} %get-tuple-element.32), calls=%async_computation.1 | async-start | bytes 131072 | tf_op jit(solution)/shard_map/all_to_all | solution.py:470
  33.6 4.7 %collective-permute-start.3 = (bf16[64,512]{1,0:T(8,128)(2,1)}, bf16[64,512]{1,0:T(8,128)(2,1)S(1)}, u32[]{:S(2)}, u32[]{:S(2)}) collective-permute-start(bf16[64,512]{1,0:T(8,128)(2,1)} %get-tuple-element.29), channel_id=1, source_target_pairs={{0,2},{2,0},{1,3},{3,1},{4,6},{6,4},{5,7},{7,5},{8,10},{10,8},{9,1... | collective-permute-start | bytes 196616 | tf_op jit(solution)/shard_map/ppermute | solution.py:472
  34.0 7.1 %collective-permute-start.4 = (bf16[64,512]{1,0:T(8,128)(2,1)}, bf16[64,512]{1,0:T(8,128)(2,1)S(1)}, u32[]{:S(2)}, u32[]{:S(2)}) collective-permute-start(bf16[64,512]{1,0:T(8,128)(2,1)} %get-tuple-element.30), channel_id=1, source_target_pairs={{2,4},{4,2},{3,5},{5,3},{6,8},{8,6},{7,9},{9,7},{10,12},{12,10},{1... | collective-permute-start | bytes 196616 | tf_op jit(solution)/shard_map/ppermute | solution.py:472
  41.1 0.9 %copy-start.1 = (f32[64,512]{1,0:T(8,128)S(1)}, f32[64,512]{1,0:T(8,128)}, u32[]{:S(2)}) copy-start(f32[64,512]{1,0:T(8,128)} %get-tuple-element.28.kept) | copy-start | bytes 393220
  42.0 5.3 %collective-permute-start.5 = (bf16[32,512]{1,0:T(8,128)(2,1)S(1)}, bf16[32,512]{1,0:T(8,128)(2,1)S(1)}, u32[]{:S(2)}, u32[]{:S(2)}) collective-permute-start(bf16[32,512]{1,0:T(8,128)(2,1)S(1)} %get-tuple-element.33), channel_id=1, source_target_pairs={{0,1},{1,0},{2,3},{3,2},{4,5},{5,4},{6,7},{7,6},{8,9},{9,8},{10,11... | collective-permute-start | bytes 98312 | tf_op jit(solution)/shard_map/ppermute | solution.py:502
  43.5 3.7 %copy-start.4 = (s32[1,1,32]{2,1,0:T(1,128)S(1)}, s32[1,1,32]{2,1,0:T(1,128)}, u32[]{:S(2)}) copy-start(s32[1,1,32]{2,1,0:T(1,128)} %refs_2_.7) | copy-start | bytes 388
  47.3 0.9 %copy-start.2 = (f32[64,512]{1,0:T(8,128)S(1)}, f32[64,512]{1,0:T(8,128)}, u32[]{:S(2)}) copy-start(f32[64,512]{1,0:T(8,128)} %get-tuple-element.27.refs_0_) | copy-start | bytes 393220

commit v3 on v2

v3 whole, which is shorter than its diff:
```python
import functools

import jax
import jax.numpy as jnp
from jax import lax
from jax.experimental import pallas as pl
from jax.experimental.pallas import tpu as pltpu
from jax.sharding import PartitionSpec as P

F32 = jnp.float32
BF16 = jnp.bfloat16
VMEM = pltpu.VMEM
SENT_ROWS = 128


def dot_nn(a, b):
    return jnp.dot(a, b, preferred_element_type=F32)


def dot_tn(a, b):
    return lax.dot_general(a, b, (((0,), (0,)), ((), ())), preferred_element_type=F32)


def dot_nt(a, b):
    return lax.dot_general(a, b, (((1,), (1,)), ((), ())), preferred_element_type=F32)


def as_one_hot(mask):
    return jnp.where(mask, 1.0, 0.0).astype(BF16)


def one_hot_rows(index_row, rows):
    return lax.broadcasted_iota(jnp.int32, (rows, index_row.shape[1]), 0) == index_row


def live_one_hot(index_row, rows, count):
    lanes = lax.broadcasted_iota(jnp.int32, (rows, index_row.shape[1]), 1)
    return as_one_hot(one_hot_rows(index_row, rows) & (lanes < count))


def in_two(values):
    head = values.astype(BF16)
    tail = (values - head.astype(F32)).astype(BF16)
    return jnp.concatenate([head, tail], axis=0)


def normed_rows(out_rows):
    centre = out_rows - jnp.mean(out_rows, axis=1, keepdims=True)
    inv_std = lax.rsqrt(jnp.mean(centre * centre, axis=1, keepdims=True) + 1e-05)
    return centre * inv_std, inv_std


def norm_backward(grad_norm, normed, inv_std):
    return inv_std * (
        grad_norm
        - jnp.mean(grad_norm, axis=1, keepdims=True)
        - normed * jnp.mean(grad_norm * normed, axis=1, keepdims=True)
    )


def silu_slope(pre, sig):
    return sig * (1.0 + pre * (1.0 - sig))


class Moves:
    def __init__(self, sems):
        self.sems, self.used = sems, 0

    def start(self, source, target):
        copy = pltpu.make_async_copy(source, target, self.sems.at[self.used])
        self.used += 1
        copy.start()
        return copy


class Plan:
    def __init__(self, lon, lat, nodes, edges, halo, owned, width):
        self.lon, self.lat = lon, lat
        self.nodes, self.edges, self.halo, self.owned, self.width = nodes, edges, halo, owned, width
        self.devices = lon * lat
        self.coarse = self.devices * owned
        flat = lambda i, j: (i % lon) * lat + j
        swap = lambda pairs: [p for a, b in pairs for p in ((a, b), (b, a))]
        lat_sets = [
            [(k, k + 1) for k in range(0, lat - 1, 2)],
            [(k, k + 1) for k in range(1, lat - 1, 2)],
        ]
        self.lat_pairs = [
            swap([(flat(i, a), flat(i, b)) for i in range(lon) for a, b in pairs])
            for pairs in lat_sets
            if pairs
        ]
        self.lon_pairs = [
            swap([(flat(i, j), flat(i + 1, j)) for i in range(first, lon, 2) for j in range(lat)])
            for first in (0, 1)
        ]
        self.per_lon = 1 + len(self.lat_pairs)
        self.blocks = 3 * self.per_lon
        self.table = nodes + self.blocks * halo + self.coarse

    def positions(self, sender):
        nodes, halo = self.nodes, self.halo
        lon_odd = lax.rem(lax.axis_index("lon"), 2)
        lat_odd = lax.rem(lax.axis_index("lat"), 2)
        lon_step = [1, 2 - 2 * lon_odd, 2 * lon_odd]
        lat_step = [1, 2 - 2 * lat_odd, 2 * lat_odd][: self.per_lon]
        past = sender - (nodes + 9 * halo)
        if self.owned > 1:
            past = jnp.where(
                past >= 0, lax.rem(past, self.owned) * self.devices + past // self.owned, past
            )
        found = jnp.where(past >= 0, past + (nodes + self.blocks * halo), sender)
        place = 0
        for a in lon_step:
            for b in lat_step:
                row = sender - (nodes + (3 * a + b) * halo)
                inside = (row >= 0) & (row < halo) & (sender >= nodes)
                found = jnp.where(inside, row + (nodes + place * halo), found)
                place += 1
        return found


def pack_kernel(plan, node, halo_list, coarse_list, border, coarse, node_s, halo_s, list_s, sems):
    moves = Moves(sems)
    pairs = ((coarse_list, list_s), (halo_list, halo_s), (node, node_s))
    for copy in [moves.start(*pair) for pair in pairs]:
        copy.wait()
    rows = node_s[0, 0]
    pick = as_one_hot(one_hot_rows(halo_s[0], plan.nodes))
    border[: plan.halo] = dot_tn(pick, rows).astype(BF16)
    own = dot_tn(as_one_hot(one_hot_rows(list_s[0], plan.nodes)), rows)
    parts = plan.width // 128
    for k in range(plan.owned):
        for q in range(parts):
            piece = own[k : k + 1, q * 128 : (q + 1) * 128]
            coarse[:, k * parts + q, :] = jnp.broadcast_to(piece, (plan.devices, 128))


def block_of(ref, part, width):
    return ref if part is None else ref.at[pl.ds(part * width, width)]


def ahead_kernel(plan, *refs):
    operands = dict(zip(plan.ahead_in, refs))
    refs = refs[len(plan.ahead_in) :]
    held = dict(zip(plan.ahead_out, refs))
    sems = refs[-1]
    held.update(zip(plan.ahead_held, refs[len(plan.ahead_out) : -1]))
    moves = Moves(sems)
    width, nodes = plan.width, plan.nodes
    copies = {
        name: moves.start(block_of(operands[source], part, width), held[name])
        for name, (source, part) in plan.ahead_copies.items()
    }

    def got(name):
        if name in copies:
            copies.pop(name).wait()
        return held[name]

    count = got("count")[...]
    received = live_one_hot(got("receivers")[0], nodes, count)
    held["received"][...] = received
    held["sent"][...] = as_one_hot(
        one_hot_rows(plan.positions(got("senders")[0]), plan.table)
    )
    place = as_one_hot(one_hot_rows(got("halo_list")[0], nodes))
    held["place"][...] = jnp.concatenate([place, place], axis=1)
    at_coarse = one_hot_rows(got("coarse_list")[0], nodes)
    held["at_coarse"][...] = jnp.where(at_coarse, 1.0, 0.0).astype(F32)
    rows = got("node")[0, 0]
    at_receiver = dot_tn(received, rows).astype(BF16)
    held["edge_part"][...] = (
        dot_nn(got("edge")[0, 0], got("w_edge_top")[...])
        + dot_nn(at_receiver, got("w_edge_low")[...])
        + got("b_edge_in")[...]
    )
    held["node_part"][...] = dot_nn(rows, got("w_node_top")[...]) + got("b_node_in")[...]
    for copy in copies.values():
        copy.wait()


def join_kernel(plan, *refs):
    for k, part in enumerate(refs[:-1]):
        refs[-1][k * plan.halo : (k + 1) * plan.halo] = part[: plan.halo]


def gather_kernel(plan, rows, _, coarse):
    parts = plan.width // 128
    for k in range(plan.owned):
        for q in range(parts):
            coarse[:, k * parts + q, :] = rows[
                k * plan.devices : (k + 1) * plan.devices, q * 128 : (q + 1) * 128
            ]


def edge_cotangent(cot_edge, received, agg_grad):
    twice = jnp.concatenate([received, received], axis=0)
    return cot_edge[0, 0].astype(F32) + dot_tn(twice, agg_grad)


def main_kernel(plan, *refs):
    here = dict(zip(plan.main_names, refs))
    refs = refs[len(plan.main_names) :]
    even_grad, odd_grad, coarse_grad, kept_grad, agg_out, edge_dpre_out, local = refs[:7]
    new_nodes, table, new_s = refs[7:10]
    sems, held = refs[-1], dict(zip(plan.main_held, refs[10:-1]))
    nodes, halo, width = plan.nodes, plan.halo, plan.width
    sent, received = here["sent"], here["received"][...]
    live = jnp.where(
        lax.broadcasted_iota(jnp.int32, (plan.edges, 1), 0) < here["count"][0, 0], 1.0, 0.0
    ).astype(F32)
    moves = Moves(sems)
    copies = {
        name: moves.start(block_of(here[source], part, width), held[name])
        for name, (source, part) in plan.main_copies.items()
    }

    def got(name):
        if name in copies:
            copies.pop(name).wait()
        return held[name] if name in held else here[name]

    start = nodes
    table[:nodes] = got("node")[0, 0]
    for name in ("wide", "even_rows", "odd_rows"):
        rim = plan.per_lon * halo
        table[start : start + rim] = got(name)[:rim]
        start += rim
    parts = width // 128
    for k in range(plan.owned):
        for q in range(parts):
            table[start : start + plan.devices, q * 128 : (q + 1) * 128] = got("coarse_rows")[
                :, k * parts + q, :
            ].astype(BF16)
        start += plan.devices

    w_edge_mid = got("w_edge_mid")[...]
    at_sender = dot_tn(sent[...], table[...]).astype(BF16)
    edge_pre = got("edge_part")[...] + dot_nn(at_sender, w_edge_mid)
    edge_sig = jax.nn.sigmoid(edge_pre)
    edge_out = dot_nn((edge_pre * edge_sig).astype(BF16), got("w_edge_out")[...])
    edge_normed, edge_rstd = normed_rows(edge_out)
    edge_upd = edge_normed * got("gain_edge")[...] + got("shift_edge")[...]
    new_edge = (got("edge")[0, 0].astype(F32) + live * edge_upd).astype(BF16)
    aggregated = dot_nn(received, new_edge).astype(BF16)

    node_pre = got("node_part")[...] + dot_nn(aggregated, got("w_node_low")[...])
    node_sig = jax.nn.sigmoid(node_pre)
    node_out = dot_nn((node_pre * node_sig).astype(BF16), got("w_node_out")[...])
    node_normed, node_rstd = normed_rows(node_out)
    node_upd = node_normed * got("gain_node")[...] + got("shift_node")[...]
    new_s[0, 0] = (got("node")[0, 0].astype(F32) + node_upd).astype(BF16)
    leaving = moves.start(new_s, new_nodes)

    node_dout = norm_backward(
        got("cot_node")[0, 0].astype(F32) * got("gain_node")[...], node_normed, node_rstd
    ).astype(BF16)
    node_dpre = (
        dot_nt(node_dout, got("w_node_out")[...]) * silu_slope(node_pre, node_sig)
    ).astype(BF16)
    agg_grad = in_two(dot_nt(node_dpre, got("w_node_low")[...]))
    agg_out[...] = agg_grad
    edge_cot = edge_cotangent(got("cot_edge"), received, agg_grad)

    edge_dout = norm_backward(
        live * edge_cot * got("gain_edge")[...], edge_normed, edge_rstd
    ).astype(BF16)
    edge_dpre = (
        dot_nt(edge_dout, got("w_edge_out")[...]) * silu_slope(edge_pre, edge_sig)
    ).astype(BF16)
    edge_dpre_out[...] = edge_dpre
    away_grad = dot_nt(dot_nn(sent[...], edge_dpre).astype(BF16), w_edge_mid)
    own_grad, away_grad = away_grad[:nodes], away_grad[nodes:]
    kept = plan.per_lon * halo
    kept_grad[...] = away_grad[:kept]
    even_grad[:kept] = away_grad[kept : 2 * kept].astype(BF16)
    odd_grad[:kept] = away_grad[2 * kept : 3 * kept].astype(BF16)
    coarse_grad[...] = away_grad[3 * kept :]
    local[...] = (
        got("cot_node")[0, 0].astype(F32) + dot_nt(node_dpre, got("w_node_top")[...]) + own_grad
    )
    leaving.wait()


def behind_kernel(plan, *refs):
    received, edge_dpre, agg_grad, local, _, w_edge_in, cot_edge, grad_local, grad_edges = refs[:9]
    w_top_s, w_low_s, cot_s, grad_s, sems = refs[9:]
    moves, width = Moves(sems), plan.width
    top = moves.start(block_of(w_edge_in, 0, width), w_top_s)
    cot = moves.start(cot_edge, cot_s)
    low = moves.start(block_of(w_edge_in, 2, width), w_low_s)
    dpre = edge_dpre[...]
    at_receiver = dot_nn(received[...], dpre).astype(BF16)
    cot.wait()
    edge_cot = edge_cotangent(cot_s, received[...], agg_grad[...])
    top.wait()
    grad_s[0, 0] = (edge_cot + dot_nt(dpre, w_top_s[...])).astype(BF16)
    leaving = moves.start(grad_s, grad_edges)
    low.wait()
    grad_local[...] = local[...] + dot_nt(at_receiver, w_low_s[...])
    leaving.wait()


def middle_kernel(plan, kept, even, odd, mine, *lat_sends):
    rows = kept.shape[0]
    total = kept[...] + even[:rows].astype(F32) + odd[:rows].astype(F32)
    mine[...] = total[: plan.halo]
    for k, out in enumerate(lat_sends):
        out[...] = total[(k + 1) * plan.halo : (k + 2) * plan.halo].astype(BF16)


def last_kernel(plan, *refs):
    grad_local, mine, place, at_coarse, coarse = refs[:5]
    out = refs[-1]
    total = mine[...]
    for part in refs[5:-1]:
        total = total + part[...].astype(F32)
    result = grad_local[...] + dot_nn(place[...], in_two(total))
    share = jnp.sum(coarse[...], axis=0)
    parts = plan.width // 128
    for k in range(plan.owned):
        row = jnp.concatenate([share[k * parts + q : k * parts + q + 1] for q in range(parts)], axis=1)
        result = result + at_coarse[:, k : k + 1] * row
    out[0, 0] = result.astype(BF16)


def call(body, name, outs, operands, far=(), scratch=(), flops=0, mib=4, results=0):
    whole = pl.BlockSpec(memory_space=VMEM)
    scalars = pl.BlockSpec(memory_space=pltpu.SMEM)
    anywhere = pl.BlockSpec(memory_space=pl.ANY)
    far = [pltpu.with_memory_space_constraint(a, pltpu.HBM) if a.size > 1 else a for a in far]
    moved = sum(a.size * a.dtype.itemsize for a in (*operands, *far))
    near = len(outs) - results
    return pl.pallas_call(
        body,
        name=name,
        out_shape=[VMEM(shape, dtype) for shape, dtype in outs[:near]]
        + [jax.ShapeDtypeStruct(shape, dtype) for shape, dtype in outs[near:]],
        in_specs=[scalars if a.size == 1 else whole for a in operands] + [anywhere] * len(far),
        out_specs=[whole] * near + [anywhere if scratch else whole] * results,
        scratch_shapes=list(scratch),
        compiler_params=pltpu.CompilerParams(vmem_limit_bytes=mib * 1024 * 1024),
        cost_estimate=pl.CostEstimate(flops=flops, bytes_accessed=moved, transcendentals=0),
    )(*operands, *far)


def like(arrays):
    return [VMEM(a.shape, a.dtype) for a in arrays]


def sems(count):
    return pltpu.SemaphoreType.DMA((count,))


def body(
    plan,
    node_feat,
    edge_feat,
    senders,
    receivers,
    edge_count,
    halo_list,
    coarse_list,
    w_edge_in,
    b_edge_in,
    w_edge_out,
    gain_edge,
    shift_edge,
    w_node_in,
    b_node_in,
    w_node_out,
    gain_node,
    shift_node,
    cot_node,
    cot_edge,
):
    axes = ("lon", "lat")
    halo, width, nodes, edges = plan.halo, plan.width, plan.nodes, plan.edges
    row = lambda vec: vec.reshape(1, width)
    with_plan = lambda kernel: functools.partial(kernel, plan)
    coarse_shape = (plan.devices, plan.owned * width // 128, 128)
    kept = plan.per_lon * halo

    operands = [node_feat, halo_list, coarse_list]
    border, coarse_out = call(
        with_plan(pack_kernel),
        "pack",
        [((max(halo, SENT_ROWS), width), BF16), (coarse_shape, F32)],
        [],
        far=operands,
        scratch=like(operands) + [sems(3)],
    )
    coarse_rows = lax.all_to_all(coarse_out, axes, 0, 0, tiled=True)
    lat_rows = [lax.ppermute(border, axes, pairs) for pairs in plan.lat_pairs]

    far = {
        "count": edge_count,
        "receivers": receivers,
        "node": node_feat,
        "edge": edge_feat,
        "w_edge_in": w_edge_in,
        "b_edge_in": row(b_edge_in),
        "senders": senders,
        "halo_list": halo_list,
        "coarse_list": coarse_list,
        "w_node_in": w_node_in,
        "b_node_in": row(b_node_in),
    }
    square = ((width, width), BF16)
    copies = {name: (name, None) for name in far if name not in ("w_edge_in", "w_node_in")}
    copies["w_edge_top"] = ("w_edge_in", 0)
    copies["w_edge_low"] = ("w_edge_in", 2)
    copies["w_node_top"] = ("w_node_in", 0)
    copies["w_edge_mid"] = ("w_edge_in", 1)
    outs = {
        "w_edge_mid": square,
        "edge_part": ((edges, width), F32),
        "node_part": ((nodes, width), F32),
        "sent": ((plan.table, edges), BF16),
        "received": ((nodes, edges), BF16),
        "place": ((nodes, 2 * halo), BF16),
        "at_coarse": ((nodes, plan.owned), F32),
    }
    held = {
        name: square if part is not None else (far[source].shape, far[source].dtype)
        for name, (source, part) in copies.items()
        if name not in outs
    }
    plan.ahead_in, plan.ahead_out, plan.ahead_held = list(far), list(outs), list(held)
    plan.ahead_copies = copies
    at = dict(
        zip(
            outs,
            call(
                with_plan(ahead_kernel),
                "ahead",
                list(outs.values()),
                [],
                far=list(far.values()),
                scratch=[VMEM(*kind) for kind in held.values()] + [sems(len(copies))],
                flops=2 * (2 * edges + nodes) * width * width,
                mib=12,
            ),
        )
    )

    (wide,) = call(with_plan(join_kernel), "join", [((kept, width), BF16)], [border, *lat_rows])
    even_rows, odd_rows = [lax.ppermute(wide, axes, pairs) for pairs in plan.lon_pairs]

    near = {
        "count": edge_count,
        "wide": wide,
        "even_rows": even_rows,
        "odd_rows": odd_rows,
        "coarse_rows": coarse_rows,
        **{
            name: at[name]
            for name in (
                "w_edge_mid",
                "edge_part",
                "node_part",
                "sent",
                "received",
            )
        },
    }
    far = {
        "w_edge_out": w_edge_out,
        "node": node_feat,
        "gain_edge": row(gain_edge),
        "shift_edge": row(shift_edge),
        "edge": edge_feat,
        "w_node_in": w_node_in,
        "w_node_out": w_node_out,
        "gain_node": row(gain_node),
        "shift_node": row(shift_node),
        "cot_node": cot_node,
        "cot_edge": cot_edge,
    }
    copies = {name: (name, None) for name in far if name not in ("w_edge_in", "w_node_in")}
    copies["w_node_low"] = ("w_node_in", 1)
    copies["w_node_top"] = ("w_node_in", 0)
    plan.main_names, plan.main_copies, plan.main_held = [*near, *far], copies, list(copies)
    outs = [
        ((max(kept, SENT_ROWS), width), BF16),
        ((max(kept, SENT_ROWS), width), BF16),
        ((plan.coarse, width), F32),
        ((kept, width), F32),
        ((2 * nodes, width), BF16),
        ((edges, width), BF16),
        ((nodes, width), F32),
        (node_feat.shape, BF16),
    ]
    (
        even_grad,
        odd_grad,
        coarse_grad,
        kept_grad,
        agg_grad,
        edge_dpre,
        local,
        new_nodes,
    ) = call(
        with_plan(main_kernel),
        "main",
        outs,
        list(near.values()),
        far=list(far.values()),
        scratch=[VMEM((plan.table, width), BF16), VMEM(node_feat.shape, BF16)]
        + [
            VMEM(*(square if part is not None else (far[source].shape, far[source].dtype)))
            for source, part in copies.values()
        ]
        + [sems(len(copies) + 1)],
        flops=2 * 5 * edges * width * width,
        mib=20,
        results=1,
    )

    even_back, odd_back = [
        lax.ppermute(grad, axes, pairs)
        for grad, pairs in zip((even_grad, odd_grad), plan.lon_pairs)
    ]
    (coarse_send,) = call(
        with_plan(gather_kernel), "gather", [(coarse_shape, F32)], [coarse_grad, coarse_grad]
    )
    coarse_back = lax.all_to_all(coarse_send, axes, 0, 0, tiled=True)
    mine, *lat_sends = call(
        with_plan(middle_kernel),
        "middle",
        [((halo, width), F32)] + [((halo, width), BF16)] * len(plan.lat_pairs),
        [kept_grad, even_back, odd_back],
    )
    lat_back = [
        lax.ppermute(grad, axes, pairs) for grad, pairs in zip(lat_sends, plan.lat_pairs)
    ]
    grad_local, grad_edges = call(
        with_plan(behind_kernel),
        "behind",
        [((nodes, width), F32), (edge_feat.shape, BF16)],
        [at["received"], edge_dpre, agg_grad, local, mine],
        far=[w_edge_in, cot_edge],
        scratch=[VMEM(*square), VMEM(*square), *like([cot_edge, edge_feat]), sems(4)],
        flops=2 * (edges + nodes) * width * width,
        mib=8,
        results=1,
    )
    (grad_nodes,) = call(
        with_plan(last_kernel),
        "last",
        [(node_feat.shape, BF16)],
        [grad_local, mine, at["place"], at["at_coarse"], coarse_back, *lat_back],
        results=1,
    )
    return new_nodes, grad_nodes, grad_edges


def solution(mesh):
    lon, lat = mesh.shape["lon"], mesh.shape["lat"]
    cells = lambda rank: P("lon", "lat", *([None] * (rank - 2)))

    def sharded(*args):
        node_feat, edge_feat, halo_list, coarse_list = args[0], args[1], args[5], args[6]
        plan = Plan(
            lon,
            lat,
            node_feat.shape[2],
            edge_feat.shape[2],
            halo_list.shape[2],
            coarse_list.shape[2],
            node_feat.shape[3],
        )
        return body(plan, *args)

    ranks = (4, 4, 3, 3, 2, 3, 3)
    return jax.shard_map(
        sharded,
        mesh=mesh,
        in_specs=tuple(cells(r) for r in ranks) + (P(),) * 10 + (cells(4), cells(4)),
        out_specs=(cells(4), cells(4), cells(4)),
        check_vma=False,
    )
```

time: 49.5 us -> 39.6 us (0.80)
  local copies, waits for them, and re-layouts: 3.18 us -> 0 us
  Pallas kernels: 16.5 us -> 13.6 us
  starting transfers between devices: 22.2 us -> 19.5 us
  waiting for transfers between devices: 5.11 us -> 4.1 us
    unnamed x16 -> x0, local copies, waits for them, and re-layouts: 3.18 us -> none
    pallas_call x7 -> x8, Pallas kernels: 16.5 us -> 13.6 us  [call(): pl.pallas_call(body, name=name, out_shape=[VMEM(shape, dtype) for shape,...]
    all_to_all x1, waiting for transfers between devices: 0.01 us -> 2.78 us  [body(): coarse_back = lax.all_to_all(coarse_send, axes, 0, 0, tiled=True)]
    ppermute x1, waiting for transfers between devices: 2.41 us -> 0.01 us  [body(): lat_rows = [lax.ppermute(border, axes, pairs) for pairs in plan.lat_pairs]]
    all_to_all x1, starting transfers between devices: 7.3 us -> 4.92 us  [body(): coarse_rows = lax.all_to_all(coarse_out, axes, 0, 0, tiled=True)]
    ppermute x3, starting transfers between devices: 6.28 us -> 4.34 us  [body(): lax.ppermute(grad, axes, pairs)]
    ppermute x3, waiting for transfers between devices: 2.68 us -> 0.76 us  [body(): lax.ppermute(grad, axes, pairs)]
    ppermute x1, starting transfers between devices: 1.83 us -> 3 us  [body(): lat_rows = [lax.ppermute(border, axes, pairs) for pairs in plan.lat_pairs]]
  transfers between devices with their start and end apart: 8 -> 8, of which waited for: 2 -> 3; matrix products, arithmetic and copies ran while one was open for 0% -> 0% of each run, Pallas kernels for 14% -> 14%
where the time goes in v3:
time: 39.6 us; the launch traced here: 39.3 us
  starting transfers between devices  19.5 us (49%)
  Pallas kernels  13.6 us (34%)
  waiting for transfers between devices  4.1 us (10%)
  between operations  2.02 us (5%)
    pallas_call x8, Pallas kernels, call(): pl.pallas_call(body, name=name, out_shape=[VMEM(shape, dtype) for shape,...  13.6 us
    all_to_all x1, starting transfers between devices, body(): coarse_rows = lax.all_to_all(coarse_out, axes, 0, 0, tiled=True)  4.92 us
    ppermute x2, starting transfers between devices, body(): lax.ppermute(wide, axes, pairs)  4.37 us
    ppermute x3, starting transfers between devices, body(): lax.ppermute(grad, axes, pairs)  4.34 us
    ppermute x1, starting transfers between devices, body(): lat_rows = [lax.ppermute(border, axes, pairs) for pairs in plan.lat_pairs]  3 us
    all_to_all x1, starting transfers between devices, body(): coarse_back = lax.all_to_all(coarse_send, axes, 0, 0, tiled=True)  2.9 us
    all_to_all x1, waiting for transfers between devices, body(): coarse_back = lax.all_to_all(coarse_send, axes, 0, 0, tiled=True)  2.78 us
  transfers between devices with their start and end apart: 8, of which 3 were waited for; matrix products, arithmetic and copies ran while one was open for 0% of the time, Pallas kernels for 14%

profile of v3, /device:TPU:0, one launch (start us, length us, event | category | flops | bytes accessed | tf_op | source)
XLA Modules:
  0.0 39.3 jit_solution(8091658819366104206)
XLA Ops:
  1.3 1.7 %pack.1 = (bf16[128,512]{1,0:T(8,128)(2,1)S(1)}, f32[32,4,128]{2,1,0:T(4,128)}) custom-call(bf16[1,1,64,512]{3,2,1,0:T(8,128)(2,1)} %refs_11_.1, s32[1,1,32]{2,1,0:T(1,128)} %refs_7_.1, s32[1,1,1]{2,1,0:T(1,128)S(6)} %copy.23.coarse_list.refs_8_), custom_call_target="tpu_custom_call" | custom-call | bytes 65668 | tf_op jit(solution)/shard_map/pack/pallas_call | solution.py:335
  3.0 3.0 %collective-permute-start = (bf16[128,512]{1,0:T(8,128)(2,1)S(1)}, bf16[128,512]{1,0:T(8,128)(2,1)S(1)}, u32[]{:S(2)}, u32[]{:S(2)}) collective-permute-start(bf16[128,512]{1,0:T(8,128)(2,1)S(1)} %get-tuple-element.24.refs_0_), channel_id=1, source_target_pairs={{0,1},{1,0},{2,3},{3,2},{4,5},{5,4},{6,7},{7,6},{8,9},{9,8},{10,11... | collective-permute-start | bytes 393224 | tf_op jit(solution)/shard_map/ppermute | solution.py:395
  6.0 4.9 %all-to-all-start = ((f32[32,4,128]{2,1,0:T(4,128)}), f32[32,4,128]{2,1,0:T(4,128)S(1)}, u32[]{:S(2)}, u32[]{:S(2)}) async-start(f32[32,4,128]{2,1,0:T(4,128)} %get-tuple-element.25), calls=%async_computation | async-start | bytes 131072 | tf_op jit(solution)/shard_map/all_to_all | solution.py:394
  11.0 0.0 collective-permute-done.refs_1_
  11.0 4.4 %collective-permute-start.2 = (bf16[64,512]{1,0:T(8,128)(2,1)S(1)}, bf16[64,512]{1,0:T(8,128)(2,1)S(1)}, u32[]{:S(2)}, u32[]{:S(2)}) collective-permute-start(bf16[64,512]{1,0:T(8,128)(2,1)S(1)} %join.1.refs_1_), channel_id=1, source_target_pairs={{2,4},{4,2},{3,5},{5,3},{6,8},{8,6},{7,9},{9,7},{10,12},{12,10},{1... | collective-permute-start | bytes 196616 | tf_op jit(solution)/shard_map/ppermute | solution.py:449
  15.3 0.0 collective-permute-start.1
  16.0 2.4 %ahead.1 = (bf16[512,512]{1,0:T(8,128)(2,1)S(1)}, f32[384,512]{1,0:T(8,128)S(1)}, f32[64,512]{1,0:T(8,128)S(1)}, bf16[288,384]{1,0:T(8,128)(2,1)S(1)}, bf16[64,3...) custom-call(s32[1,1]{1,0:T(1,128)S(6)} %copy.22.refs_0_, s32[1,1,384]{2,1,0:T(1,128)} %refs_1_.1, ...), custom_call_target="tpu_custom_call" | custom-call | flops 436207616 | bytes 3087496 | tf_op jit(solution)/shard_map/ahead/pallas_call | solution.py:335
  18.4 0.5 %all-to-all-done.refs_4_ = f32[32,4,128]{2,1,0:T(4,128)S(1)} async-done(((f32[32,4,128]{2,1,0:T(4,128)}), f32[32,4,128]{2,1,0:T(4,128)S(1)}, u32[]{:S(2)}, u32[]{:S(2)}) %all-to-all-start) | async-done | bytes 65568 | tf_op jit(solution)/shard_map/all_to_all | solution.py:394
  19.0 0.0 collective-permute-done.2.refs_3_
  19.0 0.0 collective-permute-done.1.refs_2_
  19.0 5.4 %main.1 = (bf16[128,512]{1,0:T(8,128)(2,1)S(1)}, bf16[128,512]{1,0:T(8,128)(2,1)S(1)}, f32[32,512]{1,0:T(8,128)S(1)}, f32[64,512]{1,0:T(8,128)S(1)}, bf16[128,51...) custom-call(s32[1,1]{1,0:T(1,128)S(6)} %copy.22.refs_0_, ...), custom_call_target="tpu_custom_call" | custom-call | flops 1006632960 | bytes 4997124 | tf_op jit(solution)/shard_map/main/pallas_call | solution.py:335
  24.4 0.1 collective-permute-start.3
  24.5 2.8 %collective-permute-start.4 = (bf16[128,512]{1,0:T(8,128)(2,1)S(1)}, bf16[128,512]{1,0:T(8,128)(2,1)S(1)}, u32[]{:S(2)}, u32[]{:S(2)}) collective-permute-start(bf16[128,512]{1,0:T(8,128)(2,1)S(1)} %get-tuple-element.37), channel_id=1, source_target_pairs={{2,4},{4,2},{3,5},{5,3},{6,8},{8,6},{7,9},{9,7},{10,12},{12,10},{1... | collective-permute-start | bytes 393224 | tf_op jit(solution)/shard_map/ppermute | solution.py:522
  27.3 0.7 %gather.1 = f32[32,4,128]{2,1,0:T(4,128)} custom-call(f32[32,512]{1,0:T(8,128)S(1)} %get-tuple-element.42.rows._, f32[32,512]{1,0:T(8,128)S(1)} %get-tuple-element.42.rows._), custom_call_target="tpu_custom_call" | custom-call | bytes 131072 | tf_op jit(solution)/shard_map/gather/pallas_call | solution.py:335
  27.9 2.9 %all-to-all-start.1 = ((f32[32,4,128]{2,1,0:T(4,128)}), f32[32,4,128]{2,1,0:T(4,128)S(1)}, u32[]{:S(2)}, u32[]{:S(2)}) async-start(f32[32,4,128]{2,1,0:T(4,128)} %gather.1), calls=%async_computation.1 | async-start | bytes 131072 | tf_op jit(solution)/shard_map/all_to_all | solution.py:528
  30.9 0.0 collective-permute-done.3.even
  30.9 0.8 %collective-permute-done.4.odd = bf16[128,512]{1,0:T(8,128)(2,1)S(1)} collective-permute-done((bf16[128,512]{1,0:T(8,128)(2,1)S(1)}, bf16[128,512]{1,0:T(8,128)(2,1)S(1)}, u32[]{:S(2)}, u32[]{:S(2)}) %collective-permute-start.4) | collective-permute-done | bytes 131104 | tf_op jit(solution)/shard_map/ppermute | solution.py:522
  31.7 1.5 %collective-permute-start.5 = (bf16[32,512]{1,0:T(8,128)(2,1)S(1)}, bf16[32,512]{1,0:T(8,128)(2,1)S(1)}, u32[]{:S(2)}, u32[]{:S(2)}) collective-permute-start(bf16[32,512]{1,0:T(8,128)(2,1)S(1)} %get-tuple-element.43), channel_id=1, source_target_pairs={{0,1},{1,0},{2,3},{3,2},{4,5},{5,4},{6,7},{7,6},{8,9},{9,8},{10,11... | collective-permute-start | bytes 98312 | tf_op jit(solution)/shard_map/ppermute | solution.py:536
  33.1 2.6 %behind.1 = (f32[64,512]{1,0:T(8,128)S(1)}, bf16[1,1,384,512]{3,2,1,0:T(8,128)(2,1)}) custom-call(bf16[64,384]{1,0:T(8,128)(2,1)S(1)} %get-tuple-element.30.refs_9_.refs_0_, bf16[384,512]{1,0:T(8,128)(2,1)S(1)} %get-tuple-element.32.refs_1_, bf16[128,512]{1,0:T(8,128)(2,1)S(1)} %get-tuple-element.33.refs_2_, f32[64,512]{1,0:T(8,128)S(1)} %get-tuple-element.34.refs_3_, ...), custom_call_target="tpu_custom_call" | custom-call | flops 234881024 | bytes 2736128 | tf_op jit(solution)/shard_map/behind/pallas_call | solution.py:335
  35.7 2.8 %all-to-all-done.1.refs_4_ = f32[32,4,128]{2,1,0:T(4,128)S(1)} async-done(((f32[32,4,128]{2,1,0:T(4,128)}), f32[32,4,128]{2,1,0:T(4,128)S(1)}, u32[]{:S(2)}, u32[]{:S(2)}) %all-to-all-start.1) | async-done | bytes 65568 | tf_op jit(solution)/shard_map/all_to_all | solution.py:528
  38.5 0.0 collective-permute-done.5.refs_5_
  38.5 0.8 %last.1 = bf16[1,1,64,512]{3,2,1,0:T(8,128)(2,1)} custom-call(f32[64,512]{1,0:T(8,128)S(1)} %get-tuple-element.39.refs_0_, f32[32,512]{1,0:T(8,128)S(1)} %get-tuple-element.38.refs_4_.refs_1_, bf16[64,64]{1,0:T(8,128)(2,1)S(1)} %get-tuple-element.40.refs_2_, f32[64,1]{1,0:T(8,128)S(1)} %get-tuple-element.41.refs_3_, ...), custom_call_target="tpu_custom_call" | custom-call | bytes 303360 | tf_op jit(solution)/shard_map/last/pallas_call | solution.py:335
  (2 shorter events, 0.0 us)
Async XLA Ops:
  3.0 7.9 %collective-permute-start = (bf16[128,512]{1,0:T(8,128)(2,1)S(1)}, bf16[128,512]{1,0:T(8,128)(2,1)S(1)}, u32[]{:S(2)}, u32[]{:S(2)}) collective-permute-start(bf16[128,512]{1,0:T(8,128)(2,1)S(1)} %get-tuple-element.24.refs_0_), channel_id=1, source_target_pairs={{0,1},{1,0},{2,3},{3,2},{4,5},{5,4},{6,7},{7,6},{8,9},{9,8},{10,11... | collective-permute-start | bytes 393224 | tf_op jit(solution)/shard_map/ppermute | solution.py:395
  6.0 13.0 %all-to-all-start = ((f32[32,4,128]{2,1,0:T(4,128)}), f32[32,4,128]{2,1,0:T(4,128)S(1)}, u32[]{:S(2)}, u32[]{:S(2)}) async-start(f32[32,4,128]{2,1,0:T(4,128)} %get-tuple-element.25), calls=%async_computation | async-start | bytes 131072 | tf_op jit(solution)/shard_map/all_to_all | solution.py:394
  11.0 8.0 %collective-permute-start.2 = (bf16[64,512]{1,0:T(8,128)(2,1)S(1)}, bf16[64,512]{1,0:T(8,128)(2,1)S(1)}, u32[]{:S(2)}, u32[]{:S(2)}) collective-permute-start(bf16[64,512]{1,0:T(8,128)(2,1)S(1)} %join.1.refs_1_), channel_id=1, source_target_pairs={{2,4},{4,2},{3,5},{5,3},{6,8},{8,6},{7,9},{9,7},{10,12},{12,10},{1... | collective-permute-start | bytes 196616 | tf_op jit(solution)/shard_map/ppermute | solution.py:449
  15.3 3.7 %collective-permute-start.1 = (bf16[64,512]{1,0:T(8,128)(2,1)S(1)}, bf16[64,512]{1,0:T(8,128)(2,1)S(1)}, u32[]{:S(2)}, u32[]{:S(2)}) collective-permute-start(bf16[64,512]{1,0:T(8,128)(2,1)S(1)} %join.1.refs_1_), channel_id=1, source_target_pairs={{0,2},{2,0},{1,3},{3,1},{4,6},{6,4},{5,7},{7,5},{8,10},{10,8},{9,1... | collective-permute-start | bytes 196616 | tf_op jit(solution)/shard_map/ppermute | solution.py:449
  24.4 6.5 %collective-permute-start.3 = (bf16[128,512]{1,0:T(8,128)(2,1)S(1)}, bf16[128,512]{1,0:T(8,128)(2,1)S(1)}, u32[]{:S(2)}, u32[]{:S(2)}) collective-permute-start(bf16[128,512]{1,0:T(8,128)(2,1)S(1)} %get-tuple-element.36), channel_id=1, source_target_pairs={{0,2},{2,0},{1,3},{3,1},{4,6},{6,4},{5,7},{7,5},{8,10},{10,8},{9,1... | collective-permute-start | bytes 393224 | tf_op jit(solution)/shard_map/ppermute | solution.py:522
  24.5 7.2 %collective-permute-start.4 = (bf16[128,512]{1,0:T(8,128)(2,1)S(1)}, bf16[128,512]{1,0:T(8,128)(2,1)S(1)}, u32[]{:S(2)}, u32[]{:S(2)}) collective-permute-start(bf16[128,512]{1,0:T(8,128)(2,1)S(1)} %get-tuple-element.37), channel_id=1, source_target_pairs={{2,4},{4,2},{3,5},{5,3},{6,8},{8,6},{7,9},{9,7},{10,12},{12,10},{1... | collective-permute-start | bytes 393224 | tf_op jit(solution)/shard_map/ppermute | solution.py:522
  27.9 10.5 %all-to-all-start.1 = ((f32[32,4,128]{2,1,0:T(4,128)}), f32[32,4,128]{2,1,0:T(4,128)S(1)}, u32[]{:S(2)}, u32[]{:S(2)}) async-start(f32[32,4,128]{2,1,0:T(4,128)} %gather.1), calls=%async_computation.1 | async-start | bytes 131072 | tf_op jit(solution)/shard_map/all_to_all | solution.py:528
  31.7 6.8 %collective-permute-start.5 = (bf16[32,512]{1,0:T(8,128)(2,1)S(1)}, bf16[32,512]{1,0:T(8,128)(2,1)S(1)}, u32[]{:S(2)}, u32[]{:S(2)}) collective-permute-start(bf16[32,512]{1,0:T(8,128)(2,1)S(1)} %get-tuple-element.43), channel_id=1, source_target_pairs={{0,1},{1,0},{2,3},{3,2},{4,5},{5,4},{6,7},{7,6},{8,9},{9,8},{10,11... | collective-permute-start | bytes 98312 | tf_op jit(solution)/shard_map/ppermute | solution.py:536

commit v4 on v3

--- a/solution.py
+++ b/solution.py
@@ -130,10 +130,10 @@
     border[: plan.halo] = dot_tn(pick, rows).astype(BF16)
     own = dot_tn(as_one_hot(one_hot_rows(list_s[0], plan.nodes)), rows)
     parts = plan.width // 128
-    for k in range(plan.owned):
-        for q in range(parts):
-            piece = own[k : k + 1, q * 128 : (q + 1) * 128]
-            coarse[:, k * parts + q, :] = jnp.broadcast_to(piece, (plan.devices, 128))
+    pieces = [
+        own[k : k + 1, q * 128 : (q + 1) * 128] for k in range(plan.owned) for q in range(parts)
+    ]
+    coarse[...] = jnp.broadcast_to(jnp.concatenate(pieces, axis=0)[None], coarse.shape)
 
 
 def block_of(ref, part, width):
@@ -185,15 +185,6 @@
         refs[-1][k * plan.halo : (k + 1) * plan.halo] = part[: plan.halo]
 
 
-def gather_kernel(plan, rows, _, coarse):
-    parts = plan.width // 128
-    for k in range(plan.owned):
-        for q in range(parts):
-            coarse[:, k * parts + q, :] = rows[
-                k * plan.devices : (k + 1) * plan.devices, q * 128 : (q + 1) * 128
-            ]
-
-
 def edge_cotangent(cot_edge, received, agg_grad):
     twice = jnp.concatenate([received, received], axis=0)
     return cot_edge[0, 0].astype(F32) + dot_tn(twice, agg_grad)
@@ -202,9 +193,9 @@
 def main_kernel(plan, *refs):
     here = dict(zip(plan.main_names, refs))
     refs = refs[len(plan.main_names) :]
-    even_grad, odd_grad, coarse_grad, kept_grad, agg_out, edge_dpre_out, local = refs[:7]
-    new_nodes, table, new_s = refs[7:10]
-    sems, held = refs[-1], dict(zip(plan.main_held, refs[10:-1]))
+    even_grad, odd_grad, kept_grad, agg_out, edge_dpre_out, local = refs[:6]
+    new_nodes, coarse_grad, table, new_s, tiles, coarse_s = refs[6:12]
+    sems, held = refs[-1], dict(zip(plan.main_held, refs[12:-1]))
     nodes, halo, width = plan.nodes, plan.halo, plan.width
     sent, received = here["sent"], here["received"][...]
     live = jnp.where(
@@ -273,14 +264,23 @@
     away_grad = dot_nt(dot_nn(sent[...], edge_dpre).astype(BF16), w_edge_mid)
     own_grad, away_grad = away_grad[:nodes], away_grad[nodes:]
     kept = plan.per_lon * halo
+    start = 3 * kept
+    for k in range(plan.owned):
+        for q in range(parts):
+            tiles[:, k * parts + q, :] = away_grad[
+                start : start + plan.devices, q * 128 : (q + 1) * 128
+            ]
+        start += plan.devices
+    coarse_s[...] = tiles[...].astype(BF16)
+    coarse_leaving = moves.start(coarse_s, coarse_grad)
+    even_grad[...] = away_grad[kept : 2 * kept].astype(BF16)
+    odd_grad[...] = away_grad[2 * kept : 3 * kept].astype(BF16)
     kept_grad[...] = away_grad[:kept]
-    even_grad[:kept] = away_grad[kept : 2 * kept].astype(BF16)
-    odd_grad[:kept] = away_grad[2 * kept : 3 * kept].astype(BF16)
-    coarse_grad[...] = away_grad[3 * kept :]
     local[...] = (
         got("cot_node")[0, 0].astype(F32) + dot_nt(node_dpre, got("w_node_top")[...]) + own_grad
     )
     leaving.wait()
+    coarse_leaving.wait()
 
 
 def behind_kernel(plan, *refs):
@@ -303,8 +303,7 @@
 
 
 def middle_kernel(plan, kept, even, odd, mine, *lat_sends):
-    rows = kept.shape[0]
-    total = kept[...] + even[:rows].astype(F32) + odd[:rows].astype(F32)
+    total = kept[...] + even[...].astype(F32) + odd[...].astype(F32)
     mine[...] = total[: plan.halo]
     for k, out in enumerate(lat_sends):
         out[...] = total[(k + 1) * plan.halo : (k + 2) * plan.halo].astype(BF16)
@@ -317,7 +316,7 @@
     for part in refs[5:-1]:
         total = total + part[...].astype(F32)
     result = grad_local[...] + dot_nn(place[...], in_two(total))
-    share = jnp.sum(coarse[...], axis=0)
+    share = jnp.sum(coarse[...].astype(F32), axis=0)
     parts = plan.width // 128
     for k in range(plan.owned):
         row = jnp.concatenate([share[k * parts + q : k * parts + q + 1] for q in range(parts)], axis=1)
@@ -406,6 +405,11 @@
         "coarse_list": coarse_list,
         "w_node_in": w_node_in,
         "b_node_in": row(b_node_in),
+        "w_edge_out": w_edge_out,
+        "gain_edge": row(gain_edge),
+        "shift_edge": row(shift_edge),
+        "gain_node": row(gain_node),
+        "shift_node": row(shift_node),
     }
     square = ((width, width), BF16)
     copies = {name: (name, None) for name in far if name not in ("w_edge_in", "w_node_in")}
@@ -413,7 +417,9 @@
     copies["w_edge_low"] = ("w_edge_in", 2)
     copies["w_node_top"] = ("w_node_in", 0)
     copies["w_edge_mid"] = ("w_edge_in", 1)
+    passed_on = ("node", "w_edge_out", "gain_edge", "shift_edge", "gain_node", "shift_node")
     outs = {
+        **{name: (far[name].shape, far[name].dtype) for name in passed_on},
         "w_edge_mid": square,
         "edge_part": ((edges, width), F32),
         "node_part": ((nodes, width), F32),
@@ -462,45 +468,45 @@
                 "node_part",
                 "sent",
                 "received",
+                *passed_on,
             )
         },
     }
     far = {
-        "w_edge_out": w_edge_out,
-        "node": node_feat,
-        "gain_edge": row(gain_edge),
-        "shift_edge": row(shift_edge),
         "edge": edge_feat,
         "w_node_in": w_node_in,
         "w_node_out": w_node_out,
-        "gain_node": row(gain_node),
-        "shift_node": row(shift_node),
         "cot_node": cot_node,
         "cot_edge": cot_edge,
     }
-    copies = {name: (name, None) for name in far if name not in ("w_edge_in", "w_node_in")}
-    copies["w_node_low"] = ("w_node_in", 1)
-    copies["w_node_top"] = ("w_node_in", 0)
+    copies = {
+        "edge": ("edge", None),
+        "w_node_low": ("w_node_in", 1),
+        "w_node_out": ("w_node_out", None),
+        "cot_node": ("cot_node", None),
+        "cot_edge": ("cot_edge", None),
+        "w_node_top": ("w_node_in", 0),
+    }
     plan.main_names, plan.main_copies, plan.main_held = [*near, *far], copies, list(copies)
     outs = [
-        ((max(kept, SENT_ROWS), width), BF16),
-        ((max(kept, SENT_ROWS), width), BF16),
-        ((plan.coarse, width), F32),
+        ((kept, width), BF16),
+        ((kept, width), BF16),
         ((kept, width), F32),
         ((2 * nodes, width), BF16),
         ((edges, width), BF16),
         ((nodes, width), F32),
         (node_feat.shape, BF16),
+        (coarse_shape, BF16),
     ]
     (
         even_grad,
         odd_grad,
-        coarse_grad,
         kept_grad,
         agg_grad,
         edge_dpre,
         local,
         new_nodes,
+        coarse_send,
     ) = call(
         with_plan(main_kernel),
         "main",
@@ -508,23 +514,21 @@
         list(near.values()),
         far=list(far.values()),
         scratch=[VMEM((plan.table, width), BF16), VMEM(node_feat.shape, BF16)]
+        + [VMEM(coarse_shape, F32), VMEM(coarse_shape, BF16)]
         + [
             VMEM(*(square if part is not None else (far[source].shape, far[source].dtype)))
             for source, part in copies.values()
         ]
-        + [sems(len(copies) + 1)],
+        + [sems(len(copies) + 2)],
         flops=2 * 5 * edges * width * width,
         mib=20,
-        results=1,
+        results=2,
     )
 
     even_back, odd_back = [
         lax.ppermute(grad, axes, pairs)
         for grad, pairs in zip((even_grad, odd_grad), plan.lon_pairs)
     ]
-    (coarse_send,) = call(
-        with_plan(gather_kernel), "gather", [(coarse_shape, F32)], [coarse_grad, coarse_grad]
-    )
     coarse_back = lax.all_to_all(coarse_send, axes, 0, 0, tiled=True)
     mine, *lat_sends = call(
         with_plan(middle_kernel),

time: 39.6 us -> 38.2 us (0.965)
  Pallas kernels: 13.6 us -> 12.5 us
  waiting for transfers between devices: 4.1 us -> 3.52 us
  starting transfers between devices: 19.5 us -> 19.9 us
    pallas_call x8 -> x7, Pallas kernels: 13.6 us -> 12.5 us  [call(): pl.pallas_call(body, name=name, out_shape=[VMEM(shape, dtype) for shape,...]
where the time goes in v4:
time: 38.2 us; the launch traced here: 37.9 us
  starting transfers between devices  19.9 us (52%)
  Pallas kernels  12.5 us (33%)
  waiting for transfers between devices  3.52 us (9%)
  between operations  2.01 us (5%)
    pallas_call x7, Pallas kernels, call(): pl.pallas_call(body, name=name, out_shape=[VMEM(shape, dtype) for shape,...  12.5 us
    all_to_all x1, starting transfers between devices, body(): coarse_rows = lax.all_to_all(coarse_out, axes, 0, 0, tiled=True)  4.92 us
    ppermute x3, starting transfers between devices, body(): lax.ppermute(grad, axes, pairs)  4.43 us
    ppermute x2, starting transfers between devices, body(): lax.ppermute(wide, axes, pairs)  4.37 us
    all_to_all x1, starting transfers between devices, body(): coarse_back = lax.all_to_all(coarse_send, axes, 0, 0, tiled=True)  3.14 us
    ppermute x1, starting transfers between devices, body(): lat_rows = [lax.ppermute(border, axes, pairs) for pairs in plan.lat_pairs]  3 us
    all_to_all x1, waiting for transfers between devices, body(): coarse_back = lax.all_to_all(coarse_send, axes, 0, 0, tiled=True)  2.55 us
  transfers between devices with their start and end apart: 8, of which 3 were waited for; matrix products, arithmetic and copies ran while one was open for 0% of the time, Pallas kernels for 14%

profile of v4, /device:TPU:0, one launch (start us, length us, event | category | flops | bytes accessed | tf_op | source)
XLA Modules:
  0.0 37.9 jit_solution(5973516244283680836)
XLA Ops:
  1.3 1.7 %pack.1 = (bf16[128,512]{1,0:T(8,128)(2,1)S(1)}, f32[32,4,128]{2,1,0:T(4,128)}) custom-call(bf16[1,1,64,512]{3,2,1,0:T(8,128)(2,1)} %refs_2_.1, s32[1,1,32]{2,1,0:T(1,128)} %refs_7_.1, s32[1,1,1]{2,1,0:T(1,128)S(6)} %copy.23.coarse_list.refs_8_), custom_call_target="tpu_custom_call" | custom-call | bytes 65668 | tf_op jit(solution)/shard_map/pack/pallas_call | solution.py:334
  3.0 3.0 %collective-permute-start = (bf16[128,512]{1,0:T(8,128)(2,1)S(1)}, bf16[128,512]{1,0:T(8,128)(2,1)S(1)}, u32[]{:S(2)}, u32[]{:S(2)}) collective-permute-start(bf16[128,512]{1,0:T(8,128)(2,1)S(1)} %get-tuple-element.30.refs_0_), channel_id=1, source_target_pairs={{0,1},{1,0},{2,3},{3,2},{4,5},{5,4},{6,7},{7,6},{8,9},{9,8},{10,11... | collective-permute-start | bytes 393224 | tf_op jit(solution)/shard_map/ppermute | solution.py:394
  6.0 4.9 %all-to-all-start = ((f32[32,4,128]{2,1,0:T(4,128)}), f32[32,4,128]{2,1,0:T(4,128)S(1)}, u32[]{:S(2)}, u32[]{:S(2)}) async-start(f32[32,4,128]{2,1,0:T(4,128)} %get-tuple-element.31), calls=%async_computation | async-start | bytes 131072 | tf_op jit(solution)/shard_map/all_to_all | solution.py:393
  10.9 0.0 collective-permute-done.refs_1_
  11.0 4.4 %collective-permute-start.2 = (bf16[64,512]{1,0:T(8,128)(2,1)S(1)}, bf16[64,512]{1,0:T(8,128)(2,1)S(1)}, u32[]{:S(2)}, u32[]{:S(2)}) collective-permute-start(bf16[64,512]{1,0:T(8,128)(2,1)S(1)} %join.1.refs_1_), channel_id=1, source_target_pairs={{2,4},{4,2},{3,5},{5,3},{6,8},{8,6},{7,9},{9,7},{10,12},{12,10},{1... | collective-permute-start | bytes 196616 | tf_op jit(solution)/shard_map/ppermute | solution.py:455
  15.3 0.0 collective-permute-start.1
  16.0 2.7 %ahead.1 = (bf16[1,1,64,512]{3,2,1,0:T(8,128)(2,1)S(1)}, bf16[512,512]{1,0:T(8,128)(2,1)S(1)}, f32[1,512]{1,0:T(1,128)S(1)}, f32[1,512]{1,0:T(1,128)S(1)}, f32[1...) custom-call(s32[1,1]{1,0:T(1,128)S(6)} %copy.22.refs_0_, ...), custom_call_target="tpu_custom_call" | custom-call | flops 436207616 | bytes 3619976 | tf_op jit(solution)/shard_map/ahead/pallas_call | solution.py:334
  18.7 0.3 all-to-all-done.refs_4_
  19.0 0.0 collective-permute-done.2.refs_3_
  19.0 0.0 collective-permute-done.1.refs_2_
  19.0 4.7 %main.1 = (bf16[64,512]{1,0:T(8,128)(2,1)S(1)}, bf16[64,512]{1,0:T(8,128)(2,1)S(1)}, f32[64,512]{1,0:T(8,128)S(1)}, bf16[128,512]{1,0:T(8,128)(2,1)S(1)}, bf16[3...) custom-call(s32[1,1]{1,0:T(1,128)S(6)} %copy.22.refs_0_, ...), custom_call_target="tpu_custom_call" | custom-call | flops 1006632960 | bytes 4997124 | tf_op jit(solution)/shard_map/main/pallas_call | solution.py:334
  23.7 0.3 collective-permute-start.3
  24.0 2.6 %collective-permute-start.4 = (bf16[64,512]{1,0:T(8,128)(2,1)S(1)}, bf16[64,512]{1,0:T(8,128)(2,1)S(1)}, u32[]{:S(2)}, u32[]{:S(2)}) collective-permute-start(bf16[64,512]{1,0:T(8,128)(2,1)S(1)} %get-tuple-element.49), channel_id=1, source_target_pairs={{2,4},{4,2},{3,5},{5,3},{6,8},{8,6},{7,9},{9,7},{10,12},{12,10},{1... | collective-permute-start | bytes 196616 | tf_op jit(solution)/shard_map/ppermute | solution.py:529
  26.6 3.1 %all-to-all-start.1 = ((bf16[32,4,128]{2,1,0:T(4,128)(2,1)}), bf16[32,4,128]{2,1,0:T(4,128)(2,1)S(1)}, u32[]{:S(2)}, u32[]{:S(2)}) async-start(bf16[32,4,128]{2,1,0:T(4,128)(2,1)} %get-tuple-element.54), calls=%async_computation.1 | async-start | bytes 65536 | tf_op jit(solution)/shard_map/all_to_all | solution.py:532
  29.7 0.0 collective-permute-done.3.even
  29.7 0.6 %collective-permute-done.4.odd = bf16[64,512]{1,0:T(8,128)(2,1)S(1)} collective-permute-done((bf16[64,512]{1,0:T(8,128)(2,1)S(1)}, bf16[64,512]{1,0:T(8,128)(2,1)S(1)}, u32[]{:S(2)}, u32[]{:S(2)}) %collective-permute-start.4) | collective-permute-done | bytes 65568 | tf_op jit(solution)/shard_map/ppermute | solution.py:529
  30.4 1.5 %collective-permute-start.5 = (bf16[32,512]{1,0:T(8,128)(2,1)S(1)}, bf16[32,512]{1,0:T(8,128)(2,1)S(1)}, u32[]{:S(2)}, u32[]{:S(2)}) collective-permute-start(bf16[32,512]{1,0:T(8,128)(2,1)S(1)} %get-tuple-element.55), channel_id=1, source_target_pairs={{0,1},{1,0},{2,3},{3,2},{4,5},{5,4},{6,7},{7,6},{8,9},{9,8},{10,11... | collective-permute-start | bytes 98312 | tf_op jit(solution)/shard_map/ppermute | solution.py:540
  32.0 2.6 %behind.1 = (f32[64,512]{1,0:T(8,128)S(1)}, bf16[1,1,384,512]{3,2,1,0:T(8,128)(2,1)}) custom-call(bf16[64,384]{1,0:T(8,128)(2,1)S(1)} %get-tuple-element.36.refs_9_.refs_0_, bf16[384,512]{1,0:T(8,128)(2,1)S(1)} %get-tuple-element.44.refs_1_, bf16[128,512]{1,0:T(8,128)(2,1)S(1)} %get-tuple-element.45.refs_2_, f32[64,512]{1,0:T(8,128)S(1)} %get-tuple-element.46.refs_3_, ...), custom_call_target="tpu_custom_call" | custom-call | flops 234881024 | bytes 2736128 | tf_op jit(solution)/shard_map/behind/pallas_call | solution.py:334
  34.5 2.6 %all-to-all-done.1.refs_4_ = bf16[32,4,128]{2,1,0:T(4,128)(2,1)S(1)} async-done(((bf16[32,4,128]{2,1,0:T(4,128)(2,1)}), bf16[32,4,128]{2,1,0:T(4,128)(2,1)S(1)}, u32[]{:S(2)}, u32[]{:S(2)}) %all-to-all-start.1) | async-done | bytes 32800 | tf_op jit(solution)/shard_map/all_to_all | solution.py:532
  37.1 0.0 collective-permute-done.5.refs_5_
  37.1 0.8 %last.1 = bf16[1,1,64,512]{3,2,1,0:T(8,128)(2,1)} custom-call(f32[64,512]{1,0:T(8,128)S(1)} %get-tuple-element.51.refs_0_, f32[32,512]{1,0:T(8,128)S(1)} %get-tuple-element.50.refs_4_.refs_1_, bf16[64,64]{1,0:T(8,128)(2,1)S(1)} %get-tuple-element.52.refs_2_, f32[64,1]{1,0:T(8,128)S(1)} %get-tuple-element.53.refs_3_, ...), custom_call_target="tpu_custom_call" | custom-call | bytes 270592 | tf_op jit(solution)/shard_map/last/pallas_call | solution.py:334
  (2 shorter events, 0.0 us)
Async XLA Ops:
  3.0 7.9 %collective-permute-start = (bf16[128,512]{1,0:T(8,128)(2,1)S(1)}, bf16[128,512]{1,0:T(8,128)(2,1)S(1)}, u32[]{:S(2)}, u32[]{:S(2)}) collective-permute-start(bf16[128,512]{1,0:T(8,128)(2,1)S(1)} %get-tuple-element.30.refs_0_), channel_id=1, source_target_pairs={{0,1},{1,0},{2,3},{3,2},{4,5},{5,4},{6,7},{7,6},{8,9},{9,8},{10,11... | collective-permute-start | bytes 393224 | tf_op jit(solution)/shard_map/ppermute | solution.py:394
  6.0 13.0 %all-to-all-start = ((f32[32,4,128]{2,1,0:T(4,128)}), f32[32,4,128]{2,1,0:T(4,128)S(1)}, u32[]{:S(2)}, u32[]{:S(2)}) async-start(f32[32,4,128]{2,1,0:T(4,128)} %get-tuple-element.31), calls=%async_computation | async-start | bytes 131072 | tf_op jit(solution)/shard_map/all_to_all | solution.py:393
  11.0 8.0 %collective-permute-start.2 = (bf16[64,512]{1,0:T(8,128)(2,1)S(1)}, bf16[64,512]{1,0:T(8,128)(2,1)S(1)}, u32[]{:S(2)}, u32[]{:S(2)}) collective-permute-start(bf16[64,512]{1,0:T(8,128)(2,1)S(1)} %join.1.refs_1_), channel_id=1, source_target_pairs={{2,4},{4,2},{3,5},{5,3},{6,8},{8,6},{7,9},{9,7},{10,12},{12,10},{1... | collective-permute-start | bytes 196616 | tf_op jit(solution)/shard_map/ppermute | solution.py:455
  15.3 3.7 %collective-permute-start.1 = (bf16[64,512]{1,0:T(8,128)(2,1)S(1)}, bf16[64,512]{1,0:T(8,128)(2,1)S(1)}, u32[]{:S(2)}, u32[]{:S(2)}) collective-permute-start(bf16[64,512]{1,0:T(8,128)(2,1)S(1)} %join.1.refs_1_), channel_id=1, source_target_pairs={{0,2},{2,0},{1,3},{3,1},{4,6},{6,4},{5,7},{7,5},{8,10},{10,8},{9,1... | collective-permute-start | bytes 196616 | tf_op jit(solution)/shard_map/ppermute | solution.py:455
  23.7 6.0 %collective-permute-start.3 = (bf16[64,512]{1,0:T(8,128)(2,1)S(1)}, bf16[64,512]{1,0:T(8,128)(2,1)S(1)}, u32[]{:S(2)}, u32[]{:S(2)}) collective-permute-start(bf16[64,512]{1,0:T(8,128)(2,1)S(1)} %get-tuple-element.48), channel_id=1, source_target_pairs={{0,2},{2,0},{1,3},{3,1},{4,6},{6,4},{5,7},{7,5},{8,10},{10,8},{9,1... | collective-permute-start | bytes 196616 | tf_op jit(solution)/shard_map/ppermute | solution.py:529
  24.0 6.4 %collective-permute-start.4 = (bf16[64,512]{1,0:T(8,128)(2,1)S(1)}, bf16[64,512]{1,0:T(8,128)(2,1)S(1)}, u32[]{:S(2)}, u32[]{:S(2)}) collective-permute-start(bf16[64,512]{1,0:T(8,128)(2,1)S(1)} %get-tuple-element.49), channel_id=1, source_target_pairs={{2,4},{4,2},{3,5},{5,3},{6,8},{8,6},{7,9},{9,7},{10,12},{12,10},{1... | collective-permute-start | bytes 196616 | tf_op jit(solution)/shard_map/ppermute | solution.py:529
  26.6 10.5 %all-to-all-start.1 = ((bf16[32,4,128]{2,1,0:T(4,128)(2,1)}), bf16[32,4,128]{2,1,0:T(4,128)(2,1)S(1)}, u32[]{:S(2)}, u32[]{:S(2)}) async-start(bf16[32,4,128]{2,1,0:T(4,128)(2,1)} %get-tuple-element.54), calls=%async_computation.1 | async-start | bytes 65536 | tf_op jit(solution)/shard_map/all_to_all | solution.py:532
  30.4 6.7 %collective-permute-start.5 = (bf16[32,512]{1,0:T(8,128)(2,1)S(1)}, bf16[32,512]{1,0:T(8,128)(2,1)S(1)}, u32[]{:S(2)}, u32[]{:S(2)}) collective-permute-start(bf16[32,512]{1,0:T(8,128)(2,1)S(1)} %get-tuple-element.55), channel_id=1, source_target_pairs={{0,1},{1,0},{2,3},{3,2},{4,5},{5,4},{6,7},{7,6},{8,9},{9,8},{10,11... | collective-permute-start | bytes 98312 | tf_op jit(solution)/shard_map/ppermute | solution.py:540

commit v5 on v4

--- a/solution.py
+++ b/solution.py
@@ -193,9 +193,10 @@
 def main_kernel(plan, *refs):
     here = dict(zip(plan.main_names, refs))
     refs = refs[len(plan.main_names) :]
-    even_grad, odd_grad, kept_grad, agg_out, edge_dpre_out, local = refs[:6]
-    new_nodes, coarse_grad, table, new_s, tiles, coarse_s = refs[6:12]
-    sems, held = refs[-1], dict(zip(plan.main_held, refs[12:-1]))
+    kept_grad, agg_out, edge_dpre_out, local = refs[:4]
+    lat_grads, refs = refs[4 : 3 + plan.per_lon], refs[3 + plan.per_lon :]
+    new_nodes, coarse_grad, table, new_s, tiles, coarse_s = refs[:6]
+    sems, held = refs[-1], dict(zip(plan.main_held, refs[6:-1]))
     nodes, halo, width = plan.nodes, plan.halo, plan.width
     sent, received = here["sent"], here["received"][...]
     live = jnp.where(
@@ -273,9 +274,12 @@
         start += plan.devices
     coarse_s[...] = tiles[...].astype(BF16)
     coarse_leaving = moves.start(coarse_s, coarse_grad)
-    even_grad[...] = away_grad[kept : 2 * kept].astype(BF16)
-    odd_grad[...] = away_grad[2 * kept : 3 * kept].astype(BF16)
-    kept_grad[...] = away_grad[:kept]
+    for a in range(3):
+        rows = slice(a * halo, (a + 1) * halo)
+        kept_grad[rows] = away_grad[a * kept : a * kept + halo].astype(BF16)
+        for k, lat_grad in enumerate(lat_grads):
+            first = a * kept + (k + 1) * halo
+            lat_grad[rows] = away_grad[first : first + halo].astype(BF16)
     local[...] = (
         got("cot_node")[0, 0].astype(F32) + dot_nt(node_dpre, got("w_node_top")[...]) + own_grad
     )
@@ -302,11 +306,15 @@
     leaving.wait()
 
 
-def middle_kernel(plan, kept, even, odd, mine, *lat_sends):
-    total = kept[...] + even[...].astype(F32) + odd[...].astype(F32)
-    mine[...] = total[: plan.halo]
-    for k, out in enumerate(lat_sends):
-        out[...] = total[(k + 1) * plan.halo : (k + 2) * plan.halo].astype(BF16)
+def middle_kernel(plan, kept, *refs):
+    total = kept[...].astype(F32)
+    for part in refs[:-3]:
+        total = total + part[...].astype(F32)
+    mine, even, odd = refs[-3:]
+    halo = plan.halo
+    mine[...] = total[:halo]
+    even[...] = total[halo : 2 * halo].astype(BF16)
+    odd[...] = total[2 * halo :].astype(BF16)
 
 
 def last_kernel(plan, *refs):
@@ -489,25 +497,15 @@
     }
     plan.main_names, plan.main_copies, plan.main_held = [*near, *far], copies, list(copies)
     outs = [
-        ((kept, width), BF16),
-        ((kept, width), BF16),
-        ((kept, width), F32),
+        ((3 * halo, width), BF16),
         ((2 * nodes, width), BF16),
         ((edges, width), BF16),
         ((nodes, width), F32),
+        *[((3 * halo, width), BF16)] * len(plan.lat_pairs),
         (node_feat.shape, BF16),
         (coarse_shape, BF16),
     ]
-    (
-        even_grad,
-        odd_grad,
-        kept_grad,
-        agg_grad,
-        edge_dpre,
-        local,
-        new_nodes,
-        coarse_send,
-    ) = call(
+    kept_grad, agg_grad, edge_dpre, local, *lat_grads, new_nodes, coarse_send = call(
         with_plan(main_kernel),
         "main",
         outs,
@@ -525,19 +523,19 @@
         results=2,
     )
 
-    even_back, odd_back = [
+    lat_back = [
+        lax.ppermute(grad, axes, pairs) for grad, pairs in zip(lat_grads, plan.lat_pairs)
+    ]
+    coarse_back = lax.all_to_all(coarse_send, axes, 0, 0, tiled=True)
+    mine, even_grad, odd_grad = call(
+        with_plan(middle_kernel),
+        "middle",
+        [((halo, width), F32), ((halo, width), BF16), ((halo, width), BF16)],
+        [kept_grad, *lat_back],
+    )
+    lon_back = [
         lax.ppermute(grad, axes, pairs)
         for grad, pairs in zip((even_grad, odd_grad), plan.lon_pairs)
-    ]
-    coarse_back = lax.all_to_all(coarse_send, axes, 0, 0, tiled=True)
-    mine, *lat_sends = call(
-        with_plan(middle_kernel),
-        "middle",
-        [((halo, width), F32)] + [((halo, width), BF16)] * len(plan.lat_pairs),
-        [kept_grad, even_back, odd_back],
-    )
-    lat_back = [
-        lax.ppermute(grad, axes, pairs) for grad, pairs in zip(lat_sends, plan.lat_pairs)
     ]
     grad_local, grad_edges = call(
         with_plan(behind_kernel),
@@ -554,7 +552,7 @@
         with_plan(last_kernel),
         "last",
         [(node_feat.shape, BF16)],
-        [grad_local, mine, at["place"], at["at_coarse"], coarse_back, *lat_back],
+        [grad_local, mine, at["place"], at["at_coarse"], coarse_back, *lon_back],
         results=1,
     )
     return new_nodes, grad_nodes, grad_edges

time: 38.2 us -> 36.9 us (0.966)
  waiting for transfers between devices: 3.52 us -> 0.96 us
  starting transfers between devices: 19.9 us -> 20.8 us
    all_to_all x1, waiting for transfers between devices: 2.55 us -> 0.01 us  [body(): coarse_back = lax.all_to_all(coarse_send, axes, 0, 0, tiled=True)]
    ppermute x3, starting transfers between devices: 4.43 us -> 5.4 us  [body(): lax.ppermute(grad, axes, pairs)]
  transfers between devices with their start and end apart: 8 -> 8, of which waited for: 3 -> 2; matrix products, arithmetic and copies ran while one was open for 0% -> 0% of each run, Pallas kernels for 14% -> 14%
where the time goes in v5:
time: 36.9 us; the launch traced here: 36.6 us
  starting transfers between devices  20.8 us (56%)
  Pallas kernels  12.8 us (35%)
  between operations  2.02 us (5%)
  waiting for transfers between devices  0.96 us (3%)
    pallas_call x7, Pallas kernels, call(): pl.pallas_call(body, name=name, out_shape=[VMEM(shape, dtype) for shape,...  12.8 us
    ppermute x3, starting transfers between devices, body(): lax.ppermute(grad, axes, pairs)  5.4 us
    all_to_all x1, starting transfers between devices, body(): coarse_rows = lax.all_to_all(coarse_out, axes, 0, 0, tiled=True)  4.92 us
    ppermute x2, starting transfers between devices, body(): lax.ppermute(wide, axes, pairs)  4.37 us
    all_to_all x1, starting transfers between devices, body(): coarse_back = lax.all_to_all(coarse_send, axes, 0, 0, tiled=True)  3.09 us
    ppermute x1, starting transfers between devices, body(): lat_rows = [lax.ppermute(border, axes, pairs) for pairs in plan.lat_pairs]  3 us
  transfers between devices with their start and end apart: 8, of which 2 were waited for; matrix products, arithmetic and copies ran while one was open for 0% of the time, Pallas kernels for 14%

profile of v5, /device:TPU:0, one launch (start us, length us, event | category | flops | bytes accessed | tf_op | source)
XLA Modules:
  0.0 36.6 jit_solution(1158663319435541460)
XLA Ops:
  1.3 1.7 %pack.1 = (bf16[128,512]{1,0:T(8,128)(2,1)S(1)}, f32[32,4,128]{2,1,0:T(4,128)}) custom-call(bf16[1,1,64,512]{3,2,1,0:T(8,128)(2,1)} %refs_2_.1, s32[1,1,32]{2,1,0:T(1,128)} %refs_7_.1, s32[1,1,1]{2,1,0:T(1,128)S(6)} %copy.23.coarse_list.refs_8_), custom_call_target="tpu_custom_call" | custom-call | bytes 65668 | tf_op jit(solution)/shard_map/pack/pallas_call | solution.py:342
  3.0 3.0 %collective-permute-start = (bf16[128,512]{1,0:T(8,128)(2,1)S(1)}, bf16[128,512]{1,0:T(8,128)(2,1)S(1)}, u32[]{:S(2)}, u32[]{:S(2)}) collective-permute-start(bf16[128,512]{1,0:T(8,128)(2,1)S(1)} %get-tuple-element.30.refs_0_), channel_id=1, source_target_pairs={{0,1},{1,0},{2,3},{3,2},{4,5},{5,4},{6,7},{7,6},{8,9},{9,8},{10,11... | collective-permute-start | bytes 393224 | tf_op jit(solution)/shard_map/ppermute | solution.py:402
  6.0 4.9 %all-to-all-start = ((f32[32,4,128]{2,1,0:T(4,128)}), f32[32,4,128]{2,1,0:T(4,128)S(1)}, u32[]{:S(2)}, u32[]{:S(2)}) async-start(f32[32,4,128]{2,1,0:T(4,128)} %get-tuple-element.31), calls=%async_computation | async-start | bytes 131072 | tf_op jit(solution)/shard_map/all_to_all | solution.py:401
  10.9 0.0 collective-permute-done.refs_1_
  11.0 4.4 %collective-permute-start.2 = (bf16[64,512]{1,0:T(8,128)(2,1)S(1)}, bf16[64,512]{1,0:T(8,128)(2,1)S(1)}, u32[]{:S(2)}, u32[]{:S(2)}) collective-permute-start(bf16[64,512]{1,0:T(8,128)(2,1)S(1)} %join.1.refs_1_), channel_id=1, source_target_pairs={{2,4},{4,2},{3,5},{5,3},{6,8},{8,6},{7,9},{9,7},{10,12},{12,10},{1... | collective-permute-start | bytes 196616 | tf_op jit(solution)/shard_map/ppermute | solution.py:463
  15.3 0.0 collective-permute-start.1
  16.0 2.7 %ahead.1 = (bf16[1,1,64,512]{3,2,1,0:T(8,128)(2,1)S(1)}, bf16[512,512]{1,0:T(8,128)(2,1)S(1)}, f32[1,512]{1,0:T(1,128)S(1)}, f32[1,512]{1,0:T(1,128)S(1)}, f32[1...) custom-call(s32[1,1]{1,0:T(1,128)S(6)} %copy.22.refs_0_, ...), custom_call_target="tpu_custom_call" | custom-call | flops 436207616 | bytes 3619976 | tf_op jit(solution)/shard_map/ahead/pallas_call | solution.py:342
  18.7 0.3 all-to-all-done.refs_4_
  19.0 0.0 collective-permute-done.2.refs_3_
  19.0 0.0 collective-permute-done.1.refs_2_
  19.0 5.0 %main.1 = (bf16[96,512]{1,0:T(8,128)(2,1)S(1)}, bf16[128,512]{1,0:T(8,128)(2,1)S(1)}, bf16[384,512]{1,0:T(8,128)(2,1)S(1)}, f32[64,512]{1,0:T(8,128)S(1)}, bf16[...) custom-call(s32[1,1]{1,0:T(1,128)S(6)} %copy.22.refs_0_, ...), custom_call_target="tpu_custom_call" | custom-call | flops 1006632960 | bytes 4997124 | tf_op jit(solution)/shard_map/main/pallas_call | solution.py:342
  24.0 1.3 %collective-permute-start.3 = (bf16[96,512]{1,0:T(8,128)(2,1)S(1)}, bf16[96,512]{1,0:T(8,128)(2,1)S(1)}, u32[]{:S(2)}, u32[]{:S(2)}) collective-permute-start(bf16[96,512]{1,0:T(8,128)(2,1)S(1)} %get-tuple-element.48), channel_id=1, source_target_pairs={{0,1},{1,0},{2,3},{3,2},{4,5},{5,4},{6,7},{7,6},{8,9},{9,8},{10,11... | collective-permute-start | bytes 294920 | tf_op jit(solution)/shard_map/ppermute | solution.py:527
  25.3 3.1 %all-to-all-start.1 = ((bf16[32,4,128]{2,1,0:T(4,128)(2,1)}), bf16[32,4,128]{2,1,0:T(4,128)(2,1)S(1)}, u32[]{:S(2)}, u32[]{:S(2)}) async-start(bf16[32,4,128]{2,1,0:T(4,128)(2,1)} %get-tuple-element.53), calls=%async_computation.1 | async-start | bytes 65536 | tf_op jit(solution)/shard_map/all_to_all | solution.py:529
  28.4 0.6 %collective-permute-done.3.refs_0_ = bf16[96,512]{1,0:T(8,128)(2,1)S(1)} collective-permute-done((bf16[96,512]{1,0:T(8,128)(2,1)S(1)}, bf16[96,512]{1,0:T(8,128)(2,1)S(1)}, u32[]{:S(2)}, u32[]{:S(2)}) %collective-permute-start.3) | collective-permute-done | bytes 98336 | tf_op jit(solution)/shard_map/ppermute | solution.py:527
  29.1 0.1 collective-permute-start.4
  29.1 4.0 %collective-permute-start.5 = (bf16[32,512]{1,0:T(8,128)(2,1)S(1)}, bf16[32,512]{1,0:T(8,128)(2,1)S(1)}, u32[]{:S(2)}, u32[]{:S(2)}) collective-permute-start(bf16[32,512]{1,0:T(8,128)(2,1)S(1)} %get-tuple-element.55), channel_id=1, source_target_pairs={{2,4},{4,2},{3,5},{5,3},{6,8},{8,6},{7,9},{9,7},{10,12},{12,10},{1... | collective-permute-start | bytes 98312 | tf_op jit(solution)/shard_map/ppermute | solution.py:537
  33.2 2.5 %behind.1 = (f32[64,512]{1,0:T(8,128)S(1)}, bf16[1,1,384,512]{3,2,1,0:T(8,128)(2,1)}) custom-call(bf16[64,384]{1,0:T(8,128)(2,1)S(1)} %get-tuple-element.36.refs_9_.refs_0_, bf16[384,512]{1,0:T(8,128)(2,1)S(1)} %get-tuple-element.44.refs_1_, bf16[128,512]{1,0:T(8,128)(2,1)S(1)} %get-tuple-element.45.refs_2_, f32[64,512]{1,0:T(8,128)S(1)} %get-tuple-element.46.refs_3_, ...), custom_call_target="tpu_custom_call" | custom-call | flops 234881024 | bytes 2736128 | tf_op jit(solution)/shard_map/behind/pallas_call | solution.py:342
  35.7 0.0 all-to-all-done.1.refs_4_
  35.8 0.0 collective-permute-done.4.refs_5_
  35.8 0.0 collective-permute-done.5.refs_6_
  35.8 0.8 %last.1 = bf16[1,1,64,512]{3,2,1,0:T(8,128)(2,1)} custom-call(f32[64,512]{1,0:T(8,128)S(1)} %get-tuple-element.50.refs_0_, f32[32,512]{1,0:T(8,128)S(1)} %get-tuple-element.49.refs_4_.refs_1_, bf16[64,64]{1,0:T(8,128)(2,1)S(1)} %get-tuple-element.51.refs_2_, f32[64,1]{1,0:T(8,128)S(1)} %get-tuple-element.52.refs_3_, ...), custom_call_target="tpu_custom_call" | custom-call | bytes 303360 | tf_op jit(solution)/shard_map/last/pallas_call | solution.py:342
  (2 shorter events, 0.0 us)
Async XLA Ops:
  3.0 7.9 %collective-permute-start = (bf16[128,512]{1,0:T(8,128)(2,1)S(1)}, bf16[128,512]{1,0:T(8,128)(2,1)S(1)}, u32[]{:S(2)}, u32[]{:S(2)}) collective-permute-start(bf16[128,512]{1,0:T(8,128)(2,1)S(1)} %get-tuple-element.30.refs_0_), channel_id=1, source_target_pairs={{0,1},{1,0},{2,3},{3,2},{4,5},{5,4},{6,7},{7,6},{8,9},{9,8},{10,11... | collective-permute-start | bytes 393224 | tf_op jit(solution)/shard_map/ppermute | solution.py:402
  6.0 13.0 %all-to-all-start = ((f32[32,4,128]{2,1,0:T(4,128)}), f32[32,4,128]{2,1,0:T(4,128)S(1)}, u32[]{:S(2)}, u32[]{:S(2)}) async-start(f32[32,4,128]{2,1,0:T(4,128)} %get-tuple-element.31), calls=%async_computation | async-start | bytes 131072 | tf_op jit(solution)/shard_map/all_to_all | solution.py:401
  11.0 8.0 %collective-permute-start.2 = (bf16[64,512]{1,0:T(8,128)(2,1)S(1)}, bf16[64,512]{1,0:T(8,128)(2,1)S(1)}, u32[]{:S(2)}, u32[]{:S(2)}) collective-permute-start(bf16[64,512]{1,0:T(8,128)(2,1)S(1)} %join.1.refs_1_), channel_id=1, source_target_pairs={{2,4},{4,2},{3,5},{5,3},{6,8},{8,6},{7,9},{9,7},{10,12},{12,10},{1... | collective-permute-start | bytes 196616 | tf_op jit(solution)/shard_map/ppermute | solution.py:463
  15.3 3.7 %collective-permute-start.1 = (bf16[64,512]{1,0:T(8,128)(2,1)S(1)}, bf16[64,512]{1,0:T(8,128)(2,1)S(1)}, u32[]{:S(2)}, u32[]{:S(2)}) collective-permute-start(bf16[64,512]{1,0:T(8,128)(2,1)S(1)} %join.1.refs_1_), channel_id=1, source_target_pairs={{0,2},{2,0},{1,3},{3,1},{4,6},{6,4},{5,7},{7,5},{8,10},{10,8},{9,1... | collective-permute-start | bytes 196616 | tf_op jit(solution)/shard_map/ppermute | solution.py:463
  24.0 5.0 %collective-permute-start.3 = (bf16[96,512]{1,0:T(8,128)(2,1)S(1)}, bf16[96,512]{1,0:T(8,128)(2,1)S(1)}, u32[]{:S(2)}, u32[]{:S(2)}) collective-permute-start(bf16[96,512]{1,0:T(8,128)(2,1)S(1)} %get-tuple-element.48), channel_id=1, source_target_pairs={{0,1},{1,0},{2,3},{3,2},{4,5},{5,4},{6,7},{7,6},{8,9},{9,8},{10,11... | collective-permute-start | bytes 294920 | tf_op jit(solution)/shard_map/ppermute | solution.py:527
  25.3 10.4 %all-to-all-start.1 = ((bf16[32,4,128]{2,1,0:T(4,128)(2,1)}), bf16[32,4,128]{2,1,0:T(4,128)(2,1)S(1)}, u32[]{:S(2)}, u32[]{:S(2)}) async-start(bf16[32,4,128]{2,1,0:T(4,128)(2,1)} %get-tuple-element.53), calls=%async_computation.1 | async-start | bytes 65536 | tf_op jit(solution)/shard_map/all_to_all | solution.py:529
  29.1 6.7 %collective-permute-start.4 = (bf16[32,512]{1,0:T(8,128)(2,1)S(1)}, bf16[32,512]{1,0:T(8,128)(2,1)S(1)}, u32[]{:S(2)}, u32[]{:S(2)}) collective-permute-start(bf16[32,512]{1,0:T(8,128)(2,1)S(1)} %get-tuple-element.54), channel_id=1, source_target_pairs={{0,2},{2,0},{1,3},{3,1},{4,6},{6,4},{5,7},{7,5},{8,10},{10,8},{9,1... | collective-permute-start | bytes 98312 | tf_op jit(solution)/shard_map/ppermute | solution.py:537
  29.1 6.6 %collective-permute-start.5 = (bf16[32,512]{1,0:T(8,128)(2,1)S(1)}, bf16[32,512]{1,0:T(8,128)(2,1)S(1)}, u32[]{:S(2)}, u32[]{:S(2)}) collective-permute-start(bf16[32,512]{1,0:T(8,128)(2,1)S(1)} %get-tuple-element.55), channel_id=1, source_target_pairs={{2,4},{4,2},{3,5},{5,3},{6,8},{8,6},{7,9},{9,7},{10,12},{12,10},{1... | collective-permute-start | bytes 98312 | tf_op jit(solution)/shard_map/ppermute | solution.py:537

commit v6 on v5

--- a/solution.py
+++ b/solution.py
@@ -262,18 +262,19 @@
         dot_nt(edge_dout, got("w_edge_out")[...]) * silu_slope(edge_pre, edge_sig)
     ).astype(BF16)
     edge_dpre_out[...] = edge_dpre
-    away_grad = dot_nt(dot_nn(sent[...], edge_dpre).astype(BF16), w_edge_mid)
-    own_grad, away_grad = away_grad[:nodes], away_grad[nodes:]
+    away = dot_nn(sent[...], edge_dpre).astype(BF16)
     kept = plan.per_lon * halo
-    start = 3 * kept
+    rim_end = nodes + 3 * kept
+    coarse_sum = dot_nt(away[rim_end:], w_edge_mid)
     for k in range(plan.owned):
         for q in range(parts):
-            tiles[:, k * parts + q, :] = away_grad[
-                start : start + plan.devices, q * 128 : (q + 1) * 128
+            tiles[:, k * parts + q, :] = coarse_sum[
+                k * plan.devices : (k + 1) * plan.devices, q * 128 : (q + 1) * 128
             ]
-        start += plan.devices
     coarse_s[...] = tiles[...].astype(BF16)
     coarse_leaving = moves.start(coarse_s, coarse_grad)
+    away_grad = dot_nt(away[:rim_end], w_edge_mid)
+    own_grad, away_grad = away_grad[:nodes], away_grad[nodes:]
     for a in range(3):
         rows = slice(a * halo, (a + 1) * halo)
         kept_grad[rows] = away_grad[a * kept : a * kept + halo].astype(BF16)
@@ -402,11 +403,11 @@
     lat_rows = [lax.ppermute(border, axes, pairs) for pairs in plan.lat_pairs]
 
     far = {
+        "edge": edge_feat,
+        "w_edge_in": w_edge_in,
         "count": edge_count,
         "receivers": receivers,
         "node": node_feat,
-        "edge": edge_feat,
-        "w_edge_in": w_edge_in,
         "b_edge_in": row(b_edge_in),
         "senders": senders,
         "halo_list": halo_list,
@@ -552,7 +553,7 @@
         with_plan(last_kernel),
         "last",
         [(node_feat.shape, BF16)],
-        [grad_local, mine, at["place"], at["at_coarse"], coarse_back, *lon_back],
+        [grad_local, mine, at["place"], at["at_coarse"], coarse_back, *lon_back[::-1]],
         results=1,
     )
     return new_nodes, grad_nodes, grad_edges

time: 36.9 us -> 36.9 us (level)
  starting transfers between devices: 20.8 us -> 20.4 us
  waiting for transfers between devices: 0.96 us -> 1.36 us
    all_to_all x1, waiting for transfers between devices: 0.01 us -> 0.42 us  [body(): coarse_back = lax.all_to_all(coarse_send, axes, 0, 0, tiled=True)]
  transfers between devices with their start and end apart: 8 -> 8, of which waited for: 2 -> 3; matrix products, arithmetic and copies ran while one was open for 0% -> 0% of each run, Pallas kernels for 14% -> 14%
where the time goes in v6:
time: 36.9 us; the launch traced here: 36.6 us
  starting transfers between devices  20.4 us (55%)
  Pallas kernels  12.8 us (35%)
  between operations  2 us (5%)
  waiting for transfers between devices  1.36 us (4%)
    pallas_call x7, Pallas kernels, call(): pl.pallas_call(body, name=name, out_shape=[VMEM(shape, dtype) for shape,...  12.8 us
    ppermute x3, starting transfers between devices, body(): lax.ppermute(grad, axes, pairs)  5.04 us
    all_to_all x1, starting transfers between devices, body(): coarse_rows = lax.all_to_all(coarse_out, axes, 0, 0, tiled=True)  4.92 us
    ppermute x2, starting transfers between devices, body(): lax.ppermute(wide, axes, pairs)  4.37 us
    all_to_all x1, starting transfers between devices, body(): coarse_back = lax.all_to_all(coarse_send, axes, 0, 0, tiled=True)  3.1 us
    ppermute x1, starting transfers between devices, body(): lat_rows = [lax.ppermute(border, axes, pairs) for pairs in plan.lat_pairs]  3 us
  transfers between devices with their start and end apart: 8, of which 3 were waited for; matrix products, arithmetic and copies ran while one was open for 0% of the time, Pallas kernels for 14%

profile of v6, /device:TPU:0, one launch (start us, length us, event | category | flops | bytes accessed | tf_op | source)
XLA Modules:
  0.0 36.6 jit_solution(14924483251983760925)
XLA Ops:
  1.3 1.7 %pack.1 = (bf16[128,512]{1,0:T(8,128)(2,1)S(1)}, f32[32,4,128]{2,1,0:T(4,128)}) custom-call(bf16[1,1,64,512]{3,2,1,0:T(8,128)(2,1)} %refs_4_.1, s32[1,1,32]{2,1,0:T(1,128)} %refs_7_.1, s32[1,1,1]{2,1,0:T(1,128)S(6)} %copy.23.coarse_list.refs_8_), custom_call_target="tpu_custom_call" | custom-call | bytes 65668 | tf_op jit(solution)/shard_map/pack/pallas_call | solution.py:343
  3.0 3.0 %collective-permute-start = (bf16[128,512]{1,0:T(8,128)(2,1)S(1)}, bf16[128,512]{1,0:T(8,128)(2,1)S(1)}, u32[]{:S(2)}, u32[]{:S(2)}) collective-permute-start(bf16[128,512]{1,0:T(8,128)(2,1)S(1)} %get-tuple-element.30.refs_0_), channel_id=1, source_target_pairs={{0,1},{1,0},{2,3},{3,2},{4,5},{5,4},{6,7},{7,6},{8,9},{9,8},{10,11... | collective-permute-start | bytes 393224 | tf_op jit(solution)/shard_map/ppermute | solution.py:403
  6.0 4.9 %all-to-all-start = ((f32[32,4,128]{2,1,0:T(4,128)}), f32[32,4,128]{2,1,0:T(4,128)S(1)}, u32[]{:S(2)}, u32[]{:S(2)}) async-start(f32[32,4,128]{2,1,0:T(4,128)} %get-tuple-element.31), calls=%async_computation | async-start | bytes 131072 | tf_op jit(solution)/shard_map/all_to_all | solution.py:402
  10.9 0.0 collective-permute-done.refs_1_
  11.0 4.4 %collective-permute-start.2 = (bf16[64,512]{1,0:T(8,128)(2,1)S(1)}, bf16[64,512]{1,0:T(8,128)(2,1)S(1)}, u32[]{:S(2)}, u32[]{:S(2)}) collective-permute-start(bf16[64,512]{1,0:T(8,128)(2,1)S(1)} %join.1.refs_1_), channel_id=1, source_target_pairs={{2,4},{4,2},{3,5},{5,3},{6,8},{8,6},{7,9},{9,7},{10,12},{12,10},{1... | collective-permute-start | bytes 196616 | tf_op jit(solution)/shard_map/ppermute | solution.py:464
  15.3 0.0 collective-permute-start.1
  16.0 2.7 %ahead.1 = (bf16[1,1,64,512]{3,2,1,0:T(8,128)(2,1)S(1)}, bf16[512,512]{1,0:T(8,128)(2,1)S(1)}, f32[1,512]{1,0:T(1,128)S(1)}, f32[1,512]{1,0:T(1,128)S(1)}, f32[1...) custom-call(bf16[1,1,384,512]{3,2,1,0:T(8,128)(2,1)} %refs_16_.1, ...), custom_call_target="tpu_custom_call" | custom-call | flops 436207616 | bytes 3619976 | tf_op jit(solution)/shard_map/ahead/pallas_call | solution.py:343
  18.7 0.3 all-to-all-done.refs_4_
  19.0 0.0 collective-permute-done.2.refs_3_
  19.0 0.0 collective-permute-done.1.refs_2_
  19.0 5.0 %main.1 = (bf16[96,512]{1,0:T(8,128)(2,1)S(1)}, bf16[128,512]{1,0:T(8,128)(2,1)S(1)}, bf16[384,512]{1,0:T(8,128)(2,1)S(1)}, f32[64,512]{1,0:T(8,128)S(1)}, bf16[...) custom-call(s32[1,1]{1,0:T(1,128)S(6)} %copy.22.refs_2_.refs_0_, ...), custom_call_target="tpu_custom_call" | custom-call | flops 1006632960 | bytes 4997124 | tf_op jit(solution)/shard_map/main/pallas_call | solution.py:343
  24.0 1.3 %collective-permute-start.3 = (bf16[96,512]{1,0:T(8,128)(2,1)S(1)}, bf16[96,512]{1,0:T(8,128)(2,1)S(1)}, u32[]{:S(2)}, u32[]{:S(2)}) collective-permute-start(bf16[96,512]{1,0:T(8,128)(2,1)S(1)} %get-tuple-element.48), channel_id=1, source_target_pairs={{0,1},{1,0},{2,3},{3,2},{4,5},{5,4},{6,7},{7,6},{8,9},{9,8},{10,11... | collective-permute-start | bytes 294920 | tf_op jit(solution)/shard_map/ppermute | solution.py:528
  25.3 3.1 %all-to-all-start.1 = ((bf16[32,4,128]{2,1,0:T(4,128)(2,1)}), bf16[32,4,128]{2,1,0:T(4,128)(2,1)S(1)}, u32[]{:S(2)}, u32[]{:S(2)}) async-start(bf16[32,4,128]{2,1,0:T(4,128)(2,1)} %get-tuple-element.53), calls=%async_computation.1 | async-start | bytes 65536 | tf_op jit(solution)/shard_map/all_to_all | solution.py:530
  28.4 0.6 %collective-permute-done.3.refs_0_ = bf16[96,512]{1,0:T(8,128)(2,1)S(1)} collective-permute-done((bf16[96,512]{1,0:T(8,128)(2,1)S(1)}, bf16[96,512]{1,0:T(8,128)(2,1)S(1)}, u32[]{:S(2)}, u32[]{:S(2)}) %collective-permute-start.3) | collective-permute-done | bytes 98336 | tf_op jit(solution)/shard_map/ppermute | solution.py:528
  29.0 3.8 %collective-permute-start.4 = (bf16[32,512]{1,0:T(8,128)(2,1)S(1)}, bf16[32,512]{1,0:T(8,128)(2,1)S(1)}, u32[]{:S(2)}, u32[]{:S(2)}) collective-permute-start(bf16[32,512]{1,0:T(8,128)(2,1)S(1)} %get-tuple-element.54), channel_id=1, source_target_pairs={{2,4},{4,2},{3,5},{5,3},{6,8},{8,6},{7,9},{9,7},{10,12},{12,10},{1... | collective-permute-start | bytes 98312 | tf_op jit(solution)/shard_map/ppermute | solution.py:538
  32.8 0.0 collective-permute-start.5
  32.8 2.5 %behind.1 = (f32[64,512]{1,0:T(8,128)S(1)}, bf16[1,1,384,512]{3,2,1,0:T(8,128)(2,1)}) custom-call(bf16[64,384]{1,0:T(8,128)(2,1)S(1)} %get-tuple-element.36.refs_9_.refs_0_, bf16[384,512]{1,0:T(8,128)(2,1)S(1)} %get-tuple-element.44.refs_1_, bf16[128,512]{1,0:T(8,128)(2,1)S(1)} %get-tuple-element.45.refs_2_, f32[64,512]{1,0:T(8,128)S(1)} %get-tuple-element.46.refs_3_, ...), custom_call_target="tpu_custom_call" | custom-call | flops 234881024 | bytes 2736128 | tf_op jit(solution)/shard_map/behind/pallas_call | solution.py:343
  35.4 0.4 %all-to-all-done.1.refs_4_ = bf16[32,4,128]{2,1,0:T(4,128)(2,1)S(1)} async-done(((bf16[32,4,128]{2,1,0:T(4,128)(2,1)}), bf16[32,4,128]{2,1,0:T(4,128)(2,1)S(1)}, u32[]{:S(2)}, u32[]{:S(2)}) %all-to-all-start.1) | async-done | bytes 32800 | tf_op jit(solution)/shard_map/all_to_all | solution.py:530
  35.8 0.0 collective-permute-done.4.refs_5_
  35.8 0.0 collective-permute-done.5.refs_6_
  35.8 0.8 %last.1 = bf16[1,1,64,512]{3,2,1,0:T(8,128)(2,1)} custom-call(f32[64,512]{1,0:T(8,128)S(1)} %get-tuple-element.50.refs_0_, f32[32,512]{1,0:T(8,128)S(1)} %get-tuple-element.49.refs_4_.refs_1_, bf16[64,64]{1,0:T(8,128)(2,1)S(1)} %get-tuple-element.51.refs_2_, f32[64,1]{1,0:T(8,128)S(1)} %get-tuple-element.52.refs_3_, ...), custom_call_target="tpu_custom_call" | custom-call | bytes 303360 | tf_op jit(solution)/shard_map/last/pallas_call | solution.py:343
  (2 shorter events, 0.0 us)
Async XLA Ops:
  3.0 7.9 %collective-permute-start = (bf16[128,512]{1,0:T(8,128)(2,1)S(1)}, bf16[128,512]{1,0:T(8,128)(2,1)S(1)}, u32[]{:S(2)}, u32[]{:S(2)}) collective-permute-start(bf16[128,512]{1,0:T(8,128)(2,1)S(1)} %get-tuple-element.30.refs_0_), channel_id=1, source_target_pairs={{0,1},{1,0},{2,3},{3,2},{4,5},{5,4},{6,7},{7,6},{8,9},{9,8},{10,11... | collective-permute-start | bytes 393224 | tf_op jit(solution)/shard_map/ppermute | solution.py:403
  6.0 13.0 %all-to-all-start = ((f32[32,4,128]{2,1,0:T(4,128)}), f32[32,4,128]{2,1,0:T(4,128)S(1)}, u32[]{:S(2)}, u32[]{:S(2)}) async-start(f32[32,4,128]{2,1,0:T(4,128)} %get-tuple-element.31), calls=%async_computation | async-start | bytes 131072 | tf_op jit(solution)/shard_map/all_to_all | solution.py:402
  11.0 8.0 %collective-permute-start.2 = (bf16[64,512]{1,0:T(8,128)(2,1)S(1)}, bf16[64,512]{1,0:T(8,128)(2,1)S(1)}, u32[]{:S(2)}, u32[]{:S(2)}) collective-permute-start(bf16[64,512]{1,0:T(8,128)(2,1)S(1)} %join.1.refs_1_), channel_id=1, source_target_pairs={{2,4},{4,2},{3,5},{5,3},{6,8},{8,6},{7,9},{9,7},{10,12},{12,10},{1... | collective-permute-start | bytes 196616 | tf_op jit(solution)/shard_map/ppermute | solution.py:464
  15.3 3.7 %collective-permute-start.1 = (bf16[64,512]{1,0:T(8,128)(2,1)S(1)}, bf16[64,512]{1,0:T(8,128)(2,1)S(1)}, u32[]{:S(2)}, u32[]{:S(2)}) collective-permute-start(bf16[64,512]{1,0:T(8,128)(2,1)S(1)} %join.1.refs_1_), channel_id=1, source_target_pairs={{0,2},{2,0},{1,3},{3,1},{4,6},{6,4},{5,7},{7,5},{8,10},{10,8},{9,1... | collective-permute-start | bytes 196616 | tf_op jit(solution)/shard_map/ppermute | solution.py:464
  24.0 5.0 %collective-permute-start.3 = (bf16[96,512]{1,0:T(8,128)(2,1)S(1)}, bf16[96,512]{1,0:T(8,128)(2,1)S(1)}, u32[]{:S(2)}, u32[]{:S(2)}) collective-permute-start(bf16[96,512]{1,0:T(8,128)(2,1)S(1)} %get-tuple-element.48), channel_id=1, source_target_pairs={{0,1},{1,0},{2,3},{3,2},{4,5},{5,4},{6,7},{7,6},{8,9},{9,8},{10,11... | collective-permute-start | bytes 294920 | tf_op jit(solution)/shard_map/ppermute | solution.py:528
  25.3 10.5 %all-to-all-start.1 = ((bf16[32,4,128]{2,1,0:T(4,128)(2,1)}), bf16[32,4,128]{2,1,0:T(4,128)(2,1)S(1)}, u32[]{:S(2)}, u32[]{:S(2)}) async-start(bf16[32,4,128]{2,1,0:T(4,128)(2,1)} %get-tuple-element.53), calls=%async_computation.1 | async-start | bytes 65536 | tf_op jit(solution)/shard_map/all_to_all | solution.py:530
  29.0 6.8 %collective-permute-start.4 = (bf16[32,512]{1,0:T(8,128)(2,1)S(1)}, bf16[32,512]{1,0:T(8,128)(2,1)S(1)}, u32[]{:S(2)}, u32[]{:S(2)}) collective-permute-start(bf16[32,512]{1,0:T(8,128)(2,1)S(1)} %get-tuple-element.54), channel_id=1, source_target_pairs={{2,4},{4,2},{3,5},{5,3},{6,8},{8,6},{7,9},{9,7},{10,12},{12,10},{1... | collective-permute-start | bytes 98312 | tf_op jit(solution)/shard_map/ppermute | solution.py:538
  32.8 3.0 %collective-permute-start.5 = (bf16[32,512]{1,0:T(8,128)(2,1)S(1)}, bf16[32,512]{1,0:T(8,128)(2,1)S(1)}, u32[]{:S(2)}, u32[]{:S(2)}) collective-permute-start(bf16[32,512]{1,0:T(8,128)(2,1)S(1)} %get-tuple-element.55), channel_id=1, source_target_pairs={{0,2},{2,0},{1,3},{3,1},{4,6},{6,4},{5,7},{7,5},{8,10},{10,8},{9,1... | collective-permute-start | bytes 98312 | tf_op jit(solution)/shard_map/ppermute | solution.py:538
